TPU v7x, 128 devices: a whole 4x4x4 slice. The times are simulated.
128 devices in a mesh: section: 2 (over core), dp: 16 (over y, x), tensor: 4 (over z).
Axes of the slice: x: 4, y: 4, z: 4, core: 2. Of those that a mesh axis runs over, the one named last changes fastest.
Arguments:
- boundary_copies: bfloat16 [2, 2, 32, 128, 4096], P('section', None, 'dp', None, 'tensor'), may hold values from -6 to 6
- arriving: bfloat16 [2, 16, 128, 4096], P('section', 'dp', None, 'tensor'), may hold values from -7 to 7
- first_delta: bfloat16 [2, 16, 128, 4096], P(None, 'dp', None, 'tensor'), may hold values from -7 to 7
- sample_index: int32 [4, 16], P(None, 'dp'), may hold values from 0 to 1
- exponents: int32 [3, 32], P(None, 'tensor'), may hold values from -3 to -1
- norm_gain: float32 [2, 4096], P('section'), may hold values from 0.25 to 1.75
- w_query: bfloat16 [2, 4096, 4096], P('section', 'dp', 'tensor'), may hold values from -0.09375 to 0.09375
- w_key: bfloat16 [2, 4096, 512], P('section', 'dp', 'tensor'), may hold values from -0.09375 to 0.09375
- w_value: bfloat16 [2, 4096, 512], P('section', 'dp', 'tensor'), may hold values from -0.09375 to 0.09375
- w_out: bfloat16 [2, 4096, 4096], P('section', 'tensor', 'dp'), may hold values from -0.09375 to 0.09375
- out_grad: bfloat16 [2, 3, 16, 128, 4096], P('section', None, 'dp'), may hold values from -6 to 6
Outputs:
- copies_new: bfloat16 [2, 2, 32, 128, 4096], P('section', None, 'dp', None, 'tensor')
- grad_query: bfloat16 [2, 4096, 4096], P('section', 'dp', 'tensor')
- grad_value: bfloat16 [2, 4096, 512], P('section', 'dp', 'tensor')
All inputs are finite; a program needn't handle non-finite values.
Results may differ from a plain program's by a relative error of at most 0.025.
Values may be sent and summed in bfloat16 or wider, within the bound.
No kernel may reach another device: no remote copies, remote signals or barrier semaphores. Data moves between devices by JAX's collectives and lax.ppermute only.
A program may use at most 128 MiB of HBM per device.

v0:
```python
import functools

import jax
import jax.numpy as jnp
from jax import lax
from jax.experimental import pallas as pl
from jax.experimental.pallas import tpu as pltpu
from jax.sharding import Mesh, PartitionSpec as P

HQ = 32
HK = 4
HD = 128
QB = 128
SEQ = 128

eps_norm = 1e-05
qmax = 7.0
f32 = jnp.float32
bf16 = jnp.bfloat16


GROUP = HQ // HK
NT = (((1,), (1,)), ((), ()))
TN = (((0,), (0,)), ((), ()))


def stacked(rows):
    return jnp.concatenate([rows[:, h * HD : (h + 1) * HD] for h in range(GROUP)], axis=0)


def side_by_side(rows):
    return jnp.concatenate([rows[h * SEQ : (h + 1) * SEQ] for h in range(GROUP)], axis=1)


def probs_of(query, key_in):
    scores = lax.dot_general(query, key_in, NT, preferred_element_type=f32) * HD ** (-0.5)
    at = lax.broadcasted_iota(jnp.int32, scores.shape, 0) % SEQ
    key_at = lax.broadcasted_iota(jnp.int32, scores.shape, 1)
    scores = jnp.where(at >= key_at, scores, -1e30)
    weight = jnp.exp(scores - jnp.max(scores, axis=-1, keepdims=True))
    return weight / jnp.sum(weight, axis=-1, keepdims=True)


def attend_unit(qkv):
    wide = GROUP * HD
    probs = probs_of(stacked(qkv[:, :wide]), qkv[:, wide : wide + HD])
    mixed = jnp.dot(probs.astype(bf16), qkv[:, wide + HD :], preferred_element_type=f32)
    return side_by_side(mixed.astype(bf16))


def attend_back_kernel(qkv_ref, d_mixed_ref, out_ref):
    wide = GROUP * HD
    key_in = qkv_ref[:, wide : wide + HD]
    probs = probs_of(stacked(qkv_ref[:, :wide]), key_in)
    d_rows = stacked(d_mixed_ref[...])
    d_probs = lax.dot_general(d_rows, qkv_ref[:, wide + HD :], NT, preferred_element_type=f32)
    d_scores = (
        probs * (d_probs - jnp.sum(d_probs * probs, axis=-1, keepdims=True)) * HD ** (-0.5)
    )
    d_query = jnp.dot(d_scores.astype(bf16), key_in, preferred_element_type=f32).astype(bf16)
    d_value = lax.dot_general(probs.astype(bf16), d_rows, TN, preferred_element_type=f32)
    out_ref[:, :wide] = side_by_side(d_query)
    out_ref[:, wide:] = d_value.astype(bf16)


def attend_back(qkv, d_mixed):
    rows = qkv.shape[0]
    return pl.pallas_call(
        attend_back_kernel,
        grid=(rows // SEQ,),
        in_specs=[
            pl.BlockSpec((SEQ, (GROUP + 2) * HD), lambda u: (u, 0)),
            pl.BlockSpec((SEQ, GROUP * HD), lambda u: (u, 0)),
        ],
        out_specs=pl.BlockSpec((SEQ, (GROUP + 1) * HD), lambda u: (u, 0)),
        out_shape=jax.ShapeDtypeStruct((rows, (GROUP + 1) * HD), bf16),
        compiler_params=pltpu.CompilerParams(vmem_limit_bytes=32 * 1024 * 1024),
        cost_estimate=pl.CostEstimate(
            flops=rows * SEQ * GROUP * HD * 8,
            bytes_accessed=rows * 3456 * 2,
            transcendentals=rows * SEQ * GROUP,
        ),
        name="attend_back",
    )(qkv, d_mixed)


ROWS = 16
HALF = 512
ORDER = (0, 3, 1, 2)


def known_a(flags, known_ref, x_ref):
    from_0 = (flags[0] == 1) | (flags[1] == 0)

    def step(i, carry):
        at = pl.multiple_of(i * ROWS, ROWS)
        for j in range(4):
            one = known_ref[j, pl.ds(at, ROWS), :]
            two = known_ref[j, pl.ds(at + SEQ, ROWS), :]
            columns = slice(j * 1024, (j + 1) * 1024)
            x_ref[pl.ds(at, ROWS), columns] = jnp.where(from_0, one, two)
            x_ref[pl.ds(at + SEQ, ROWS), columns] = two
        return carry

    lax.fori_loop(0, SEQ // ROWS, step, 0)


def known_b(flags, known_ref, got_refs, x_ref):
    first = flags[0] == 1
    slot_1, slot_2 = flags[2], flags[3]

    def step(i, carry):
        at = pl.multiple_of(i * ROWS, ROWS)
        for by in range(4):
            j = lax.rem(flags[6] + 4 - by, 4)
            one = known_ref[j, pl.ds(at, ROWS), :].astype(f32)
            two = known_ref[j, pl.ds(at + SEQ, ROWS), :].astype(f32)
            third = known_ref[j, pl.ds(at + 2 * SEQ, ROWS), :]
            step_1 = got_refs[by][pl.ds(at, ROWS), :].astype(f32)
            step_2 = got_refs[by][pl.ds(at + SEQ, ROWS), :].astype(f32)
            x_1 = (jnp.where(slot_1 == 0, one, two) + step_1).astype(bf16)
            old = jnp.where(
                slot_1 == slot_2, x_1.astype(f32), jnp.where(slot_2 == 0, one, two)
            )
            columns = pl.ds(pl.multiple_of(j * 1024, 1024), 1024)
            x_ref[pl.ds(at, ROWS), columns] = jnp.where(first, third, x_1)
            x_ref[pl.ds(at + SEQ, ROWS), columns] = (old + step_2).astype(bf16)
        return carry

    lax.fori_loop(0, SEQ // ROWS, step, 0)


def normalize(gain_ref, x_ref):
    def step(i, carry):
        rows = pl.ds(pl.multiple_of(i * ROWS, ROWS), ROWS)
        values = x_ref[rows, :].astype(f32)
        square = jnp.mean(values * values, axis=-1, keepdims=True)
        x_ref[rows, :] = (values * lax.rsqrt(square + eps_norm) * gain_ref[...]).astype(bf16)
        return carry

    lax.fori_loop(0, 2 * SEQ // ROWS, step, 0)


def prepare_kernel(flags, gain_ref, known_ref, normed_ref):
    known_a(flags, known_ref, normed_ref)
    normalize(gain_ref, normed_ref)


VMEM = pl.BlockSpec(memory_space=pltpu.VMEM)
SMEM = pl.BlockSpec(memory_space=pltpu.SMEM)
ANY = pl.BlockSpec(memory_space=pl.ANY)
GRANT = pltpu.CompilerParams(vmem_limit_bytes=60 * 1024 * 1024)


def prepare(flags, gain, known):
    return pl.pallas_call(
        prepare_kernel,
        in_specs=[SMEM, VMEM, VMEM],
        out_specs=VMEM,
        out_shape=jax.ShapeDtypeStruct((2 * SEQ, 4096), bf16),
        compiler_params=pltpu.CompilerParams(vmem_limit_bytes=32 * 1024 * 1024),
        cost_estimate=pl.CostEstimate(flops=2**23, bytes_accessed=5 * 2**20, transcendentals=0),
        name="prepare",
    )(flags, gain, known)


def project_kernel(flags, pieces, normed_ref, qkv_ref, mixed_ref, held, held_kv, sems, begin):
    full_ref, pieces = pieces[0], pieces[1:]
    copies = []
    for at in range(5):
        for half in range(2):
            target = held.at[half, at] if at < 3 else held.at[half, 3, pl.ds(2 * (at - 3), 2)]
            copies.append(
                pltpu.make_async_copy(pieces[half * 5 + at], target, sems.at[2 * at + half])
            )
    copies.append(pltpu.make_async_copy(full_ref.at[:, pl.ds(1024, 256)], held_kv, sems.at[10]))
    for copy in copies:
        copy.start()
    begin()
    totals = [None, None]
    for at in range(4):
        for half in range(2):
            lhs = []
            for block in range(4):
                along, across = ORDER[at], ORDER[block]
                dy, dx = (along, across) if half == 0 else (across, along)
                row = lax.rem(flags[5] + dy, 4) * 4 + lax.rem(flags[4] + dx, 4)
                lhs.append(normed_ref[:, pl.ds(pl.multiple_of(row * 256, 256), 256)])
            copies[2 * at + half].wait()
            if at == 3:
                copies[8 + half].wait()
            part = jnp.dot(
                jnp.concatenate(lhs, axis=1),
                held[half, at].reshape(1024, HALF),
                preferred_element_type=f32,
            )
            totals[half] = part if totals[half] is None else totals[half] + part
    for half in range(2):
        qkv_ref[:, half * HALF : (half + 1) * HALF] = totals[half].astype(bf16)
    copies[10].wait()
    qkv_ref[:, 1024:] = jnp.dot(
        normed_ref[...], held_kv[...], preferred_element_type=f32
    ).astype(bf16)
    for unit in range(2):
        rows = slice(unit * SEQ, (unit + 1) * SEQ)
        mixed_ref[rows, :] = attend_unit(qkv_ref[rows, :])


def project_a_kernel(flags, normed_ref, *refs):
    pieces, (qkv_ref, mixed_ref, held, held_kv, sems) = refs[:11], refs[11:]
    project_kernel(flags, pieces, normed_ref, qkv_ref, mixed_ref, held, held_kv, sems, lambda: None)


def project_b_kernel(flags, gain_ref, known_ref, *refs):
    got_refs, pieces = refs[:4], refs[4:15]
    normed_ref, qkv_ref, mixed_ref, held, held_kv, sems = refs[15:]

    def begin():
        known_b(flags, known_ref, got_refs, normed_ref)
        normalize(gain_ref, normed_ref)

    project_kernel(flags, pieces, normed_ref, qkv_ref, mixed_ref, held, held_kv, sems, begin)


def project_call(kernel, name, operands, pieces, with_normed):
    rows = 2 * SEQ
    shapes = [
        jax.ShapeDtypeStruct((rows, 4096), bf16),
        jax.ShapeDtypeStruct((rows, (GROUP + 2) * HD), bf16),
        jax.ShapeDtypeStruct((rows, GROUP * HD), bf16),
    ][0 if with_normed else 1 :]
    return pl.pallas_call(
        kernel,
        in_specs=[SMEM] + [VMEM] * (len(operands) - 1) + [ANY] * 11,
        out_specs=[VMEM] * len(shapes),
        out_shape=shapes,
        scratch_shapes=[
            pltpu.VMEM((2, 4, 4, 256, HALF), bf16),
            pltpu.VMEM((4096, 256), bf16),
            pltpu.SemaphoreType.DMA((11,)),
        ],
        compiler_params=GRANT,
        cost_estimate=pl.CostEstimate(
            flops=2 * rows * 4096 * 2 * HALF, bytes_accessed=18 * 2**20, transcendentals=rows * 1024
        ),
        name=name,
    )(*operands, *pieces)


def spread_kernel(flags, mixed_ref, full_ref, *refs):
    outs, (held, sems) = refs[:4], refs[4:]
    copies = []
    for i, by in enumerate((2, 1, 3, 0)):
        row = pl.multiple_of(lax.rem(flags[6] + by, 4) * 1024, 1024)
        copies.append(
            pltpu.make_async_copy(full_ref.at[pl.ds(row, 1024), pl.ds(0, 1024)], held.at[i], sems.at[i])
        )
        copies[-1].start()
    for i in range(4):
        copies[i].wait()
        outs[i][...] = lax.dot_general(
            mixed_ref[...], held[i], NT, preferred_element_type=f32
        ).astype(bf16)


def spread(flags, mixed, full):
    rows = mixed.shape[0]
    return pl.pallas_call(
        spread_kernel,
        in_specs=[SMEM, VMEM, ANY],
        out_specs=[VMEM] * 4,
        out_shape=[jax.ShapeDtypeStruct((rows, 1024), bf16)] * 4,
        scratch_shapes=[pltpu.VMEM((4, 1024, 1024), bf16), pltpu.SemaphoreType.DMA((4,))],
        compiler_params=GRANT,
        cost_estimate=pl.CostEstimate(
            flops=2 * rows * 4096 * 1024, bytes_accessed=12 * 2**20, transcendentals=0
        ),
        name="spread",
    )(flags, mixed, full)


def around(shard, axis, by):
    return lax.ppermute(shard, axis, [(i, (i + by) % 4) for i in range(4)])


def from_first(shard, by, to_section):
    return lax.ppermute(
        shard, ("section", "tensor"), [(i, 4 * to_section + (i + by) % 4) for i in range(4)]
    )


def gathered(shard, axis):
    before, after, far = around(shard, axis, 1), around(shard, axis, -1), around(shard, axis, 2)
    return jnp.stack([shard, before, after, far])


def spread_on(own, then):
    before, after = around(own, then, 1), around(own, then, -1)
    return [own, before, after, around(before[:2], then, 1), around(after[2:], then, -1)]


def pick(state, slot):
    return jnp.where(slot == 0, state[0], state[1])


def put(state, slot, new, active=True):
    mask = (jnp.arange(2) == slot) & active
    return jnp.where(mask[:, None, None], new[None], state)


def on_device(
    boundary_copies,
    arriving,
    first_delta,
    sample_index,
    exponents,
    norm_gain,
    w_query,
    w_key,
    w_value,
    w_out,
    out_grad,
):
    first = lax.axis_index("section") == 0
    z = lax.axis_index("tensor")

    packed = jnp.concatenate([w_out[0].T, w_key[0], w_value[0]], axis=1)
    full = lax.all_gather(packed, ("y", "x"), axis=0, tiled=True)
    full_o = full[:, :1024]
    own_a = gathered(w_query[0, :, :HALF], "x")
    own_b = gathered(w_query[0, :, HALF:], "y")
    arriving, first_delta, own_a, own_b = lax.optimization_barrier(
        (arriving, first_delta, own_a, own_b)
    )
    pieces = [full] + spread_on(own_a, "y") + spread_on(own_b, "x")

    power = exponents.astype(f32)
    scale_full = jnp.repeat(jnp.exp2(power), QB, axis=1)
    inverse_full = jnp.repeat(jnp.exp2(-power), QB, axis=1)
    scale_in = jnp.where(first, scale_full[0], scale_full[1])
    scale_next = jnp.where(first, scale_full[1], scale_full[2])
    inverse_next = jnp.where(first, inverse_full[1], inverse_full[2])
    slots = sample_index[:, 0]
    slot = [jnp.where(first, slots[k + 1], slots[k]) for k in range(3)]

    def receive(state, at, delta):
        return (pick(state, at).astype(f32) + scale_in * delta.astype(f32)).astype(bf16)

    def deliver(state, at, inputs, summed):
        output = (inputs.astype(f32) + summed).astype(bf16)
        old = pick(state, at)
        sent = jnp.clip(
            (output.astype(f32) - old.astype(f32)) * inverse_next, -qmax, qmax
        ).astype(bf16)
        step = scale_next * sent.astype(f32)
        return step.astype(bf16), (old.astype(f32) + step).astype(bf16)

    state_in, state_out = boundary_copies[0, 0], boundary_copies[0, 1]
    x0 = receive(state_in, slot[0], arriving[0, 0])
    state_in = put(state_in, slot[0], x0)
    x1 = receive(state_in, slot[1], first_delta[0, 0])
    state_1 = put(state_in, slot[1], x1)
    x2 = receive(state_1, slot[2], first_delta[1, 0])
    state_2 = put(state_1, slot[2], x2)
    known = jnp.concatenate(
        [jnp.where(first, x0, state_in[0]), jnp.where(first, x1, state_in[1]), x2], 0
    )
    known = lax.all_to_all(
        jnp.broadcast_to(known[None], (4,) + known.shape),
        "tensor",
        split_axis=0,
        concat_axis=0,
        tiled=True,
    )

    flags = jnp.stack(
        [first.astype(jnp.int32), *slot, lax.axis_index("x"), lax.axis_index("y"), z]
    ).astype(jnp.int32)
    normed_a = prepare(flags, norm_gain, known)
    qkv_a, mixed_a = project_call(project_a_kernel, "project_a", [flags, normed_a], pieces, False)
    far, near_1, near_3, own = spread(flags, mixed_a, full)
    parts = [own] + [
        from_first(piece, by, 0) for piece, by in ((far, 2), (near_1, 1), (near_3, 3))
    ]
    summed = sum(part.astype(f32) for part in parts)
    step_0, renewed = deliver(state_out, slot[0], x0, summed[:SEQ])
    out_1 = put(state_out, slot[0], renewed)
    step_1, renewed = deliver(out_1, slot[1], x1, summed[SEQ:])
    out_2 = put(out_1, slot[1], renewed)
    steps = jnp.concatenate([step_0, step_1], 0)
    got = [from_first(steps, by, 1) for by in range(4)]

    def added(state, at, step):
        return (pick(state, at).astype(f32) + step.astype(f32)).astype(bf16)

    normed_b, qkv_b, mixed_b = project_call(
        project_b_kernel, "project_b", [flags, norm_gain, known, *got], pieces, True
    )
    y1 = added(state_in, slot[1], got[0][:SEQ])
    after_1 = put(state_in, slot[1], y1)
    y2 = added(after_1, slot[2], got[0][SEQ:])
    new_in = jnp.where(first, state_2, put(after_1, slot[2], y2))

    up = out_grad[0, :, 0].reshape(3 * SEQ, -1)
    d_mixed = jnp.dot(up, full_o, preferred_element_type=f32).astype(bf16)
    d_a = attend_back(qkv_a, d_mixed[: 2 * SEQ])
    d_mixed_b = jnp.concatenate(
        [jnp.where(first, d_mixed[2 * SEQ :], d_mixed[SEQ : 2 * SEQ]), d_mixed[2 * SEQ :]], 0
    )
    d_b = attend_back(qkv_b, d_mixed_b)

    def three(a, b):
        return jnp.concatenate([a[:SEQ], jnp.where(first, a[SEQ:], b[SEQ:]), b[:SEQ]], 0)

    term = lax.dot_general(
        three(normed_a, normed_b), three(d_a, d_b), TN, preferred_element_type=f32
    ).astype(bf16)
    grad = lax.psum_scatter(term, ("y", "x"), scatter_dimension=0, tiled=True)

    mixed_f = jnp.concatenate([jnp.where(first, mixed_b[:SEQ], mixed_a[:SEQ]), mixed_b], 0)
    mixed_f, _ = lax.optimization_barrier((mixed_f, term))
    partial = lax.dot_general(mixed_f, full_o, NT, preferred_element_type=f32).astype(bf16)
    parts = partial.reshape(3 * SEQ, 4, -1).swapaxes(0, 1)
    parts = lax.all_to_all(parts, "tensor", split_axis=0, concat_axis=0, tiled=True)
    summed = jnp.sum(parts.astype(f32), axis=0)
    _, renewed = deliver(out_2, slot[2], x2, summed[:SEQ])
    new_out_first = put(out_2, slot[2], renewed)
    _, renewed = deliver(state_out, slot[0], x0, summed[:SEQ])
    out_1 = put(state_out, slot[0], renewed)
    _, renewed = deliver(out_1, slot[1], y1, summed[SEQ : 2 * SEQ])
    out_1 = put(out_1, slot[1], renewed)
    _, renewed = deliver(out_1, slot[2], y2, summed[2 * SEQ :])
    new_out = jnp.where(first, new_out_first, put(out_1, slot[2], renewed))

    copies_new = jnp.stack([new_in, new_out])[None]
    return (copies_new, grad[None, :, :1024], grad[None, :, 1024:])


def solution(mesh):
    shape = dict(mesh.shape)
    grid = Mesh(
        mesh.devices.reshape(shape["section"], 4, shape["dp"] // 4, shape["tensor"]),
        ("section", "y", "x", "tensor"),
    )
    dp = ("y", "x")
    return jax.shard_map(
        on_device,
        mesh=grid,
        in_specs=(
            P("section", None, dp, None, "tensor"),
            P("section", dp, None, "tensor"),
            P(None, dp, None, "tensor"),
            P(None, dp),
            P(None, "tensor"),
            P("section", None),
            P("section", dp, "tensor"),
            P("section", dp, "tensor"),
            P("section", dp, "tensor"),
            P("section", "tensor", dp),
            P("section", None, dp, None, None),
        ),
        out_specs=(
            P("section", None, dp, None, "tensor"),
            P("section", dp, "tensor"),
            P("section", dp, "tensor"),
        ),
        check_vma=False,
    )
```

profile of v0, /device:TPU:0, one launch (start us, length us, event | category | flops | bytes accessed | tf_op | source)
XLA Modules:
  0.0 312.3 jit_solution(13667401895779025468)
XLA Ops:
  7.2 2.2 copy.15
  18.8 3.0 collective-permute-start.2
  23.2 2.8 collective-permute-start.1
  32.1 2.4 pad_maximum_fusion.1.refs_6_.refs_10_
  34.4 7.2 %collective-permute-done = bf16[256,512]{1,0:T(8,128)(2,1)} collective-permute-done((bf16[256,512]{1,0:T(8,128)(2,1)}, bf16[256,512]{1,0:T(8,128)(2,1)}, u32[]{:S(2)}, u32[]{:S(2)}) %collective-permute-start) | collective-permute-done | bytes 262176 | tf_op jit(solution)/shard_map/ppermute | solution.py:283
  41.6 2.2 pad_maximum_fusion.refs_1_.refs_5_
  48.0 6.1 %all-to-all-start = ((bf16[4,384,1024]{2,1,0:T(8,128)(2,1)}), bf16[4,384,1024]{2,1,0:T(8,128)(2,1)}, u32[]{:S(2)}, u32[]{:S(2)}) async-start(bf16[4,384,1024]{2,1,0:T(8,128)(2,1)} %broadcast_in_dim.196), calls=%async_computation | async-start | bytes 6291456 | tf_op jit(solution)/shard_map/all_to_all | solution.py:368
  54.1 2.5 collective-permute-start.10
  57.7 2.8 collective-permute-start.7
  60.6 40.7 %collective-permute-done.10.refs_7_.refs_11_ = bf16[4,256,512]{2,1,0:T(8,128)(2,1)S(1)} collective-permute-done((bf16[4,256,512]{2,1,0:T(8,128)(2,1)}, bf16[4,256,512]{2,1,0:T(8,128)(2,1)S(1)}, u32[]{:S(2)}, u32[]{:S(2)}) %collective-permute-start.10) | collective-permute-done | bytes 1048608 | tf_op jit(solution)/shard_map/ppermute | solution.py:283
  103.1 2.4 collective-permute-start.12
  112.1 3.0 collective-permute-start.9
  115.1 4.5 %prepare.1.normed_ref = bf16[256,4096]{1,0:T(8,128)(2,1)S(1)} custom-call(s32[7]{0:T(128)S(1)} %stack.72.flags, f32[1,4096]{1,0:T(1,128)S(1)} %copy-done.6, bf16[4,384,1024]{2,1,0:T(8,128)(2,1)} %all-to-all-done.known_ref), custom_call_target="tpu_custom_call" | custom-call | flops 8388608 | bytes 5242880 | tf_op jit(solution)/shard_map/prepare/pallas_call | solution.py:156
  120.9 6.8 %collective-permute-done.12.refs_9_.refs_13_ = bf16[2,256,512]{2,1,0:T(8,128)(2,1)} collective-permute-done((bf16[2,256,512]{2,1,0:T(8,128)(2,1)}, bf16[2,256,512]{2,1,0:T(8,128)(2,1)}, u32[]{:S(2)}, u32[]{:S(2)}) %collective-permute-start.12) | collective-permute-done | bytes 524320 | tf_op jit(solution)/shard_map/ppermute | solution.py:283
  127.7 2.6 collective-permute-done.13.refs_10_.refs_14_
  132.4 10.0 %project_a.1 = (bf16[256,1280]{1,0:T(8,128)(2,1)}, bf16[256,1024]{1,0:T(8,128)(2,1)}) custom-call(s32[7]{0:T(128)} %copy-done.7, bf16[256,4096]{1,0:T(8,128)(2,1)} %copy-done.2, bf16[4096,1280]{1,0:T(8,128)(2,1)} %all-gather.2.cloned.1.call-done.refs_0_.full_ref.refs_4_, bf16[4,256,512]{2,1,0:T(8,128)(2,1)} %pad_maximum_fusion.refs_1_.refs_5_, ...), custom_call_target="tpu_custom_call" | custom-call | flops 2147483648 | bytes 18874368 | tf_op jit(solution)/shard_map/project_a/pallas_call | solution.py:232
  142.4 6.4 %spread.1 = (bf16[256,1024]{1,0:T(8,128)(2,1)}, bf16[256,1024]{1,0:T(8,128)(2,1)}, bf16[256,1024]{1,0:T(8,128)(2,1)}, bf16[256,1024]{1,0:T(8,128)(2,1)}) custom-call(s32[7]{0:T(128)} %copy-done.7, bf16[256,1024]{1,0:T(8,128)(2,1)} %get-tuple-element.21.mixed_ref, bf16[4096,1280]{1,0:T(8,128)(2,1)} %all-gather.2.cloned.1.call-done.refs_0_.full_ref.refs_4_), custom_call_target="tpu_custom_call" | custom-call | flops 2147483648 | bytes 12582912 | tf_op jit(solution)/shard_map/spread/pallas_call | solution.py:268
  148.9 5.2 %collective-permute-start.14 = (bf16[256,1024]{1,0:T(8,128)(2,1)}, bf16[256,1024]{1,0:T(8,128)(2,1)S(1)}, u32[]{:S(2)}, u32[]{:S(2)}) collective-permute-start(bf16[256,1024]{1,0:T(8,128)(2,1)} %get-tuple-element.23), channel_id=1, source_target_pairs={{0,2},{1,3},{2,0},{3,1},{4,6},{5,7},{6,4},{7,5},{8,10},{9,11},{10,... | collective-permute-start | bytes 1572872 | tf_op jit(solution)/shard_map/ppermute | solution.py:287
  154.1 2.6 collective-permute-start.15
  156.6 4.5 %collective-permute-start.16 = (bf16[256,1024]{1,0:T(8,128)(2,1)}, bf16[256,1024]{1,0:T(8,128)(2,1)S(1)}, u32[]{:S(2)}, u32[]{:S(2)}) collective-permute-start(bf16[256,1024]{1,0:T(8,128)(2,1)} %get-tuple-element.25), channel_id=1, source_target_pairs={{0,3},{1,0},{2,1},{3,2},{4,7},{5,4},{6,5},{7,6},{8,11},{9,8},{10,9... | collective-permute-start | bytes 1572872 | tf_op jit(solution)/shard_map/ppermute | solution.py:287
  161.9 5.5 %collective-permute-done.15 = bf16[256,1024]{1,0:T(8,128)(2,1)S(1)} collective-permute-done((bf16[256,1024]{1,0:T(8,128)(2,1)}, bf16[256,1024]{1,0:T(8,128)(2,1)S(1)}, u32[]{:S(2)}, u32[]{:S(2)}) %collective-permute-start.15) | collective-permute-done | bytes 524320 | tf_op jit(solution)/shard_map/ppermute | solution.py:287
  171.1 2.1 collective-permute-start.17
  173.2 2.1 collective-permute-start.18
  175.3 2.1 collective-permute-start.19
  179.5 6.0 %fusion.15 = bf16[384,1024]{1,0:T(8,128)(2,1)S(1)} fusion(bf16[384,4096]{1,0:T(8,128)(2,1)S(1)} %bitcast.188, bf16[4096,1280]{1,0:T(8,128)(2,1)} %all-gather.2.cloned.1.call-done.refs_0_.full_ref.refs_4_), kind=kOutput, calls=%fused_computation.14 | convolution fusion | flops 3221618688 | bytes 12320768 | tf_op jit(solution)/shard_map/dot_general | solution.py:405
  189.2 13.1 %project_b.1 = (bf16[256,4096]{1,0:T(8,128)(2,1)}, bf16[256,1280]{1,0:T(8,128)(2,1)}, bf16[256,1024]{1,0:T(8,128)(2,1)}) custom-call(s32[7]{0:T(128)} %copy-done.7, f32[1,4096]{1,0:T(1,128)} %gain_ref.3, bf16[4,384,1024]{2,1,0:T(8,128)(2,1)} %all-to-all-done.known_ref, bf16[256,1024]{1,0:T(8,128)(2,1)} %collective-permute-done.17.refs_0_, ...), custom_call_target="tpu_custom_call" | custom-call | flops 2147483648 | bytes 18874368 | tf_op jit(solution)/shard_map/project_b/pallas_call | solution.py:232
  206.1 7.8 %convolution_convert_fusion = bf16[4096,1152]{1,0:T(8,128)(2,1)} fusion(bf16[128,4096]{1,0:T(8,128)(2,1)S(1)} %get-tuple-element.44, bf16[128,4096]{1,0:T(8,128)(2,1)S(1)} %get-tuple-element.43, bf16[128,4096]{1,0:T(8,128)(2,1)S(1)} %get-tuple-element.42, bf16[128,1152]{1,0:T(8,128)(2,1)S(1)} %get-tuple-element.53, ...), kind=kOutput, calls=%fused_computation | convolution fusion | flops 3640688640 | bytes 13467648 | tf_op jit(solution)/shard_map/dot_general | solution.py:415
  215.1 9.5 %fusion.4 = bf16[384,4096]{1,0:T(8,128)(2,1)S(1)} fusion(bf16[384,1024]{1,0:T(8,128)(2,1)S(1)} %pad_maximum_fusion.3, bf16[4096,1280]{1,0:T(8,128)(2,1)} %all-gather.2.cloned.1.call-done.refs_0_.full_ref.refs_4_), kind=kOutput, calls=%fused_computation.6 | convolution fusion | flops 3222798336 | bytes 12320768 | tf_op jit(solution)/shard_map/dot_general | solution.py:422
  226.7 5.5 %all-to-all-start.1 = ((bf16[4,384,1024]{2,1,0:T(8,128)(2,1)}), bf16[4,384,1024]{2,1,0:T(8,128)(2,1)}, u32[]{:S(2)}, u32[]{:S(2)}) async-start(bf16[4,384,1024]{2,1,0:T(8,128)(2,1)} %bitcast.189), calls=%async_computation.1 | async-start | bytes 6291456 | tf_op jit(solution)/shard_map/all_to_all | solution.py:424
  233.2 37.8 %all-to-all-done.1 = bf16[4,384,1024]{2,1,0:T(8,128)(2,1)} async-done(((bf16[4,384,1024]{2,1,0:T(8,128)(2,1)}), bf16[4,384,1024]{2,1,0:T(8,128)(2,1)}, u32[]{:S(2)}, u32[]{:S(2)}) %all-to-all-start.1) | async-done | bytes 3145760 | tf_op jit(solution)/shard_map/all_to_all | solution.py:424
  271.0 2.8 convert_reduce_fusion
  278.8 23.3 %reduce-scatter.2.cloned.1.call-done = bf16[256,1152]{1,0:T(8,128)(2,1)} async-done(((bf16[4096,1152]{1,0:T(8,128)(2,1)}), bf16[256,1152]{1,0:T(8,128)(2,1)}) %reduce-scatter.2.cloned.1.call-update) | async-done | bytes 589840 | tf_op jit(solution)/shard_map/reduce_scatter | solution.py:418
  (162 shorter events, 56.6 us)
Async XLA Ops:
  7.2 172.3 %copy-start = (bf16[1,3,1,128,4096]{4,3,2,1,0:T(8,128)(2,1)S(1)}, bf16[1,3,1,128,4096]{4,3,2,1,0:T(8,128)(2,1)}, u32[]{:S(2)}) copy-start(bf16[1,3,1,128,4096]{4,3,2,1,0:T(8,128)(2,1)} %param.21) | copy-start | bytes 9437188
  7.2 125.2 %all-gather.2.cloned.1.call-start = ((), (), s32[]{:S(2)}) async-start(), calls=%async_computation.3 | async-start | bytes 11141120 | tf_op jit(solution)/shard_map/all_gather | solution.py:328
  13.5 9.7 %collective-permute-start.3 = (bf16[256,512]{1,0:T(8,128)(2,1)}, bf16[256,512]{1,0:T(8,128)(2,1)}, u32[]{:S(2)}, u32[]{:S(2)}) collective-permute-start(bf16[256,512]{1,0:T(8,128)(2,1)} %get-tuple-element.57), channel_id=1, source_target_pairs={{0,16},{16,32},{32,48},{48,0},{1,17},{17,33},{33,49},{49,1},{2,18}... | collective-permute-start | bytes 786440 | tf_op jit(solution)/shard_map/ppermute | solution.py:283
  15.1 15.2 %collective-permute-start.4 = (bf16[256,512]{1,0:T(8,128)(2,1)}, bf16[256,512]{1,0:T(8,128)(2,1)}, u32[]{:S(2)}, u32[]{:S(2)}) collective-permute-start(bf16[256,512]{1,0:T(8,128)(2,1)} %get-tuple-element.57), channel_id=1, source_target_pairs={{0,48},{16,0},{32,16},{48,32},{1,49},{17,1},{33,17},{49,33},{2,50}... | collective-permute-start | bytes 786440 | tf_op jit(solution)/shard_map/ppermute | solution.py:283
  16.7 15.4 %collective-permute-start.5 = (bf16[256,512]{1,0:T(8,128)(2,1)}, bf16[256,512]{1,0:T(8,128)(2,1)}, u32[]{:S(2)}, u32[]{:S(2)}) collective-permute-start(bf16[256,512]{1,0:T(8,128)(2,1)} %get-tuple-element.57), channel_id=1, source_target_pairs={{0,32},{16,48},{32,0},{48,16},{1,33},{17,49},{33,1},{49,17},{2,34}... | collective-permute-start | bytes 786440 | tf_op jit(solution)/shard_map/ppermute | solution.py:283
  18.8 15.7 %collective-permute-start.2 = (bf16[256,512]{1,0:T(8,128)(2,1)}, bf16[256,512]{1,0:T(8,128)(2,1)}, u32[]{:S(2)}, u32[]{:S(2)}) collective-permute-start(bf16[256,512]{1,0:T(8,128)(2,1)} %get-tuple-element.56), channel_id=1, source_target_pairs={{0,8},{4,12},{8,0},{12,4},{1,9},{5,13},{9,1},{13,5},{2,10},{6,14},... | collective-permute-start | bytes 786440 | tf_op jit(solution)/shard_map/ppermute | solution.py:283
  21.8 19.8 %collective-permute-start = (bf16[256,512]{1,0:T(8,128)(2,1)}, bf16[256,512]{1,0:T(8,128)(2,1)}, u32[]{:S(2)}, u32[]{:S(2)}) collective-permute-start(bf16[256,512]{1,0:T(8,128)(2,1)} %get-tuple-element.56), channel_id=1, source_target_pairs={{0,4},{4,8},{8,12},{12,0},{1,5},{5,9},{9,13},{13,1},{2,6},{6,10},{... | collective-permute-start | bytes 786440 | tf_op jit(solution)/shard_map/ppermute | solution.py:283
  23.2 18.4 %collective-permute-start.1 = (bf16[256,512]{1,0:T(8,128)(2,1)}, bf16[256,512]{1,0:T(8,128)(2,1)}, u32[]{:S(2)}, u32[]{:S(2)}) collective-permute-start(bf16[256,512]{1,0:T(8,128)(2,1)} %get-tuple-element.56), channel_id=1, source_target_pairs={{0,12},{4,0},{8,4},{12,8},{1,13},{5,1},{9,5},{13,9},{2,14},{6,2},{... | collective-permute-start | bytes 786440 | tf_op jit(solution)/shard_map/ppermute | solution.py:283
  48.0 67.1 %all-to-all-start = ((bf16[4,384,1024]{2,1,0:T(8,128)(2,1)}), bf16[4,384,1024]{2,1,0:T(8,128)(2,1)}, u32[]{:S(2)}, u32[]{:S(2)}) async-start(bf16[4,384,1024]{2,1,0:T(8,128)(2,1)} %broadcast_in_dim.196), calls=%async_computation | async-start | bytes 6291456 | tf_op jit(solution)/shard_map/all_to_all | solution.py:368
  54.1 61.0 %copy-start.6 = (f32[1,4096]{1,0:T(1,128)S(1)}, f32[1,4096]{1,0:T(1,128)}, u32[]{:S(2)}) copy-start(f32[1,4096]{1,0:T(1,128)} %gain_ref.3) | copy-start | bytes 49156
  54.1 248.0 %reduce-scatter.2.cloned.1.call-start = ((), (), s32[]{:S(2)}) async-start(), calls=%async_computation.4 | async-start | bytes 10027008 | tf_op jit(solution)/shard_map/reduce_scatter | solution.py:418
  54.1 47.2 %collective-permute-start.10 = (bf16[4,256,512]{2,1,0:T(8,128)(2,1)}, bf16[4,256,512]{2,1,0:T(8,128)(2,1)S(1)}, u32[]{:S(2)}, u32[]{:S(2)}) collective-permute-start(bf16[4,256,512]{2,1,0:T(8,128)(2,1)} %pad_maximum_fusion.1.refs_6_.refs_10_), channel_id=1, source_target_pairs={{0,4},{4,8},{8,12},{12,0},{1,5},{5,9},{9,13},{13,1},{2,6},{6,10},{... | collective-permute-start | bytes 3145736 | tf_op jit(solution)/shard_map/ppermute | solution.py:283
  56.6 48.9 %collective-permute-start.11 = (bf16[4,256,512]{2,1,0:T(8,128)(2,1)}, bf16[4,256,512]{2,1,0:T(8,128)(2,1)S(1)}, u32[]{:S(2)}, u32[]{:S(2)}) collective-permute-start(bf16[4,256,512]{2,1,0:T(8,128)(2,1)} %pad_maximum_fusion.1.refs_6_.refs_10_), channel_id=1, source_target_pairs={{0,12},{4,0},{8,4},{12,8},{1,13},{5,1},{9,5},{13,9},{2,14},{6,2},{... | collective-permute-start | bytes 3145736 | tf_op jit(solution)/shard_map/ppermute | solution.py:283
  57.3 50.8 %collective-permute-start.6 = (bf16[4,256,512]{2,1,0:T(8,128)(2,1)}, bf16[4,256,512]{2,1,0:T(8,128)(2,1)S(1)}, u32[]{:S(2)}, u32[]{:S(2)}) collective-permute-start(bf16[4,256,512]{2,1,0:T(8,128)(2,1)} %pad_maximum_fusion.refs_1_.refs_5_), channel_id=1, source_target_pairs={{0,16},{16,32},{32,48},{48,0},{1,17},{17,33},{33,49},{49,1},{2,18}... | collective-permute-start | bytes 3145736 | tf_op jit(solution)/shard_map/ppermute | solution.py:283
  57.7 52.5 %collective-permute-start.7 = (bf16[4,256,512]{2,1,0:T(8,128)(2,1)}, bf16[4,256,512]{2,1,0:T(8,128)(2,1)S(1)}, u32[]{:S(2)}, u32[]{:S(2)}) collective-permute-start(bf16[4,256,512]{2,1,0:T(8,128)(2,1)} %pad_maximum_fusion.refs_1_.refs_5_), channel_id=1, source_target_pairs={{0,48},{16,0},{32,16},{48,32},{1,49},{17,1},{33,17},{49,33},{2,50}... | collective-permute-start | bytes 3145736 | tf_op jit(solution)/shard_map/ppermute | solution.py:283
  103.1 24.6 %collective-permute-start.12 = (bf16[2,256,512]{2,1,0:T(8,128)(2,1)}, bf16[2,256,512]{2,1,0:T(8,128)(2,1)}, u32[]{:S(2)}, u32[]{:S(2)}) collective-permute-start(bf16[2,256,512]{2,1,0:T(8,128)(2,1)} %slice.279), channel_id=1, source_target_pairs={{0,4},{4,8},{8,12},{12,0},{1,5},{5,9},{9,13},{13,1},{2,6},{6,10},{... | collective-permute-start | bytes 1572872 | tf_op jit(solution)/shard_map/ppermute | solution.py:283
  107.3 23.0 %collective-permute-start.13 = (bf16[2,256,512]{2,1,0:T(8,128)(2,1)}, bf16[2,256,512]{2,1,0:T(8,128)(2,1)}, u32[]{:S(2)}, u32[]{:S(2)}) collective-permute-start(bf16[2,256,512]{2,1,0:T(8,128)(2,1)} %slice.280), channel_id=1, source_target_pairs={{0,12},{4,0},{8,4},{12,8},{1,13},{5,1},{9,5},{13,9},{2,14},{6,2},{... | collective-permute-start | bytes 1572872 | tf_op jit(solution)/shard_map/ppermute | solution.py:283
  110.0 22.4 %collective-permute-start.8 = (bf16[2,256,512]{2,1,0:T(8,128)(2,1)}, bf16[2,256,512]{2,1,0:T(8,128)(2,1)}, u32[]{:S(2)}, u32[]{:S(2)}) collective-permute-start(bf16[2,256,512]{2,1,0:T(8,128)(2,1)} %slice.277), channel_id=1, source_target_pairs={{0,16},{16,32},{32,48},{48,0},{1,17},{17,33},{33,49},{49,1},{2,18}... | collective-permute-start | bytes 1572872 | tf_op jit(solution)/shard_map/ppermute | solution.py:283
  112.1 20.3 %collective-permute-start.9 = (bf16[2,256,512]{2,1,0:T(8,128)(2,1)}, bf16[2,256,512]{2,1,0:T(8,128)(2,1)}, u32[]{:S(2)}, u32[]{:S(2)}) collective-permute-start(bf16[2,256,512]{2,1,0:T(8,128)(2,1)} %slice.278), channel_id=1, source_target_pairs={{0,48},{16,0},{32,16},{48,32},{1,49},{17,1},{33,17},{49,33},{2,50}... | collective-permute-start | bytes 1572872 | tf_op jit(solution)/shard_map/ppermute | solution.py:283
  148.9 20.7 %copy-start.9 = (bf16[1,2,2,128,1024]{4,3,2,1,0:T(8,128)(2,1)S(1)}, bf16[1,2,2,128,1024]{4,3,2,1,0:T(8,128)(2,1)}, u32[]{:S(2)}) copy-start(bf16[1,2,2,128,1024]{4,3,2,1,0:T(8,128)(2,1)} %param.11) | copy-start | bytes 3145732
  148.9 13.0 %collective-permute-start.14 = (bf16[256,1024]{1,0:T(8,128)(2,1)}, bf16[256,1024]{1,0:T(8,128)(2,1)S(1)}, u32[]{:S(2)}, u32[]{:S(2)}) collective-permute-start(bf16[256,1024]{1,0:T(8,128)(2,1)} %get-tuple-element.23), channel_id=1, source_target_pairs={{0,2},{1,3},{2,0},{3,1},{4,6},{5,7},{6,4},{7,5},{8,10},{9,11},{10,... | collective-permute-start | bytes 1572872 | tf_op jit(solution)/shard_map/ppermute | solution.py:287
  154.1 13.3 %collective-permute-start.15 = (bf16[256,1024]{1,0:T(8,128)(2,1)}, bf16[256,1024]{1,0:T(8,128)(2,1)S(1)}, u32[]{:S(2)}, u32[]{:S(2)}) collective-permute-start(bf16[256,1024]{1,0:T(8,128)(2,1)} %get-tuple-element.24), channel_id=1, source_target_pairs={{0,1},{1,2},{2,3},{3,0},{4,5},{5,6},{6,7},{7,4},{8,9},{9,10},{10,1... | collective-permute-start | bytes 1572872 | tf_op jit(solution)/shard_map/ppermute | solution.py:287
  156.6 11.5 %collective-permute-start.16 = (bf16[256,1024]{1,0:T(8,128)(2,1)}, bf16[256,1024]{1,0:T(8,128)(2,1)S(1)}, u32[]{:S(2)}, u32[]{:S(2)}) collective-permute-start(bf16[256,1024]{1,0:T(8,128)(2,1)} %get-tuple-element.25), channel_id=1, source_target_pairs={{0,3},{1,0},{2,1},{3,2},{4,7},{5,4},{6,5},{7,6},{8,11},{9,8},{10,9... | collective-permute-start | bytes 1572872 | tf_op jit(solution)/shard_map/ppermute | solution.py:287
  171.1 16.4 %collective-permute-start.17 = (bf16[256,1024]{1,0:T(8,128)(2,1)S(1)}, bf16[256,1024]{1,0:T(8,128)(2,1)}, u32[]{:S(2)}, u32[]{:S(2)}) collective-permute-start(bf16[256,1024]{1,0:T(8,128)(2,1)S(1)} %pad_maximum_fusion.5), channel_id=1, source_target_pairs={{0,64},{1,65},{2,66},{3,67},{4,68},{5,69},{6,70},{7,71},{8,72},{9,... | collective-permute-start | bytes 1572872 | tf_op jit(solution)/shard_map/ppermute | solution.py:287
  173.2 14.3 %collective-permute-start.18 = (bf16[256,1024]{1,0:T(8,128)(2,1)S(1)}, bf16[256,1024]{1,0:T(8,128)(2,1)}, u32[]{:S(2)}, u32[]{:S(2)}) collective-permute-start(bf16[256,1024]{1,0:T(8,128)(2,1)S(1)} %pad_maximum_fusion.5), channel_id=1, source_target_pairs={{0,65},{1,66},{2,67},{3,64},{4,69},{5,70},{6,71},{7,68},{8,73},{9,... | collective-permute-start | bytes 1572872 | tf_op jit(solution)/shard_map/ppermute | solution.py:287
  175.3 12.2 %collective-permute-start.19 = (bf16[256,1024]{1,0:T(8,128)(2,1)S(1)}, bf16[256,1024]{1,0:T(8,128)(2,1)}, u32[]{:S(2)}, u32[]{:S(2)}) collective-permute-start(bf16[256,1024]{1,0:T(8,128)(2,1)S(1)} %pad_maximum_fusion.5), channel_id=1, source_target_pairs={{0,66},{1,67},{2,64},{3,65},{4,70},{5,71},{6,68},{7,69},{8,74},{9,... | collective-permute-start | bytes 1572872 | tf_op jit(solution)/shard_map/ppermute | solution.py:287
  177.4 11.8 %collective-permute-start.20 = (bf16[256,1024]{1,0:T(8,128)(2,1)S(1)}, bf16[256,1024]{1,0:T(8,128)(2,1)}, u32[]{:S(2)}, u32[]{:S(2)}) collective-permute-start(bf16[256,1024]{1,0:T(8,128)(2,1)S(1)} %pad_maximum_fusion.5), channel_id=1, source_target_pairs={{0,67},{1,64},{2,65},{3,66},{4,71},{5,68},{6,69},{7,70},{8,75},{9,... | collective-permute-start | bytes 1572872 | tf_op jit(solution)/shard_map/ppermute | solution.py:287
  226.7 44.3 %all-to-all-start.1 = ((bf16[4,384,1024]{2,1,0:T(8,128)(2,1)}), bf16[4,384,1024]{2,1,0:T(8,128)(2,1)}, u32[]{:S(2)}, u32[]{:S(2)}) async-start(bf16[4,384,1024]{2,1,0:T(8,128)(2,1)} %bitcast.189), calls=%async_computation.1 | async-start | bytes 6291456 | tf_op jit(solution)/shard_map/all_to_all | solution.py:424
  233.1 40.7 %copy-start.28 = (bf16[1,1,1,128,1024]{4,3,2,1,0:T(8,128)(2,1)S(1)}, bf16[1,1,1,128,1024]{4,3,2,1,0:T(8,128)(2,1)}, u32[]{:S(2)}) copy-start(bf16[1,1,1,128,1024]{4,3,2,1,0:T(8,128)(2,1)} %copy-done.27) | copy-start | bytes 786436
  233.1 40.7 %copy-start.30 = (bf16[128,1024]{1,0:T(8,128)(2,1)S(1)}, bf16[128,1024]{1,0:T(8,128)(2,1)}, u32[]{:S(2)}) copy-start(bf16[128,1024]{1,0:T(8,128)(2,1)} %copy-done.29) | copy-start | bytes 786436
  233.2 41.1 %copy-start.13 = (bf16[2,128,1024]{2,1,0:T(8,128)(2,1)S(1)}, bf16[2,128,1024]{2,1,0:T(8,128)(2,1)}, u32[]{:S(2)}) copy-start(bf16[2,128,1024]{2,1,0:T(8,128)(2,1)} %copy-done.12) | copy-start | bytes 1572868
  277.3 28.2 %copy-start.1 = (bf16[1,3,1,128,4096]{4,3,2,1,0:T(8,128)(2,1)S(1)}, bf16[1,3,1,128,4096]{4,3,2,1,0:T(8,128)(2,1)}, u32[]{:S(2)}) copy-start(bf16[1,3,1,128,4096]{4,3,2,1,0:T(8,128)(2,1)} %param.21) | copy-start | bytes 9437188
  (33 other events, 185.5 us)
Sparse Core Ops, SparseCore 0:
  11.6 119.8 all-gather.1
  214.0 88.0 reduce-scatter.1
where the time goes:
time: 313 us; the launch traced here: 312 us
  waiting for transfers between devices  132 us (42%)
  starting transfers between devices  56.9 us (18%)
  Pallas kernels  37.6 us (12%)
  matrix products  23.2 us (7%)
  local copies, waits for them, and re-layouts  22.7 us (7%)
  other arithmetic  21.8 us (7%)
  between operations  18.4 us (6%)
    ppermute x14, waiting for transfers between devices, around(): return lax.ppermute(shard, axis, [(i, (i + by) % 4) for i in range(4)])  61.8 us
    all_to_all x1, waiting for transfers between devices, on_device(): lax.all_to_all(parts, 'tensor', split_axis=0, concat_axis=0, tiled=True)  37.8 us
    ppermute x14, starting transfers between devices, around(): return lax.ppermute(shard, axis, [(i, (i + by) % 4) for i in range(4)])  24.6 us
    reduce_scatter x1, waiting for transfers between devices, on_device(): grad = lax.psum_scatter(term, ('y', 'x'), scatter_dimension=0, tiled=True)  23.3 us
    pallas_call x2, Pallas kernels, project_call(): pl.pallas_call(kernel, in_specs=[SMEM] + [VMEM] * (len(operands) - 1) + [...  23.1 us
    ppermute x7, starting transfers between devices, from_first(): lax.ppermute(shard, ('section', 'tensor'), [(i, 4 * to_section + (i + by)...  20.7 us
    dot_general x1, matrix products, on_device(): lax.dot_general(mixed_f, full_o, NT, preferred_element_type=f32)  9.52 us
    unnamed x81, local copies, waits for them, and re-layouts  9.15 us
  transfers between devices with their start and end apart: 25, of which 13 were waited for; matrix products, arithmetic and copies ran while one was open for 13% of the time, Pallas kernels for 2%

commit v1 on v0

--- a/solution.py
+++ b/solution.py
@@ -85,7 +85,6 @@
 
 
 ROWS = 16
-HALF = 512
 ORDER = (0, 3, 1, 2)
 
 
@@ -168,36 +167,30 @@
     full_ref, pieces = pieces[0], pieces[1:]
     copies = []
     for at in range(5):
-        for half in range(2):
-            target = held.at[half, at] if at < 3 else held.at[half, 3, pl.ds(2 * (at - 3), 2)]
-            copies.append(
-                pltpu.make_async_copy(pieces[half * 5 + at], target, sems.at[2 * at + half])
-            )
-    copies.append(pltpu.make_async_copy(full_ref.at[:, pl.ds(1024, 256)], held_kv, sems.at[10]))
+        target = held.at[at] if at < 3 else held.at[3, pl.ds(2 * (at - 3), 2)]
+        copies.append(pltpu.make_async_copy(pieces[at], target, sems.at[at]))
+    copies.append(pltpu.make_async_copy(full_ref.at[:, pl.ds(1024, 256)], held_kv, sems.at[5]))
     for copy in copies:
         copy.start()
     begin()
-    totals = [None, None]
+    total = None
     for at in range(4):
-        for half in range(2):
-            lhs = []
-            for block in range(4):
-                along, across = ORDER[at], ORDER[block]
-                dy, dx = (along, across) if half == 0 else (across, along)
-                row = lax.rem(flags[5] + dy, 4) * 4 + lax.rem(flags[4] + dx, 4)
-                lhs.append(normed_ref[:, pl.ds(pl.multiple_of(row * 256, 256), 256)])
-            copies[2 * at + half].wait()
-            if at == 3:
-                copies[8 + half].wait()
-            part = jnp.dot(
-                jnp.concatenate(lhs, axis=1),
-                held[half, at].reshape(1024, HALF),
-                preferred_element_type=f32,
-            )
-            totals[half] = part if totals[half] is None else totals[half] + part
-    for half in range(2):
-        qkv_ref[:, half * HALF : (half + 1) * HALF] = totals[half].astype(bf16)
-    copies[10].wait()
+        lhs = []
+        for block in range(4):
+            second, inner = ORDER[at], ORDER[block]
+            dy = jnp.where(flags[0] == 1, second, inner)
+            dx = jnp.where(flags[0] == 1, inner, second)
+            row = lax.rem(flags[5] + dy, 4) * 4 + lax.rem(flags[4] + dx, 4)
+            lhs.append(normed_ref[:, pl.ds(pl.multiple_of(row * 256, 256), 256)])
+        copies[at].wait()
+        if at == 3:
+            copies[4].wait()
+        part = jnp.dot(
+            jnp.concatenate(lhs, axis=1), held[at].reshape(1024, 1024), preferred_element_type=f32
+        )
+        total = part if total is None else total + part
+    qkv_ref[:, :1024] = total.astype(bf16)
+    copies[5].wait()
     qkv_ref[:, 1024:] = jnp.dot(
         normed_ref[...], held_kv[...], preferred_element_type=f32
     ).astype(bf16)
@@ -207,13 +200,13 @@
 
 
 def project_a_kernel(flags, normed_ref, *refs):
-    pieces, (qkv_ref, mixed_ref, held, held_kv, sems) = refs[:11], refs[11:]
+    pieces, (qkv_ref, mixed_ref, held, held_kv, sems) = refs[:6], refs[6:]
     project_kernel(flags, pieces, normed_ref, qkv_ref, mixed_ref, held, held_kv, sems, lambda: None)
 
 
 def project_b_kernel(flags, gain_ref, known_ref, *refs):
-    got_refs, pieces = refs[:4], refs[4:15]
-    normed_ref, qkv_ref, mixed_ref, held, held_kv, sems = refs[15:]
+    got_refs, pieces = refs[:4], refs[4:10]
+    normed_ref, qkv_ref, mixed_ref, held, held_kv, sems = refs[10:]
 
     def begin():
         known_b(flags, known_ref, got_refs, normed_ref)
@@ -231,17 +224,17 @@
     ][0 if with_normed else 1 :]
     return pl.pallas_call(
         kernel,
-        in_specs=[SMEM] + [VMEM] * (len(operands) - 1) + [ANY] * 11,
+        in_specs=[SMEM] + [VMEM] * (len(operands) - 1) + [ANY] * 6,
         out_specs=[VMEM] * len(shapes),
         out_shape=shapes,
         scratch_shapes=[
-            pltpu.VMEM((2, 4, 4, 256, HALF), bf16),
+            pltpu.VMEM((4, 4, 256, 1024), bf16),
             pltpu.VMEM((4096, 256), bf16),
-            pltpu.SemaphoreType.DMA((11,)),
+            pltpu.SemaphoreType.DMA((6,)),
         ],
         compiler_params=GRANT,
         cost_estimate=pl.CostEstimate(
-            flops=2 * rows * 4096 * 2 * HALF, bytes_accessed=18 * 2**20, transcendentals=rows * 1024
+            flops=2 * rows * 4096 * 1280, bytes_accessed=18 * 2**20, transcendentals=rows * 1024
         ),
         name=name,
     )(*operands, *pieces)
@@ -279,8 +272,14 @@
     )(flags, mixed, full)
 
 
-def around(shard, axis, by):
-    return lax.ppermute(shard, axis, [(i, (i + by) % 4) for i in range(4)])
+def along(shard, second, by):
+    pairs = []
+    for y in range(4):
+        for x in range(4):
+            by_x, by_y = y * 4 + (x + by) % 4, (y + by) % 4 * 4 + x
+            pairs.append((y * 4 + x, by_y if second else by_x))
+            pairs.append((16 + y * 4 + x, 16 + (by_x if second else by_y)))
+    return lax.ppermute(shard, ("section", "y", "x"), pairs)
 
 
 def from_first(shard, by, to_section):
@@ -289,14 +288,11 @@
     )
 
 
-def gathered(shard, axis):
-    before, after, far = around(shard, axis, 1), around(shard, axis, -1), around(shard, axis, 2)
-    return jnp.stack([shard, before, after, far])
-
-
-def spread_on(own, then):
-    before, after = around(own, then, 1), around(own, then, -1)
-    return [own, before, after, around(before[:2], then, 1), around(after[2:], then, -1)]
+def gathered(shard):
+    before, after, far = along(shard, False, 1), along(shard, False, -1), along(shard, False, 2)
+    own = jnp.stack([shard, before, after, far])
+    before, after = along(own, True, 1), along(own, True, -1)
+    return [own, before, after, along(before[:2], True, 1), along(after[2:], True, -1)]
 
 
 def pick(state, slot):
@@ -325,14 +321,10 @@
     z = lax.axis_index("tensor")
 
     packed = jnp.concatenate([w_out[0].T, w_key[0], w_value[0]], axis=1)
+    arriving, first_delta, packed = lax.optimization_barrier((arriving, first_delta, packed))
     full = lax.all_gather(packed, ("y", "x"), axis=0, tiled=True)
     full_o = full[:, :1024]
-    own_a = gathered(w_query[0, :, :HALF], "x")
-    own_b = gathered(w_query[0, :, HALF:], "y")
-    arriving, first_delta, own_a, own_b = lax.optimization_barrier(
-        (arriving, first_delta, own_a, own_b)
-    )
-    pieces = [full] + spread_on(own_a, "y") + spread_on(own_b, "x")
+    pieces = [full] + gathered(w_query[0])
 
     power = exponents.astype(f32)
     scale_full = jnp.repeat(jnp.exp2(power), QB, axis=1)

time: 313 us -> 300 us (0.958)
  starting transfers between devices: 56.9 us -> 46.6 us
  local copies, waits for them, and re-layouts: 22.7 us -> 18.7 us
    ppermute x14 -> x7, starting transfers between devices: 24.6 us -> 11.9 us  [along(): return lax.ppermute(shard, ('section', 'y', 'x'), pairs)]
    unnamed x81 -> x73, local copies, waits for them, and re-layouts: 9.15 us -> 5.87 us
    ppermute x14 -> x7, waiting for transfers between devices: 61.8 us -> 60.9 us  [along(): return lax.ppermute(shard, ('section', 'y', 'x'), pairs)]
  transfers between devices with their start and end apart: 25 -> 18, of which waited for: 13 -> 9; matrix products, arithmetic and copies ran while one was open for 13% -> 14% of each run, Pallas kernels for 2% -> 2%
where the time goes in v1:
time: 300 us; the launch traced here: 299 us
  waiting for transfers between devices  132 us (44%)
  starting transfers between devices  46.6 us (16%)
  Pallas kernels  36.7 us (12%)
  other arithmetic  23.6 us (8%)
  matrix products  23.1 us (8%)
  local copies, waits for them, and re-layouts  18.7 us (6%)
  between operations  18.6 us (6%)
    ppermute x7, waiting for transfers between devices, along(): return lax.ppermute(shard, ('section', 'y', 'x'), pairs)  60.9 us
    all_to_all x1, waiting for transfers between devices, on_device(): lax.all_to_all(parts, 'tensor', split_axis=0, concat_axis=0, tiled=True)  37.9 us
    reduce_scatter x1, waiting for transfers between devices, on_device(): grad = lax.psum_scatter(term, ('y', 'x'), scatter_dimension=0, tiled=True)  24.2 us
    pallas_call x2, Pallas kernels, project_call(): pl.pallas_call(kernel, in_specs=[SMEM] + [VMEM] * (len(operands) - 1) + [...  22.1 us
    ppermute x7, starting transfers between devices, from_first(): lax.ppermute(shard, ('section', 'tensor'), [(i, 4 * to_section + (i + by)...  21.6 us
    ppermute x7, starting transfers between devices, along(): return lax.ppermute(shard, ('section', 'y', 'x'), pairs)  11.9 us
    dot_general x1, matrix products, on_device(): lax.dot_general(mixed_f, full_o, NT, preferred_element_type=f32)  9.43 us
    ppermute x7, waiting for transfers between devices, from_first(): lax.ppermute(shard, ('section', 'tensor'), [(i, 4 * to_section + (i + by)...  8.6 us
  transfers between devices with their start and end apart: 18, of which 9 were waited for; matrix products, arithmetic and copies ran while one was open for 14% of the time, Pallas kernels for 2%

profile of v1, /device:TPU:0, one launch (start us, length us, event | category | flops | bytes accessed | tf_op | source)
XLA Modules:
  0.0 298.9 jit_solution(2959915353471822381)
XLA Ops:
  7.2 2.2 copy.15
  9.4 2.1 pad_maximum_fusion.3
  14.8 1.9 collective-permute-start.2
  25.2 4.6 %collective-permute-done.2 = bf16[256,1024]{1,0:T(8,128)(2,1)} collective-permute-done((bf16[256,1024]{1,0:T(8,128)(2,1)}, bf16[256,1024]{1,0:T(8,128)(2,1)}, u32[]{:S(2)}, u32[]{:S(2)}) %collective-permute-start.2) | collective-permute-done | bytes 524320 | tf_op jit(solution)/shard_map/ppermute | solution.py:282
  29.8 3.1 %pad_maximum_fusion.refs_1_.refs_5_ = bf16[4,256,1024]{2,1,0:T(8,128)(2,1)} fusion(bf16[1,256,1024]{2,1,0:T(8,128)(2,1)} %bitcast.35, bf16[1,256,1024]{2,1,0:T(8,128)(2,1)} %bitcast.34, bf16[1,256,1024]{2,1,0:T(8,128)(2,1)} %bitcast.33, bf16[1,256,1024]{2,1,0:T(8,128)(2,1)S(1)} %copy-done.33), kind=kLoop, calls=%fused_computation.13 | loop fusion | flops 3145728 | bytes 4194304 | tf_op jit(solution)/shard_map/stack | solution.py:293
  37.7 2.0 broadcast_in_dim.196
  39.7 7.5 %all-to-all-start = ((bf16[4,384,1024]{2,1,0:T(8,128)(2,1)}), bf16[4,384,1024]{2,1,0:T(8,128)(2,1)}, u32[]{:S(2)}, u32[]{:S(2)}) async-start(bf16[4,384,1024]{2,1,0:T(8,128)(2,1)} %broadcast_in_dim.196), calls=%async_computation | async-start | bytes 6291456 | tf_op jit(solution)/shard_map/all_to_all | solution.py:360
  47.2 33.1 %collective-permute-done.3.refs_2_.refs_6_ = bf16[4,256,1024]{2,1,0:T(8,128)(2,1)} collective-permute-done((bf16[4,256,1024]{2,1,0:T(8,128)(2,1)}, bf16[4,256,1024]{2,1,0:T(8,128)(2,1)}, u32[]{:S(2)}, u32[]{:S(2)}) %collective-permute-start.3) | collective-permute-done | bytes 2097184 | tf_op jit(solution)/shard_map/ppermute | solution.py:282
  80.3 2.3 slice.261
  82.6 2.5 collective-permute-start.5
  85.1 2.3 slice.262
  88.3 4.5 %prepare.1.normed_ref = bf16[256,4096]{1,0:T(8,128)(2,1)S(1)} custom-call(s32[7]{0:T(128)S(1)} %stack.52.flags, f32[1,4096]{1,0:T(1,128)S(1)} %copy-done.6, bf16[4,384,1024]{2,1,0:T(8,128)(2,1)} %all-to-all-done.known_ref), custom_call_target="tpu_custom_call" | custom-call | flops 8388608 | bytes 5242880 | tf_op jit(solution)/shard_map/prepare/pallas_call | solution.py:155
  94.0 23.2 %collective-permute-done.5.refs_4_.refs_8_ = bf16[2,256,1024]{2,1,0:T(8,128)(2,1)} collective-permute-done((bf16[2,256,1024]{2,1,0:T(8,128)(2,1)}, bf16[2,256,1024]{2,1,0:T(8,128)(2,1)}, u32[]{:S(2)}, u32[]{:S(2)}) %collective-permute-start.5) | collective-permute-done | bytes 1048608 | tf_op jit(solution)/shard_map/ppermute | solution.py:282
  117.2 9.8 %project_a.1 = (bf16[256,1280]{1,0:T(8,128)(2,1)}, bf16[256,1024]{1,0:T(8,128)(2,1)}) custom-call(s32[7]{0:T(128)} %copy-done.7, bf16[256,4096]{1,0:T(8,128)(2,1)} %copy-done.2, bf16[4096,1280]{1,0:T(8,128)(2,1)} %all-gather.2.cloned.1.call-done.refs_0_.full_ref.refs_4_, bf16[4,256,1024]{2,1,0:T(8,128)(2,1)} %pad_maximum_fusion.refs_1_.refs_5_, ...), custom_call_target="tpu_custom_call" | custom-call | flops 2684354560 | bytes 18874368 | tf_op jit(solution)/shard_map/project_a/pallas_call | solution.py:225
  127.0 6.5 %spread.1 = (bf16[256,1024]{1,0:T(8,128)(2,1)}, bf16[256,1024]{1,0:T(8,128)(2,1)}, bf16[256,1024]{1,0:T(8,128)(2,1)}, bf16[256,1024]{1,0:T(8,128)(2,1)}) custom-call(s32[7]{0:T(128)} %copy-done.7, bf16[256,1024]{1,0:T(8,128)(2,1)} %get-tuple-element.19.mixed_ref, bf16[4096,1280]{1,0:T(8,128)(2,1)} %all-gather.2.cloned.1.call-done.refs_0_.full_ref.refs_4_), custom_call_target="tpu_custom_call" | custom-call | flops 2147483648 | bytes 12582912 | tf_op jit(solution)/shard_map/spread/pallas_call | solution.py:261
  133.5 6.0 %collective-permute-start.7 = (bf16[256,1024]{1,0:T(8,128)(2,1)}, bf16[256,1024]{1,0:T(8,128)(2,1)S(1)}, u32[]{:S(2)}, u32[]{:S(2)}) collective-permute-start(bf16[256,1024]{1,0:T(8,128)(2,1)} %get-tuple-element.21), channel_id=1, source_target_pairs={{0,2},{1,3},{2,0},{3,1},{4,6},{5,7},{6,4},{7,5},{8,10},{9,11},{10,... | collective-permute-start | bytes 1572872 | tf_op jit(solution)/shard_map/ppermute | solution.py:286
  139.6 2.9 collective-permute-start.8
  142.5 4.3 %collective-permute-start.9 = (bf16[256,1024]{1,0:T(8,128)(2,1)}, bf16[256,1024]{1,0:T(8,128)(2,1)S(1)}, u32[]{:S(2)}, u32[]{:S(2)}) collective-permute-start(bf16[256,1024]{1,0:T(8,128)(2,1)} %get-tuple-element.23), channel_id=1, source_target_pairs={{0,3},{1,0},{2,1},{3,2},{4,7},{5,4},{6,5},{7,6},{8,11},{9,8},{10,9... | collective-permute-start | bytes 1572872 | tf_op jit(solution)/shard_map/ppermute | solution.py:286
  147.0 5.6 %collective-permute-done.8 = bf16[256,1024]{1,0:T(8,128)(2,1)S(1)} collective-permute-done((bf16[256,1024]{1,0:T(8,128)(2,1)}, bf16[256,1024]{1,0:T(8,128)(2,1)S(1)}, u32[]{:S(2)}, u32[]{:S(2)}) %collective-permute-start.8) | collective-permute-done | bytes 524320 | tf_op jit(solution)/shard_map/ppermute | solution.py:286
  157.2 2.1 collective-permute-start.10
  159.3 2.1 collective-permute-start.11
  161.4 2.1 collective-permute-start.12
  163.5 2.1 collective-permute-start.13
  165.6 6.0 %fusion.15 = bf16[384,1024]{1,0:T(8,128)(2,1)S(1)} fusion(bf16[384,4096]{1,0:T(8,128)(2,1)S(1)} %bitcast.182, bf16[4096,1280]{1,0:T(8,128)(2,1)} %all-gather.2.cloned.1.call-done.refs_0_.full_ref.refs_4_), kind=kOutput, calls=%fused_computation.15 | convolution fusion | flops 3221618688 | bytes 12320768 | tf_op jit(solution)/shard_map/dot_general | solution.py:397
  175.2 12.3 %project_b.1 = (bf16[256,4096]{1,0:T(8,128)(2,1)}, bf16[256,1280]{1,0:T(8,128)(2,1)}, bf16[256,1024]{1,0:T(8,128)(2,1)}) custom-call(s32[7]{0:T(128)} %copy-done.7, f32[1,4096]{1,0:T(1,128)} %gain_ref.3, bf16[4,384,1024]{2,1,0:T(8,128)(2,1)} %all-to-all-done.known_ref, bf16[256,1024]{1,0:T(8,128)(2,1)} %collective-permute-done.10.refs_0_, ...), custom_call_target="tpu_custom_call" | custom-call | flops 2684354560 | bytes 18874368 | tf_op jit(solution)/shard_map/project_b/pallas_call | solution.py:225
  191.3 7.8 %convolution_convert_fusion = bf16[4096,1152]{1,0:T(8,128)(2,1)} fusion(bf16[128,4096]{1,0:T(8,128)(2,1)S(1)} %get-tuple-element.42, bf16[128,4096]{1,0:T(8,128)(2,1)S(1)} %get-tuple-element.41, bf16[128,4096]{1,0:T(8,128)(2,1)S(1)} %get-tuple-element.40, bf16[128,1152]{1,0:T(8,128)(2,1)S(1)} %get-tuple-element.51, ...), kind=kOutput, calls=%fused_computation | convolution fusion | flops 3640688640 | bytes 13467648 | tf_op jit(solution)/shard_map/dot_general | solution.py:407
  200.4 9.4 %fusion.4 = bf16[384,4096]{1,0:T(8,128)(2,1)S(1)} fusion(bf16[384,1024]{1,0:T(8,128)(2,1)S(1)} %pad_maximum_fusion.2, bf16[4096,1280]{1,0:T(8,128)(2,1)} %all-gather.2.cloned.1.call-done.refs_0_.full_ref.refs_4_), kind=kOutput, calls=%fused_computation.6 | convolution fusion | flops 3222798336 | bytes 12320768 | tf_op jit(solution)/shard_map/dot_general | solution.py:414
  209.8 2.0 copy.19
  211.8 5.5 %all-to-all-start.1 = ((bf16[4,384,1024]{2,1,0:T(8,128)(2,1)}), bf16[4,384,1024]{2,1,0:T(8,128)(2,1)}, u32[]{:S(2)}, u32[]{:S(2)}) async-start(bf16[4,384,1024]{2,1,0:T(8,128)(2,1)} %bitcast.183), calls=%async_computation.1 | async-start | bytes 6291456 | tf_op jit(solution)/shard_map/all_to_all | solution.py:416
  218.3 37.9 %all-to-all-done.1 = bf16[4,384,1024]{2,1,0:T(8,128)(2,1)} async-done(((bf16[4,384,1024]{2,1,0:T(8,128)(2,1)}), bf16[4,384,1024]{2,1,0:T(8,128)(2,1)}, u32[]{:S(2)}, u32[]{:S(2)}) %all-to-all-start.1) | async-done | bytes 3145760 | tf_op jit(solution)/shard_map/all_to_all | solution.py:416
  256.2 2.8 convert_reduce_fusion
  264.6 24.2 %reduce-scatter.2.cloned.1.call-done = bf16[256,1152]{1,0:T(8,128)(2,1)} async-done(((bf16[4096,1152]{1,0:T(8,128)(2,1)}), bf16[256,1152]{1,0:T(8,128)(2,1)}) %reduce-scatter.2.cloned.1.call-update) | async-done | bytes 589840 | tf_op jit(solution)/shard_map/reduce_scatter | solution.py:410
  (136 shorter events, 37.9 us)
Async XLA Ops:
  7.2 158.4 %copy-start = (bf16[1,3,1,128,4096]{4,3,2,1,0:T(8,128)(2,1)S(1)}, bf16[1,3,1,128,4096]{4,3,2,1,0:T(8,128)(2,1)}, u32[]{:S(2)}) copy-start(bf16[1,3,1,128,4096]{4,3,2,1,0:T(8,128)(2,1)} %param.21) | copy-start | bytes 9437188
  7.2 9.5 %copy-start.34 = (s32[4,1]{0,1:T(1,128)S(1)}, s32[4,1]{0,1:T(1,128)}, u32[]{:S(2)}) copy-start(s32[4,1]{0,1:T(1,128)} %param.14) | copy-start | bytes 52
  7.2 12.7 %copy-start.35 = (s32[3,8]{1,0:T(4,128)S(1)}, s32[3,8]{1,0:T(4,128)}, u32[]{:S(2)}) copy-start(s32[3,8]{1,0:T(4,128)} %param.15) | copy-start | bytes 292
  7.2 110.0 %all-gather.2.cloned.1.call-start = ((), (), s32[]{:S(2)}) async-start(), calls=%async_computation.3 | async-start | bytes 11141120 | tf_op jit(solution)/shard_map/all_gather | solution.py:325
  11.5 13.6 %collective-permute-start = (bf16[256,1024]{1,0:T(8,128)(2,1)}, bf16[256,1024]{1,0:T(8,128)(2,1)}, u32[]{:S(2)}, u32[]{:S(2)}) collective-permute-start(bf16[256,1024]{1,0:T(8,128)(2,1)} %bitcast.186), channel_id=1, source_target_pairs={{0,4},{64,80},{4,8},{68,84},{8,12},{72,88},{12,0},{76,92},{16,20},... | collective-permute-start | bytes 1572872 | tf_op jit(solution)/shard_map/ppermute | solution.py:282
  13.2 12.0 %collective-permute-start.1 = (bf16[256,1024]{1,0:T(8,128)(2,1)}, bf16[256,1024]{1,0:T(8,128)(2,1)}, u32[]{:S(2)}, u32[]{:S(2)}) collective-permute-start(bf16[256,1024]{1,0:T(8,128)(2,1)} %bitcast.187), channel_id=1, source_target_pairs={{0,12},{64,112},{4,0},{68,116},{8,4},{72,120},{12,8},{76,124},{16,... | collective-permute-start | bytes 1572872 | tf_op jit(solution)/shard_map/ppermute | solution.py:282
  14.8 14.9 %collective-permute-start.2 = (bf16[256,1024]{1,0:T(8,128)(2,1)}, bf16[256,1024]{1,0:T(8,128)(2,1)}, u32[]{:S(2)}, u32[]{:S(2)}) collective-permute-start(bf16[256,1024]{1,0:T(8,128)(2,1)} %bitcast.188), channel_id=1, source_target_pairs={{0,8},{64,96},{4,12},{68,100},{8,0},{72,104},{12,4},{76,108},{16,2... | collective-permute-start | bytes 1572872 | tf_op jit(solution)/shard_map/ppermute | solution.py:282
  22.6 7.2 %copy-start.33 = (bf16[1,256,1024]{2,1,0:T(8,128)(2,1)S(1)}, bf16[1,256,1024]{2,1,0:T(8,128)(2,1)}, u32[]{:S(2)}) copy-start(bf16[1,256,1024]{2,1,0:T(8,128)(2,1)} %param.17) | copy-start | bytes 1572868
  23.9 12.8 %copy-start.12 = (bf16[2,128,1024]{2,1,0:T(8,128)(2,1)}, bf16[2,128,1024]{2,1,0:T(8,128)(2,1)S(1)}, u32[]{:S(2)}) copy-start(bf16[2,128,1024]{2,1,0:T(8,128)(2,1)S(1)} %bitcast_select_fusion.5) | copy-start | bytes 1572868
  25.1 11.2 %copy-start.19 = (bf16[128,1024]{1,0:T(8,128)(2,1)}, bf16[128,1024]{1,0:T(8,128)(2,1)S(1)}, u32[]{:S(2)}) copy-start(bf16[128,1024]{1,0:T(8,128)(2,1)S(1)} %fusion.73) | copy-start | bytes 786436
  29.8 6.6 %copy-start.8 = (bf16[1,2,2,128,1024]{4,3,2,1,0:T(8,128)(2,1)S(1)}, bf16[1,2,2,128,1024]{4,3,2,1,0:T(8,128)(2,1)}, u32[]{:S(2)}) copy-start(bf16[1,2,2,128,1024]{4,3,2,1,0:T(8,128)(2,1)} %param.11) | copy-start | bytes 3145732
  29.8 6.8 %copy-start.27 = (bf16[2,1,128,1024]{3,2,1,0:T(8,128)(2,1)S(1)}, bf16[2,1,128,1024]{3,2,1,0:T(8,128)(2,1)}, u32[]{:S(2)}) copy-start(bf16[2,1,128,1024]{3,2,1,0:T(8,128)(2,1)} %param.13) | copy-start | bytes 1572868
  32.8 47.5 %collective-permute-start.3 = (bf16[4,256,1024]{2,1,0:T(8,128)(2,1)}, bf16[4,256,1024]{2,1,0:T(8,128)(2,1)}, u32[]{:S(2)}, u32[]{:S(2)}) collective-permute-start(bf16[4,256,1024]{2,1,0:T(8,128)(2,1)} %pad_maximum_fusion.refs_1_.refs_5_), channel_id=1, source_target_pairs={{0,16},{64,68},{4,20},{68,72},{8,24},{72,76},{12,28},{76,64},{16,3... | collective-permute-start | bytes 6291464 | tf_op jit(solution)/shard_map/ppermute | solution.py:282
  34.6 50.5 %collective-permute-start.4 = (bf16[4,256,1024]{2,1,0:T(8,128)(2,1)}, bf16[4,256,1024]{2,1,0:T(8,128)(2,1)}, u32[]{:S(2)}, u32[]{:S(2)}) collective-permute-start(bf16[4,256,1024]{2,1,0:T(8,128)(2,1)} %pad_maximum_fusion.refs_1_.refs_5_), channel_id=1, source_target_pairs={{0,48},{64,76},{4,52},{68,64},{8,56},{72,68},{12,60},{76,72},{16,0... | collective-permute-start | bytes 6291464 | tf_op jit(solution)/shard_map/ppermute | solution.py:282
  39.7 48.5 %all-to-all-start = ((bf16[4,384,1024]{2,1,0:T(8,128)(2,1)}), bf16[4,384,1024]{2,1,0:T(8,128)(2,1)}, u32[]{:S(2)}, u32[]{:S(2)}) async-start(bf16[4,384,1024]{2,1,0:T(8,128)(2,1)} %broadcast_in_dim.196), calls=%async_computation | async-start | bytes 6291456 | tf_op jit(solution)/shard_map/all_to_all | solution.py:360
  47.2 41.0 %copy-start.6 = (f32[1,4096]{1,0:T(1,128)S(1)}, f32[1,4096]{1,0:T(1,128)}, u32[]{:S(2)}) copy-start(f32[1,4096]{1,0:T(1,128)} %gain_ref.3) | copy-start | bytes 49156
  47.2 241.5 %reduce-scatter.2.cloned.1.call-start = ((), (), s32[]{:S(2)}) async-start(), calls=%async_computation.4 | async-start | bytes 10027008 | tf_op jit(solution)/shard_map/reduce_scatter | solution.py:410
  82.6 34.6 %collective-permute-start.5 = (bf16[2,256,1024]{2,1,0:T(8,128)(2,1)}, bf16[2,256,1024]{2,1,0:T(8,128)(2,1)}, u32[]{:S(2)}, u32[]{:S(2)}) collective-permute-start(bf16[2,256,1024]{2,1,0:T(8,128)(2,1)} %slice.261), channel_id=1, source_target_pairs={{0,16},{64,68},{4,20},{68,72},{8,24},{72,76},{12,28},{76,64},{16,3... | collective-permute-start | bytes 3145736 | tf_op jit(solution)/shard_map/ppermute | solution.py:282
  87.5 29.7 %collective-permute-start.6 = (bf16[2,256,1024]{2,1,0:T(8,128)(2,1)}, bf16[2,256,1024]{2,1,0:T(8,128)(2,1)}, u32[]{:S(2)}, u32[]{:S(2)}) collective-permute-start(bf16[2,256,1024]{2,1,0:T(8,128)(2,1)} %slice.262), channel_id=1, source_target_pairs={{0,48},{64,76},{4,52},{68,64},{8,56},{72,68},{12,60},{76,72},{16,0... | collective-permute-start | bytes 3145736 | tf_op jit(solution)/shard_map/ppermute | solution.py:282
  133.5 21.7 %copy-start.9 = (bf16[1,2,2,128,1024]{4,3,2,1,0:T(8,128)(2,1)S(1)}, bf16[1,2,2,128,1024]{4,3,2,1,0:T(8,128)(2,1)}, u32[]{:S(2)}) copy-start(bf16[1,2,2,128,1024]{4,3,2,1,0:T(8,128)(2,1)} %param.11) | copy-start | bytes 3145732
  133.5 13.5 %collective-permute-start.7 = (bf16[256,1024]{1,0:T(8,128)(2,1)}, bf16[256,1024]{1,0:T(8,128)(2,1)S(1)}, u32[]{:S(2)}, u32[]{:S(2)}) collective-permute-start(bf16[256,1024]{1,0:T(8,128)(2,1)} %get-tuple-element.21), channel_id=1, source_target_pairs={{0,2},{1,3},{2,0},{3,1},{4,6},{5,7},{6,4},{7,5},{8,10},{9,11},{10,... | collective-permute-start | bytes 1572872 | tf_op jit(solution)/shard_map/ppermute | solution.py:286
  139.6 13.0 %collective-permute-start.8 = (bf16[256,1024]{1,0:T(8,128)(2,1)}, bf16[256,1024]{1,0:T(8,128)(2,1)S(1)}, u32[]{:S(2)}, u32[]{:S(2)}) collective-permute-start(bf16[256,1024]{1,0:T(8,128)(2,1)} %get-tuple-element.22), channel_id=1, source_target_pairs={{0,1},{1,2},{2,3},{3,0},{4,5},{5,6},{6,7},{7,4},{8,9},{9,10},{10,1... | collective-permute-start | bytes 1572872 | tf_op jit(solution)/shard_map/ppermute | solution.py:286
  142.5 11.3 %collective-permute-start.9 = (bf16[256,1024]{1,0:T(8,128)(2,1)}, bf16[256,1024]{1,0:T(8,128)(2,1)S(1)}, u32[]{:S(2)}, u32[]{:S(2)}) collective-permute-start(bf16[256,1024]{1,0:T(8,128)(2,1)} %get-tuple-element.23), channel_id=1, source_target_pairs={{0,3},{1,0},{2,1},{3,2},{4,7},{5,4},{6,5},{7,6},{8,11},{9,8},{10,9... | collective-permute-start | bytes 1572872 | tf_op jit(solution)/shard_map/ppermute | solution.py:286
  157.2 16.3 %collective-permute-start.10 = (bf16[256,1024]{1,0:T(8,128)(2,1)S(1)}, bf16[256,1024]{1,0:T(8,128)(2,1)}, u32[]{:S(2)}, u32[]{:S(2)}) collective-permute-start(bf16[256,1024]{1,0:T(8,128)(2,1)S(1)} %pad_maximum_fusion.4), channel_id=1, source_target_pairs={{0,64},{1,65},{2,66},{3,67},{4,68},{5,69},{6,70},{7,71},{8,72},{9,... | collective-permute-start | bytes 1572872 | tf_op jit(solution)/shard_map/ppermute | solution.py:286
  159.3 14.2 %collective-permute-start.11 = (bf16[256,1024]{1,0:T(8,128)(2,1)S(1)}, bf16[256,1024]{1,0:T(8,128)(2,1)}, u32[]{:S(2)}, u32[]{:S(2)}) collective-permute-start(bf16[256,1024]{1,0:T(8,128)(2,1)S(1)} %pad_maximum_fusion.4), channel_id=1, source_target_pairs={{0,65},{1,66},{2,67},{3,64},{4,69},{5,70},{6,71},{7,68},{8,73},{9,... | collective-permute-start | bytes 1572872 | tf_op jit(solution)/shard_map/ppermute | solution.py:286
  161.4 12.1 %collective-permute-start.12 = (bf16[256,1024]{1,0:T(8,128)(2,1)S(1)}, bf16[256,1024]{1,0:T(8,128)(2,1)}, u32[]{:S(2)}, u32[]{:S(2)}) collective-permute-start(bf16[256,1024]{1,0:T(8,128)(2,1)S(1)} %pad_maximum_fusion.4), channel_id=1, source_target_pairs={{0,66},{1,67},{2,64},{3,65},{4,70},{5,71},{6,68},{7,69},{8,74},{9,... | collective-permute-start | bytes 1572872 | tf_op jit(solution)/shard_map/ppermute | solution.py:286
  163.5 11.8 %collective-permute-start.13 = (bf16[256,1024]{1,0:T(8,128)(2,1)S(1)}, bf16[256,1024]{1,0:T(8,128)(2,1)}, u32[]{:S(2)}, u32[]{:S(2)}) collective-permute-start(bf16[256,1024]{1,0:T(8,128)(2,1)S(1)} %pad_maximum_fusion.4), channel_id=1, source_target_pairs={{0,67},{1,64},{2,65},{3,66},{4,71},{5,68},{6,69},{7,70},{8,75},{9,... | collective-permute-start | bytes 1572872 | tf_op jit(solution)/shard_map/ppermute | solution.py:286
  173.5 14.0 %copy-start.3 = (bf16[256,4096]{1,0:T(8,128)(2,1)S(1)}, bf16[256,4096]{1,0:T(8,128)(2,1)}, u32[]{:S(2)}) copy-start(bf16[256,4096]{1,0:T(8,128)(2,1)} %copy-done.2) | copy-start | bytes 6291460
  211.8 44.4 %all-to-all-start.1 = ((bf16[4,384,1024]{2,1,0:T(8,128)(2,1)}), bf16[4,384,1024]{2,1,0:T(8,128)(2,1)}, u32[]{:S(2)}, u32[]{:S(2)}) async-start(bf16[4,384,1024]{2,1,0:T(8,128)(2,1)} %bitcast.183), calls=%async_computation.1 | async-start | bytes 6291456 | tf_op jit(solution)/shard_map/all_to_all | solution.py:416
  218.3 40.7 %copy-start.24 = (bf16[1,1,1,128,1024]{4,3,2,1,0:T(8,128)(2,1)S(1)}, bf16[1,1,1,128,1024]{4,3,2,1,0:T(8,128)(2,1)}, u32[]{:S(2)}) copy-start(bf16[1,1,1,128,1024]{4,3,2,1,0:T(8,128)(2,1)} %copy-done.23) | copy-start | bytes 786436
  218.3 40.7 %copy-start.26 = (bf16[128,1024]{1,0:T(8,128)(2,1)S(1)}, bf16[128,1024]{1,0:T(8,128)(2,1)}, u32[]{:S(2)}) copy-start(bf16[128,1024]{1,0:T(8,128)(2,1)} %copy-done.25) | copy-start | bytes 786436
  263.1 29.0 %copy-start.1 = (bf16[1,3,1,128,4096]{4,3,2,1,0:T(8,128)(2,1)S(1)}, bf16[1,3,1,128,4096]{4,3,2,1,0:T(8,128)(2,1)}, u32[]{:S(2)}) copy-start(bf16[1,3,1,128,4096]{4,3,2,1,0:T(8,128)(2,1)} %param.21) | copy-start | bytes 9437188
  (22 other events, 61.9 us)
Sparse Core Ops, SparseCore 0:
  11.6 104.0 all-gather.1
  199.2 89.4 reduce-scatter.1

commit v2 on v1

--- a/solution.py
+++ b/solution.py
@@ -272,6 +272,55 @@
     )(flags, mixed, full)
 
 
+WIDE = (GROUP + 1) * HD
+
+
+def three(flags, a_ref, b_ref, columns):
+    middle = jnp.where(flags[0] == 1, a_ref[SEQ:, columns], b_ref[SEQ:, columns])
+    return jnp.concatenate([a_ref[:SEQ, columns], middle, b_ref[:SEQ, columns]], axis=0)
+
+
+PLACES = (((2, 0), (1, 1)), ((2, 1), (3, 0)), ((1, 0),), ((3, 1),), ((0, 0), (0, 1)))
+
+
+def terms_kernel(flags, normed_a, normed_b, d_a, d_b, *refs):
+    outs, (held, sems) = refs[:5], refs[5:]
+    d_rows = three(flags, d_a, d_b, slice(None)).T
+    copies = []
+    places = [(out, k, place) for out, parts in zip(outs, PLACES) for k, place in enumerate(parts)]
+    for i, (out, k, (outer, pair)) in enumerate(places):
+        features = []
+        for inner in (2 * pair, 2 * pair + 1):
+            dy = jnp.where(flags[0] == 1, outer, inner)
+            dx = jnp.where(flags[0] == 1, inner, outer)
+            row = lax.rem(flags[5] + dy, 4) * 4 + lax.rem(flags[4] + dx, 4)
+            columns = pl.ds(pl.multiple_of(row * 256, 256), 256)
+            features.append(three(flags, normed_a, normed_b, columns))
+        held[i] = jnp.dot(
+            d_rows, jnp.concatenate(features, axis=1), preferred_element_type=f32
+        ).astype(bf16)
+        target = out.at[:, pl.ds(512 * k, 512)]
+        copies.append(pltpu.make_async_copy(held.at[i], target, sems.at[i]))
+        copies[-1].start()
+    for copy in copies:
+        copy.wait()
+
+
+def terms(operands):
+    return pl.pallas_call(
+        terms_kernel,
+        in_specs=[SMEM] + [VMEM] * 4,
+        out_specs=[ANY] * 5,
+        out_shape=[jax.ShapeDtypeStruct((WIDE, 512 * len(parts)), bf16) for parts in PLACES],
+        scratch_shapes=[pltpu.VMEM((8, WIDE, 512), bf16), pltpu.SemaphoreType.DMA((8,))],
+        compiler_params=pltpu.CompilerParams(vmem_limit_bytes=32 * 1024 * 1024),
+        cost_estimate=pl.CostEstimate(
+            flops=2 * 3 * SEQ * 4096 * WIDE, bytes_accessed=14 * 2**20, transcendentals=0
+        ),
+        name="terms",
+    )(*operands)
+
+
 def along(shard, second, by):
     pairs = []
     for y in range(4):
@@ -293,6 +342,35 @@
     own = jnp.stack([shard, before, after, far])
     before, after = along(own, True, 1), along(own, True, -1)
     return [own, before, after, along(before[:2], True, 1), along(after[2:], True, -1)]
+
+
+def plus(*shards):
+    return sum(shard.astype(f32) for shard in shards).astype(bf16)
+
+
+def summed_over_plane(operands):
+    ahead, back, next_low, last_high, own = terms(operands)
+    from_before, from_after = lax.optimization_barrier(
+        (along(ahead, True, 1), along(back, True, -1))
+    )
+    sum_before, sum_after = lax.optimization_barrier(
+        (
+            along(plus(next_low, from_before[:, :512]), True, 1),
+            along(plus(last_high, from_after[:, :512]), True, -1),
+        )
+    )
+    low = (own[:, :512], sum_before, from_after[:, 512:])
+    high = (own[:, 512:], from_before[:, 512:], sum_after)
+    blocks = []
+    for parts in (low, high):
+        for columns in (slice(0, 256), slice(256, 512)):
+            blocks.append(plus(*(part[:, columns] for part in parts)))
+    got = [
+        along(blocks[2], False, 2),
+        along(blocks[1], False, 1),
+        along(blocks[3], False, -1),
+    ]
+    return plus(blocks[0], *got), own
 
 
 def pick(state, slot):
@@ -401,20 +479,13 @@
     )
     d_b = attend_back(qkv_b, d_mixed_b)
 
-    def three(a, b):
-        return jnp.concatenate([a[:SEQ], jnp.where(first, a[SEQ:], b[SEQ:]), b[:SEQ]], 0)
-
-    term = lax.dot_general(
-        three(normed_a, normed_b), three(d_a, d_b), TN, preferred_element_type=f32
-    ).astype(bf16)
-    grad = lax.psum_scatter(term, ("y", "x"), scatter_dimension=0, tiled=True)
+    grad, own_terms = summed_over_plane([flags, normed_a, normed_b, d_a, d_b])
+    grad = grad.T
 
     mixed_f = jnp.concatenate([jnp.where(first, mixed_b[:SEQ], mixed_a[:SEQ]), mixed_b], 0)
-    mixed_f, _ = lax.optimization_barrier((mixed_f, term))
+    mixed_f, _ = lax.optimization_barrier((mixed_f, own_terms))
     partial = lax.dot_general(mixed_f, full_o, NT, preferred_element_type=f32).astype(bf16)
-    parts = partial.reshape(3 * SEQ, 4, -1).swapaxes(0, 1)
-    parts = lax.all_to_all(parts, "tensor", split_axis=0, concat_axis=0, tiled=True)
-    summed = jnp.sum(parts.astype(f32), axis=0)
+    summed = lax.psum_scatter(partial, "tensor", scatter_dimension=1, tiled=True).astype(f32)
     _, renewed = deliver(out_2, slot[2], x2, summed[:SEQ])
     new_out_first = put(out_2, slot[2], renewed)
     _, renewed = deliver(state_out, slot[0], x0, summed[:SEQ])

time: 300 us -> 295 us (0.983)
  waiting for transfers between devices: 132 us -> 114 us
  Pallas kernels: 36.7 us -> 44.1 us
  matrix products: 23.1 us -> 16.3 us
  starting transfers between devices: 46.6 us -> 50.5 us
  other arithmetic: 23.6 us -> 27.4 us
  local copies, waits for them, and re-layouts: 18.7 us -> 21.8 us
    ppermute x7 -> x14, waiting for transfers between devices: 60.9 us -> 105 us  [along(): return lax.ppermute(shard, ('section', 'y', 'x'), pairs)]
    all_to_all x1 -> x0, waiting for transfers between devices: 37.9 us -> none  [on_device(): lax.all_to_all(parts, 'tensor', split_axis=0, concat_axis=0, tiled=True)]
    reduce_scatter x1, waiting for transfers between devices: 24.2 us -> 0.01 us  [on_device(): lax.psum_scatter(partial, 'tensor', scatter_dimension=1, tiled=True)]
    ppermute x7 -> x14, starting transfers between devices: 11.9 us -> 23.7 us  [along(): return lax.ppermute(shard, ('section', 'y', 'x'), pairs)]
    unnamed x73 -> x117, local copies, waits for them, and re-layouts: 5.87 us -> 14.2 us
    dot_general x1 -> x0, matrix products: 7.76 us -> none  [on_device(): lax.dot_general(three(normed_a, normed_b), three(d_a, d_b), TN, preferred...]
    pallas_call x0 -> x1, Pallas kernels: none -> 7.37 us  [terms(): pl.pallas_call(terms_kernel, in_specs=[SMEM] + [VMEM] * 4, out_specs=[ANY...]
    convert_element_type x0 -> x4, other arithmetic: none -> 6.86 us  [the longest x3 5.56 us: plus(): return sum((shard.astype(f32) for shard in shards)).astype(bf16)]
  transfers between devices with their start and end apart: 18 -> 24, of which waited for: 9 -> 13; matrix products, arithmetic and copies ran while one was open for 14% -> 15% of each run, Pallas kernels for 2% -> 2%
where the time goes in v2:
time: 295 us; the launch traced here: 293 us
  waiting for transfers between devices  114 us (39%)
  starting transfers between devices  50.5 us (17%)
  Pallas kernels  44.1 us (15%)
  other arithmetic  27.4 us (9%)
  local copies, waits for them, and re-layouts  21.8 us (7%)
  between operations  18.9 us (6%)
  matrix products  16.3 us (6%)
    ppermute x14, waiting for transfers between devices, along(): return lax.ppermute(shard, ('section', 'y', 'x'), pairs)  105 us
    ppermute x14, starting transfers between devices, along(): return lax.ppermute(shard, ('section', 'y', 'x'), pairs)  23.7 us
    pallas_call x2, Pallas kernels, project_call(): pl.pallas_call(kernel, in_specs=[SMEM] + [VMEM] * (len(operands) - 1) + [...  22.2 us
    ppermute x7, starting transfers between devices, from_first(): lax.ppermute(shard, ('section', 'tensor'), [(i, 4 * to_section + (i + by)...  19.2 us
    unnamed x117, local copies, waits for them, and re-layouts  14.2 us
    dot_general x1, matrix products, on_device(): lax.dot_general(mixed_f, full_o, NT, preferred_element_type=f32)  10.4 us
    ppermute x7, waiting for transfers between devices, from_first(): lax.ppermute(shard, ('section', 'tensor'), [(i, 4 * to_section + (i + by)...  8.44 us
    all_to_all x1, starting transfers between devices, on_device(): lax.all_to_all(jnp.broadcast_to(known[None], (4,) + known.shape), 'tensor...  7.55 us
  transfers between devices with their start and end apart: 24, of which 13 were waited for; matrix products, arithmetic and copies ran while one was open for 15% of the time, Pallas kernels for 2%

profile of v2, /device:TPU:0, one launch (start us, length us, event | category | flops | bytes accessed | tf_op | source)
XLA Modules:
  0.0 293.0 jit_solution(1780934185564696403)
XLA Ops:
  7.2 2.2 copy.14
  9.4 2.1 pad_maximum_fusion.3
  25.4 4.4 %collective-permute-done.2 = bf16[256,1024]{1,0:T(8,128)(2,1)} collective-permute-done((bf16[256,1024]{1,0:T(8,128)(2,1)}, bf16[256,1024]{1,0:T(8,128)(2,1)}, u32[]{:S(2)}, u32[]{:S(2)}) %collective-permute-start.2) | collective-permute-done | bytes 524320 | tf_op jit(solution)/shard_map/ppermute | solution.py:331
  29.8 3.1 %pad_maximum_fusion.refs_1_.refs_5_ = bf16[4,256,1024]{2,1,0:T(8,128)(2,1)} fusion(bf16[1,256,1024]{2,1,0:T(8,128)(2,1)} %bitcast.35, bf16[1,256,1024]{2,1,0:T(8,128)(2,1)} %bitcast.34, bf16[1,256,1024]{2,1,0:T(8,128)(2,1)} %bitcast.33, bf16[1,256,1024]{2,1,0:T(8,128)(2,1)S(1)} %copy-done.43), kind=kLoop, calls=%fused_computation.7 | loop fusion | flops 3145728 | bytes 4194304 | tf_op jit(solution)/shard_map/stack | solution.py:342
  37.7 2.0 broadcast_in_dim.196
  39.7 7.6 %all-to-all-start = ((bf16[4,384,1024]{2,1,0:T(8,128)(2,1)}), bf16[4,384,1024]{2,1,0:T(8,128)(2,1)}, u32[]{:S(2)}, u32[]{:S(2)}) async-start(bf16[4,384,1024]{2,1,0:T(8,128)(2,1)} %broadcast_in_dim.196), calls=%async_computation | async-start | bytes 6291456 | tf_op jit(solution)/shard_map/all_to_all | solution.py:438
  47.3 33.0 %collective-permute-done.3.refs_2_.refs_6_ = bf16[4,256,1024]{2,1,0:T(8,128)(2,1)} collective-permute-done((bf16[4,256,1024]{2,1,0:T(8,128)(2,1)}, bf16[4,256,1024]{2,1,0:T(8,128)(2,1)}, u32[]{:S(2)}, u32[]{:S(2)}) %collective-permute-start.3) | collective-permute-done | bytes 2097184 | tf_op jit(solution)/shard_map/ppermute | solution.py:331
  80.3 2.3 slice.297
  82.6 2.5 collective-permute-start.5
  85.1 2.4 slice.298
  88.3 4.5 %prepare.1.normed_ref.normed_a = bf16[256,4096]{1,0:T(8,128)(2,1)S(1)} custom-call(s32[7]{0:T(128)S(1)} %stack.52.flags, f32[1,4096]{1,0:T(1,128)S(1)} %copy-done.10, bf16[4,384,1024]{2,1,0:T(8,128)(2,1)} %all-to-all-done.known_ref), custom_call_target="tpu_custom_call" | custom-call | flops 8388608 | bytes 5242880 | tf_op jit(solution)/shard_map/prepare/pallas_call | solution.py:155
  94.1 23.1 %collective-permute-done.5.refs_4_.refs_8_ = bf16[2,256,1024]{2,1,0:T(8,128)(2,1)} collective-permute-done((bf16[2,256,1024]{2,1,0:T(8,128)(2,1)}, bf16[2,256,1024]{2,1,0:T(8,128)(2,1)}, u32[]{:S(2)}, u32[]{:S(2)}) %collective-permute-start.5) | collective-permute-done | bytes 1048608 | tf_op jit(solution)/shard_map/ppermute | solution.py:331
  117.2 9.8 %project_a.1 = (bf16[256,1280]{1,0:T(8,128)(2,1)}, bf16[256,1024]{1,0:T(8,128)(2,1)}) custom-call(s32[7]{0:T(128)} %copy-done.11, bf16[256,4096]{1,0:T(8,128)(2,1)} %copy-done.2, bf16[4096,1280]{1,0:T(8,128)(2,1)} %all-gather.2.cloned.1.call-done.refs_0_.full_ref.refs_4_, bf16[4,256,1024]{2,1,0:T(8,128)(2,1)} %pad_maximum_fusion.refs_1_.refs_5_, ...), custom_call_target="tpu_custom_call" | custom-call | flops 2684354560 | bytes 18874368 | tf_op jit(solution)/shard_map/project_a/pallas_call | solution.py:225
  127.0 6.5 %spread.1 = (bf16[256,1024]{1,0:T(8,128)(2,1)}, bf16[256,1024]{1,0:T(8,128)(2,1)}, bf16[256,1024]{1,0:T(8,128)(2,1)}, bf16[256,1024]{1,0:T(8,128)(2,1)}) custom-call(s32[7]{0:T(128)} %copy-done.11, bf16[256,1024]{1,0:T(8,128)(2,1)} %get-tuple-element.28.mixed_ref, bf16[4096,1280]{1,0:T(8,128)(2,1)} %all-gather.2.cloned.1.call-done.refs_0_.full_ref.refs_4_), custom_call_target="tpu_custom_call" | custom-call | flops 2147483648 | bytes 12582912 | tf_op jit(solution)/shard_map/spread/pallas_call | solution.py:261
  133.5 5.9 %collective-permute-start.7 = (bf16[256,1024]{1,0:T(8,128)(2,1)}, bf16[256,1024]{1,0:T(8,128)(2,1)S(1)}, u32[]{:S(2)}, u32[]{:S(2)}) collective-permute-start(bf16[256,1024]{1,0:T(8,128)(2,1)} %get-tuple-element.30), channel_id=1, source_target_pairs={{0,2},{1,3},{2,0},{3,1},{4,6},{5,7},{6,4},{7,5},{8,10},{9,11},{10,... | collective-permute-start | bytes 1572872 | tf_op jit(solution)/shard_map/ppermute | solution.py:335
  139.4 2.9 collective-permute-start.8
  142.4 4.3 %collective-permute-start.9 = (bf16[256,1024]{1,0:T(8,128)(2,1)}, bf16[256,1024]{1,0:T(8,128)(2,1)S(1)}, u32[]{:S(2)}, u32[]{:S(2)}) collective-permute-start(bf16[256,1024]{1,0:T(8,128)(2,1)} %get-tuple-element.32), channel_id=1, source_target_pairs={{0,3},{1,0},{2,1},{3,2},{4,7},{5,4},{6,5},{7,6},{8,11},{9,8},{10,9... | collective-permute-start | bytes 1572872 | tf_op jit(solution)/shard_map/ppermute | solution.py:335
  146.8 5.6 %collective-permute-done.8 = bf16[256,1024]{1,0:T(8,128)(2,1)S(1)} collective-permute-done((bf16[256,1024]{1,0:T(8,128)(2,1)}, bf16[256,1024]{1,0:T(8,128)(2,1)S(1)}, u32[]{:S(2)}, u32[]{:S(2)}) %collective-permute-start.8) | collective-permute-done | bytes 524320 | tf_op jit(solution)/shard_map/ppermute | solution.py:335
  161.5 2.1 collective-permute-start.13
  163.6 6.0 %fusion.10 = bf16[384,1024]{1,0:T(8,128)(2,1)S(1)} fusion(bf16[384,4096]{1,0:T(8,128)(2,1)S(1)} %bitcast.177, bf16[4096,1280]{1,0:T(8,128)(2,1)} %all-gather.2.cloned.1.call-done.refs_0_.full_ref.refs_4_), kind=kOutput, calls=%fused_computation.9 | convolution fusion | flops 3221618688 | bytes 12320768 | tf_op jit(solution)/shard_map/dot_general | solution.py:475
  174.0 12.4 %project_b.1 = (bf16[256,4096]{1,0:T(8,128)(2,1)}, bf16[256,1280]{1,0:T(8,128)(2,1)}, bf16[256,1024]{1,0:T(8,128)(2,1)}) custom-call(s32[7]{0:T(128)} %copy-done.11, f32[1,4096]{1,0:T(1,128)} %gain_ref.3, bf16[4,384,1024]{2,1,0:T(8,128)(2,1)} %all-to-all-done.known_ref, bf16[256,1024]{1,0:T(8,128)(2,1)} %copy-done.33, bf16[256,1024]{1,0:T(8,128)(2,1)} %copy-done.41, ...), custom_call_target="tpu_custom_call" | custom-call | flops 2684354560 | bytes 18874368 | tf_op jit(solution)/shard_map/project_b/pallas_call | solution.py:225
  190.9 7.4 %terms.1 = (bf16[1152,1024]{1,0:T(8,128)(2,1)}, bf16[1152,1024]{1,0:T(8,128)(2,1)}, bf16[1152,512]{1,0:T(8,128)(2,1)S(1)}, bf16[1152,512]{1,0:T(8,128)(2,1)S(1)}, bf16[1152,1024]{1,0:T(8,128)(2,1)S(1)}) custom-call(s32[7]{0:T(128)S(1)} %copy-done.12, bf16[256,4096]{1,0:T(8,128)(2,1)S(1)} %copy-done.3, bf16[256,4096]{1,0:T(8,128)(2,1)S(1)} %copy-done.13, ...), custom_call_target="tpu_custom_call" | custom-call | flops 3623878656 | bytes 14680064 | tf_op jit(solution)/shard_map/terms/pallas_call | solution.py:310
  201.9 2.1 collective-permute-start.15
  204.1 10.4 %fusion.4 = bf16[384,4096]{1,0:T(8,128)(2,1)} fusion(bf16[384,1024]{1,0:T(8,128)(2,1)S(1)} %pad_maximum_fusion.2, bf16[4096,1280]{1,0:T(8,128)(2,1)} %all-gather.2.cloned.1.call-done.refs_0_.full_ref.refs_4_), kind=kOutput, calls=%fused_computation.4 | convolution fusion | flops 3222798336 | bytes 12320768 | tf_op jit(solution)/shard_map/dot_general | solution.py:487
  214.4 16.7 %collective-permute-done.14 = bf16[1152,1024]{1,0:T(8,128)(2,1)} collective-permute-done((bf16[1152,1024]{1,0:T(8,128)(2,1)}, bf16[1152,1024]{1,0:T(8,128)(2,1)}, u32[]{:S(2)}, u32[]{:S(2)}) %collective-permute-start.14) | collective-permute-done | bytes 2359328 | tf_op jit(solution)/shard_map/ppermute | solution.py:331
  232.7 3.3 %collective-permute-start.17 = (bf16[1152,512]{1,0:T(8,128)(2,1)S(1)}, bf16[1152,512]{1,0:T(8,128)(2,1)S(1)}, u32[]{:S(2)}, u32[]{:S(2)}) collective-permute-start(bf16[1152,512]{1,0:T(8,128)(2,1)S(1)} %add_convert_fusion), channel_id=1, source_target_pairs={{0,48},{64,76},{4,52},{68,64},{8,56},{72,68},{12,60},{76,72},{16,0... | collective-permute-start | bytes 3538952 | tf_op jit(solution)/shard_map/ppermute | solution.py:331
  238.0 11.8 %collective-permute-done.17 = bf16[1152,512]{1,0:T(8,128)(2,1)S(1)} collective-permute-done((bf16[1152,512]{1,0:T(8,128)(2,1)S(1)}, bf16[1152,512]{1,0:T(8,128)(2,1)S(1)}, u32[]{:S(2)}, u32[]{:S(2)}) %collective-permute-start.17) | collective-permute-done | bytes 1179680 | tf_op jit(solution)/shard_map/ppermute | solution.py:331
  249.8 5.6 %collective-permute-done.16 = bf16[1152,512]{1,0:T(8,128)(2,1)S(1)} collective-permute-done((bf16[1152,512]{1,0:T(8,128)(2,1)S(1)}, bf16[1152,512]{1,0:T(8,128)(2,1)S(1)}, u32[]{:S(2)}, u32[]{:S(2)}) %collective-permute-start.16) | collective-permute-done | bytes 1179680 | tf_op jit(solution)/shard_map/ppermute | solution.py:331
  255.4 2.2 add_convert_fusion.5
  260.8 2.0 collective-permute-start.20
  264.6 4.6 %collective-permute-done.18 = bf16[1152,256]{1,0:T(8,128)(2,1)S(1)} collective-permute-done((bf16[1152,256]{1,0:T(8,128)(2,1)S(1)}, bf16[1152,256]{1,0:T(8,128)(2,1)S(1)}, u32[]{:S(2)}, u32[]{:S(2)}) %collective-permute-start.18) | collective-permute-done | bytes 589856 | tf_op jit(solution)/shard_map/ppermute | solution.py:331
  269.2 6.2 %collective-permute-done.19 = bf16[1152,256]{1,0:T(8,128)(2,1)S(1)} collective-permute-done((bf16[1152,256]{1,0:T(8,128)(2,1)S(1)}, bf16[1152,256]{1,0:T(8,128)(2,1)S(1)}, u32[]{:S(2)}, u32[]{:S(2)}) %collective-permute-start.19) | collective-permute-done | bytes 589856 | tf_op jit(solution)/shard_map/ppermute | solution.py:331
  (194 shorter events, 57.4 us)
Async XLA Ops:
  7.2 156.4 %copy-start = (bf16[1,3,1,128,4096]{4,3,2,1,0:T(8,128)(2,1)S(1)}, bf16[1,3,1,128,4096]{4,3,2,1,0:T(8,128)(2,1)}, u32[]{:S(2)}) copy-start(bf16[1,3,1,128,4096]{4,3,2,1,0:T(8,128)(2,1)} %param.21) | copy-start | bytes 9437188
  7.2 110.0 %all-gather.2.cloned.1.call-start = ((), (), s32[]{:S(2)}) async-start(), calls=%async_computation.2 | async-start | bytes 11141120 | tf_op jit(solution)/shard_map/all_gather | solution.py:403
  11.5 13.9 %collective-permute-start = (bf16[256,1024]{1,0:T(8,128)(2,1)}, bf16[256,1024]{1,0:T(8,128)(2,1)}, u32[]{:S(2)}, u32[]{:S(2)}) collective-permute-start(bf16[256,1024]{1,0:T(8,128)(2,1)} %bitcast.179), channel_id=1, source_target_pairs={{0,4},{64,80},{4,8},{68,84},{8,12},{72,88},{12,0},{76,92},{16,20},... | collective-permute-start | bytes 1572872 | tf_op jit(solution)/shard_map/ppermute | solution.py:331
  13.2 12.2 %collective-permute-start.1 = (bf16[256,1024]{1,0:T(8,128)(2,1)}, bf16[256,1024]{1,0:T(8,128)(2,1)}, u32[]{:S(2)}, u32[]{:S(2)}) collective-permute-start(bf16[256,1024]{1,0:T(8,128)(2,1)} %bitcast.180), channel_id=1, source_target_pairs={{0,12},{64,112},{4,0},{68,116},{8,4},{72,120},{12,8},{76,124},{16,... | collective-permute-start | bytes 1572872 | tf_op jit(solution)/shard_map/ppermute | solution.py:331
  14.8 14.9 %collective-permute-start.2 = (bf16[256,1024]{1,0:T(8,128)(2,1)}, bf16[256,1024]{1,0:T(8,128)(2,1)}, u32[]{:S(2)}, u32[]{:S(2)}) collective-permute-start(bf16[256,1024]{1,0:T(8,128)(2,1)} %bitcast.181), channel_id=1, source_target_pairs={{0,8},{64,96},{4,12},{68,100},{8,0},{72,104},{12,4},{76,108},{16,2... | collective-permute-start | bytes 1572872 | tf_op jit(solution)/shard_map/ppermute | solution.py:331
  32.9 47.5 %collective-permute-start.3 = (bf16[4,256,1024]{2,1,0:T(8,128)(2,1)}, bf16[4,256,1024]{2,1,0:T(8,128)(2,1)}, u32[]{:S(2)}, u32[]{:S(2)}) collective-permute-start(bf16[4,256,1024]{2,1,0:T(8,128)(2,1)} %pad_maximum_fusion.refs_1_.refs_5_), channel_id=1, source_target_pairs={{0,16},{64,68},{4,20},{68,72},{8,24},{72,76},{12,28},{76,64},{16,3... | collective-permute-start | bytes 6291464 | tf_op jit(solution)/shard_map/ppermute | solution.py:331
  34.6 50.5 %collective-permute-start.4 = (bf16[4,256,1024]{2,1,0:T(8,128)(2,1)}, bf16[4,256,1024]{2,1,0:T(8,128)(2,1)}, u32[]{:S(2)}, u32[]{:S(2)}) collective-permute-start(bf16[4,256,1024]{2,1,0:T(8,128)(2,1)} %pad_maximum_fusion.refs_1_.refs_5_), channel_id=1, source_target_pairs={{0,48},{64,76},{4,52},{68,64},{8,56},{72,68},{12,60},{76,72},{16,0... | collective-permute-start | bytes 6291464 | tf_op jit(solution)/shard_map/ppermute | solution.py:331
  39.7 48.6 %all-to-all-start = ((bf16[4,384,1024]{2,1,0:T(8,128)(2,1)}), bf16[4,384,1024]{2,1,0:T(8,128)(2,1)}, u32[]{:S(2)}, u32[]{:S(2)}) async-start(bf16[4,384,1024]{2,1,0:T(8,128)(2,1)} %broadcast_in_dim.196), calls=%async_computation | async-start | bytes 6291456 | tf_op jit(solution)/shard_map/all_to_all | solution.py:438
  47.3 231.5 %reduce-scatter.2.cloned.1.call-start = ((), (), s32[]{:S(2)}) async-start(), calls=%async_computation.3 | async-start | bytes 3932160 | tf_op jit(solution)/shard_map/reduce_scatter | solution.py:488
  82.6 34.6 %collective-permute-start.5 = (bf16[2,256,1024]{2,1,0:T(8,128)(2,1)}, bf16[2,256,1024]{2,1,0:T(8,128)(2,1)}, u32[]{:S(2)}, u32[]{:S(2)}) collective-permute-start(bf16[2,256,1024]{2,1,0:T(8,128)(2,1)} %slice.297), channel_id=1, source_target_pairs={{0,16},{64,68},{4,20},{68,72},{8,24},{72,76},{12,28},{76,64},{16,3... | collective-permute-start | bytes 3145736 | tf_op jit(solution)/shard_map/ppermute | solution.py:331
  87.5 29.7 %collective-permute-start.6 = (bf16[2,256,1024]{2,1,0:T(8,128)(2,1)}, bf16[2,256,1024]{2,1,0:T(8,128)(2,1)}, u32[]{:S(2)}, u32[]{:S(2)}) collective-permute-start(bf16[2,256,1024]{2,1,0:T(8,128)(2,1)} %slice.298), channel_id=1, source_target_pairs={{0,48},{64,76},{4,52},{68,64},{8,56},{72,68},{12,60},{76,72},{16,0... | collective-permute-start | bytes 3145736 | tf_op jit(solution)/shard_map/ppermute | solution.py:331
  133.5 13.3 %collective-permute-start.7 = (bf16[256,1024]{1,0:T(8,128)(2,1)}, bf16[256,1024]{1,0:T(8,128)(2,1)S(1)}, u32[]{:S(2)}, u32[]{:S(2)}) collective-permute-start(bf16[256,1024]{1,0:T(8,128)(2,1)} %get-tuple-element.30), channel_id=1, source_target_pairs={{0,2},{1,3},{2,0},{3,1},{4,6},{5,7},{6,4},{7,5},{8,10},{9,11},{10,... | collective-permute-start | bytes 1572872 | tf_op jit(solution)/shard_map/ppermute | solution.py:335
  139.4 13.0 %collective-permute-start.8 = (bf16[256,1024]{1,0:T(8,128)(2,1)}, bf16[256,1024]{1,0:T(8,128)(2,1)S(1)}, u32[]{:S(2)}, u32[]{:S(2)}) collective-permute-start(bf16[256,1024]{1,0:T(8,128)(2,1)} %get-tuple-element.31), channel_id=1, source_target_pairs={{0,1},{1,2},{2,3},{3,0},{4,5},{5,6},{6,7},{7,4},{8,9},{9,10},{10,1... | collective-permute-start | bytes 1572872 | tf_op jit(solution)/shard_map/ppermute | solution.py:335
  142.4 11.3 %collective-permute-start.9 = (bf16[256,1024]{1,0:T(8,128)(2,1)}, bf16[256,1024]{1,0:T(8,128)(2,1)S(1)}, u32[]{:S(2)}, u32[]{:S(2)}) collective-permute-start(bf16[256,1024]{1,0:T(8,128)(2,1)} %get-tuple-element.32), channel_id=1, source_target_pairs={{0,3},{1,0},{2,1},{3,2},{4,7},{5,4},{6,5},{7,6},{8,11},{9,8},{10,9... | collective-permute-start | bytes 1572872 | tf_op jit(solution)/shard_map/ppermute | solution.py:335
  157.5 14.0 %collective-permute-start.10 = (bf16[256,1024]{1,0:T(8,128)(2,1)S(1)}, bf16[256,1024]{1,0:T(8,128)(2,1)S(1)}, u32[]{:S(2)}, u32[]{:S(2)}) collective-permute-start(bf16[256,1024]{1,0:T(8,128)(2,1)S(1)} %pad_maximum_fusion.4), channel_id=1, source_target_pairs={{0,64},{1,65},{2,66},{3,67},{4,68},{5,69},{6,70},{7,71},{8,72},{9,... | collective-permute-start | bytes 1572872 | tf_op jit(solution)/shard_map/ppermute | solution.py:335
  158.8 12.7 %collective-permute-start.11 = (bf16[256,1024]{1,0:T(8,128)(2,1)S(1)}, bf16[256,1024]{1,0:T(8,128)(2,1)S(1)}, u32[]{:S(2)}, u32[]{:S(2)}) collective-permute-start(bf16[256,1024]{1,0:T(8,128)(2,1)S(1)} %pad_maximum_fusion.4), channel_id=1, source_target_pairs={{0,65},{1,66},{2,67},{3,64},{4,69},{5,70},{6,71},{7,68},{8,73},{9,... | collective-permute-start | bytes 1572872 | tf_op jit(solution)/shard_map/ppermute | solution.py:335
  160.1 12.3 %collective-permute-start.12 = (bf16[256,1024]{1,0:T(8,128)(2,1)S(1)}, bf16[256,1024]{1,0:T(8,128)(2,1)S(1)}, u32[]{:S(2)}, u32[]{:S(2)}) collective-permute-start(bf16[256,1024]{1,0:T(8,128)(2,1)S(1)} %pad_maximum_fusion.4), channel_id=1, source_target_pairs={{0,66},{1,67},{2,64},{3,65},{4,70},{5,71},{6,68},{7,69},{8,74},{9,... | collective-permute-start | bytes 1572872 | tf_op jit(solution)/shard_map/ppermute | solution.py:335
  161.5 12.5 %collective-permute-start.13 = (bf16[256,1024]{1,0:T(8,128)(2,1)S(1)}, bf16[256,1024]{1,0:T(8,128)(2,1)}, u32[]{:S(2)}, u32[]{:S(2)}) collective-permute-start(bf16[256,1024]{1,0:T(8,128)(2,1)S(1)} %pad_maximum_fusion.4), channel_id=1, source_target_pairs={{0,67},{1,64},{2,65},{3,66},{4,71},{5,68},{6,69},{7,70},{8,75},{9,... | collective-permute-start | bytes 1572872 | tf_op jit(solution)/shard_map/ppermute | solution.py:335
  200.7 30.4 %collective-permute-start.14 = (bf16[1152,1024]{1,0:T(8,128)(2,1)}, bf16[1152,1024]{1,0:T(8,128)(2,1)}, u32[]{:S(2)}, u32[]{:S(2)}) collective-permute-start(bf16[1152,1024]{1,0:T(8,128)(2,1)} %get-tuple-element.40), channel_id=1, source_target_pairs={{0,16},{64,68},{4,20},{68,72},{8,24},{72,76},{12,28},{76,64},{16,3... | collective-permute-start | bytes 7077896 | tf_op jit(solution)/shard_map/ppermute | solution.py:331
  201.9 29.2 %collective-permute-start.15 = (bf16[1152,1024]{1,0:T(8,128)(2,1)}, bf16[1152,1024]{1,0:T(8,128)(2,1)}, u32[]{:S(2)}, u32[]{:S(2)}) collective-permute-start(bf16[1152,1024]{1,0:T(8,128)(2,1)} %get-tuple-element.41), channel_id=1, source_target_pairs={{0,48},{64,76},{4,52},{68,64},{8,56},{72,68},{12,60},{76,72},{16,0... | collective-permute-start | bytes 7077896 | tf_op jit(solution)/shard_map/ppermute | solution.py:331
  232.7 17.1 %collective-permute-start.17 = (bf16[1152,512]{1,0:T(8,128)(2,1)S(1)}, bf16[1152,512]{1,0:T(8,128)(2,1)S(1)}, u32[]{:S(2)}, u32[]{:S(2)}) collective-permute-start(bf16[1152,512]{1,0:T(8,128)(2,1)S(1)} %add_convert_fusion), channel_id=1, source_target_pairs={{0,48},{64,76},{4,52},{68,64},{8,56},{72,68},{12,60},{76,72},{16,0... | collective-permute-start | bytes 3538952 | tf_op jit(solution)/shard_map/ppermute | solution.py:331
  237.8 24.9 %copy-start.23 = (bf16[2,128,1024]{2,1,0:T(8,128)(2,1)S(1)}, bf16[2,128,1024]{2,1,0:T(8,128)(2,1)}, u32[]{:S(2)}) copy-start(bf16[2,128,1024]{2,1,0:T(8,128)(2,1)} %copy-done.22) | copy-start | bytes 1572868
  237.8 24.9 %copy-start.36 = (bf16[2,1,128,1024]{3,2,1,0:T(8,128)(2,1)S(1)}, bf16[2,1,128,1024]{3,2,1,0:T(8,128)(2,1)}, u32[]{:S(2)}) copy-start(bf16[2,1,128,1024]{3,2,1,0:T(8,128)(2,1)} %param.13) | copy-start | bytes 1572868
  237.8 25.8 %copy-start.16 = (bf16[1,2,2,128,1024]{4,3,2,1,0:T(8,128)(2,1)S(1)}, bf16[1,2,2,128,1024]{4,3,2,1,0:T(8,128)(2,1)}, u32[]{:S(2)}) copy-start(bf16[1,2,2,128,1024]{4,3,2,1,0:T(8,128)(2,1)} %param.11) | copy-start | bytes 3145732
  237.9 25.8 %copy-start.25 = (bf16[128,1024]{1,0:T(8,128)(2,1)S(1)}, bf16[128,1024]{1,0:T(8,128)(2,1)}, u32[]{:S(2)}) copy-start(bf16[128,1024]{1,0:T(8,128)(2,1)} %copy-done.24) | copy-start | bytes 786436
  237.9 25.8 %copy-start.29 = (bf16[128,1024]{1,0:T(8,128)(2,1)S(1)}, bf16[128,1024]{1,0:T(8,128)(2,1)}, u32[]{:S(2)}) copy-start(bf16[128,1024]{1,0:T(8,128)(2,1)} %get-tuple-element.50) | copy-start | bytes 786436
  237.9 25.7 %copy-start.52 = (pred[2]{0:T(512)(128)(4,1)S(1)}, pred[2]{0:T(512)(128)(4,1)}, u32[]{:S(2)}) copy-start(pred[2]{0:T(512)(128)(4,1)} %copy-done.50) | copy-start | bytes 10
  237.9 25.7 %copy-start.54 = (pred[2]{0:T(512)(128)(4,1)S(1)}, pred[2]{0:T(512)(128)(4,1)}, u32[]{:S(2)}) copy-start(pred[2]{0:T(512)(128)(4,1)} %copy-done.53) | copy-start | bytes 10
  237.9 17.5 %collective-permute-start.16 = (bf16[1152,512]{1,0:T(8,128)(2,1)S(1)}, bf16[1152,512]{1,0:T(8,128)(2,1)S(1)}, u32[]{:S(2)}, u32[]{:S(2)}) collective-permute-start(bf16[1152,512]{1,0:T(8,128)(2,1)S(1)} %add_convert_fusion.1), channel_id=1, source_target_pairs={{0,16},{64,68},{4,20},{68,72},{8,24},{72,76},{12,28},{76,64},{16,3... | collective-permute-start | bytes 3538952 | tf_op jit(solution)/shard_map/ppermute | solution.py:331
  257.6 11.6 %collective-permute-start.18 = (bf16[1152,256]{1,0:T(8,128)(2,1)S(1)}, bf16[1152,256]{1,0:T(8,128)(2,1)S(1)}, u32[]{:S(2)}, u32[]{:S(2)}) collective-permute-start(bf16[1152,256]{1,0:T(8,128)(2,1)S(1)} %get-tuple-element.61), channel_id=1, source_target_pairs={{0,8},{64,96},{4,12},{68,100},{8,0},{72,104},{12,4},{76,108},{16,2... | collective-permute-start | bytes 1769480 | tf_op jit(solution)/shard_map/ppermute | solution.py:331
  259.5 15.9 %collective-permute-start.19 = (bf16[1152,256]{1,0:T(8,128)(2,1)S(1)}, bf16[1152,256]{1,0:T(8,128)(2,1)S(1)}, u32[]{:S(2)}, u32[]{:S(2)}) collective-permute-start(bf16[1152,256]{1,0:T(8,128)(2,1)S(1)} %get-tuple-element.63), channel_id=1, source_target_pairs={{0,4},{64,80},{4,8},{68,84},{8,12},{72,88},{12,0},{76,92},{16,20},... | collective-permute-start | bytes 1769480 | tf_op jit(solution)/shard_map/ppermute | solution.py:331
  260.8 14.6 %collective-permute-start.20 = (bf16[1152,256]{1,0:T(8,128)(2,1)S(1)}, bf16[1152,256]{1,0:T(8,128)(2,1)S(1)}, u32[]{:S(2)}, u32[]{:S(2)}) collective-permute-start(bf16[1152,256]{1,0:T(8,128)(2,1)S(1)} %get-tuple-element.62), channel_id=1, source_target_pairs={{0,12},{64,112},{4,0},{68,116},{8,4},{72,120},{12,8},{76,124},{16,... | collective-permute-start | bytes 1769480 | tf_op jit(solution)/shard_map/ppermute | solution.py:331
  (49 other events, 311.5 us)
Sparse Core Ops, SparseCore 0:
  11.7 104.0 all-gather.1
  214.6 38.6 reduce-scatter.1

commit v3 on v2

--- a/solution.py
+++ b/solution.py
@@ -20,6 +20,7 @@
 
 
 GROUP = HQ // HK
+UNITS = 3
 NT = (((1,), (1,)), ((), ()))
 TN = (((0,), (0,)), ((), ()))
 
@@ -321,6 +322,46 @@
     )(*operands)
 
 
+def finish_kernel(flags, new_in, state_out, summed, x_0, x_1, x_2, scale, inverse, copies_ref):
+    first = flags[0] == 1
+    units = (
+        (x_0, jnp.where(first, flags[3], flags[1]), first | True),
+        (x_1, flags[2], jnp.logical_not(first)),
+        (x_2, flags[3], jnp.logical_not(first)),
+    )
+
+    def step(i, carry):
+        at = pl.multiple_of(i * ROWS, ROWS)
+        rows = pl.ds(at, ROWS)
+        states = [state_out[0, rows, :], state_out[1, rows, :]]
+        for unit, (inputs, slot, active) in enumerate(units):
+            total = summed[pl.ds(at + unit * SEQ, ROWS), :].astype(f32)
+            output = (inputs[rows, :].astype(f32) + total).astype(bf16).astype(f32)
+            old = jnp.where(slot == 0, states[0], states[1]).astype(f32)
+            sent = jnp.clip((output - old) * inverse[...], -qmax, qmax).astype(bf16)
+            renewed = (old + scale[...] * sent.astype(f32)).astype(bf16)
+            for k in range(2):
+                states[k] = jnp.where(active & (slot == k), renewed, states[k])
+        for k in range(2):
+            copies_ref[0, 0, k, rows, :] = new_in[k, rows, :]
+            copies_ref[0, 1, k, rows, :] = states[k]
+        return carry
+
+    lax.fori_loop(0, SEQ // ROWS, step, 0)
+
+
+def finish(*operands):
+    return pl.pallas_call(
+        finish_kernel,
+        in_specs=[SMEM] + [VMEM] * 8,
+        out_specs=VMEM,
+        out_shape=jax.ShapeDtypeStruct((1, 2, 2, SEQ, 1024), bf16),
+        compiler_params=GRANT,
+        cost_estimate=pl.CostEstimate(flops=2**23, bytes_accessed=5 * 2**20, transcendentals=0),
+        name="finish",
+    )(*operands)
+
+
 def along(shard, second, by):
     pairs = []
     for y in range(4):
@@ -366,9 +407,9 @@
         for columns in (slice(0, 256), slice(256, 512)):
             blocks.append(plus(*(part[:, columns] for part in parts)))
     got = [
+        along(blocks[3], False, -1),
+        along(blocks[1], False, 1),
         along(blocks[2], False, 2),
-        along(blocks[1], False, 1),
-        along(blocks[3], False, -1),
     ]
     return plus(blocks[0], *got), own
 
@@ -450,7 +491,7 @@
     qkv_a, mixed_a = project_call(project_a_kernel, "project_a", [flags, normed_a], pieces, False)
     far, near_1, near_3, own = spread(flags, mixed_a, full)
     parts = [own] + [
-        from_first(piece, by, 0) for piece, by in ((far, 2), (near_1, 1), (near_3, 3))
+        from_first(piece, by, 0) for piece, by in ((near_3, 3), (near_1, 1), (far, 2))
     ]
     summed = sum(part.astype(f32) for part in parts)
     step_0, renewed = deliver(state_out, slot[0], x0, summed[:SEQ])
@@ -485,17 +526,18 @@
     mixed_f = jnp.concatenate([jnp.where(first, mixed_b[:SEQ], mixed_a[:SEQ]), mixed_b], 0)
     mixed_f, _ = lax.optimization_barrier((mixed_f, own_terms))
     partial = lax.dot_general(mixed_f, full_o, NT, preferred_element_type=f32).astype(bf16)
-    summed = lax.psum_scatter(partial, "tensor", scatter_dimension=1, tiled=True).astype(f32)
-    _, renewed = deliver(out_2, slot[2], x2, summed[:SEQ])
-    new_out_first = put(out_2, slot[2], renewed)
-    _, renewed = deliver(state_out, slot[0], x0, summed[:SEQ])
-    out_1 = put(state_out, slot[0], renewed)
-    _, renewed = deliver(out_1, slot[1], y1, summed[SEQ : 2 * SEQ])
-    out_1 = put(out_1, slot[1], renewed)
-    _, renewed = deliver(out_1, slot[2], y2, summed[2 * SEQ :])
-    new_out = jnp.where(first, new_out_first, put(out_1, slot[2], renewed))
-
-    copies_new = jnp.stack([new_in, new_out])[None]
+    summed = lax.psum_scatter(partial, "tensor", scatter_dimension=1, tiled=True)
+    copies_new = finish(
+        flags,
+        new_in,
+        jnp.where(first, out_2, state_out),
+        summed,
+        jnp.where(first, x2, x0),
+        y1,
+        y2,
+        scale_next[None],
+        inverse_next[None],
+    )
     return (copies_new, grad[None, :, :1024], grad[None, :, 1024:])
 
 

time: 295 us -> 291 us (0.986)
  waiting for transfers between devices: 114 us -> 109 us
  other arithmetic: 27.4 us -> 23.2 us
  Pallas kernels: 44.1 us -> 47.8 us
  starting transfers between devices: 50.5 us -> 53.6 us
    ppermute x14, waiting for transfers between devices: 105 us -> 99.7 us  [along(): return lax.ppermute(shard, ('section', 'y', 'x'), pairs)]
    pallas_call x0 -> x1, Pallas kernels: none -> 3.66 us  [finish(): pl.pallas_call(finish_kernel, in_specs=[SMEM] + [VMEM] * 8, out_specs=VME...]
    unnamed x117 -> x89, local copies, waits for them, and re-layouts: 14.2 us -> 12.1 us
  transfers between devices with their start and end apart: 24 -> 24, of which waited for: 13 -> 15; matrix products, arithmetic and copies ran while one was open for 15% -> 15% of each run, Pallas kernels for 2% -> 2%
where the time goes in v3:
time: 291 us; the launch traced here: 289 us
  waiting for transfers between devices  109 us (37%)
  starting transfers between devices  53.6 us (18%)
  Pallas kernels  47.8 us (16%)
  other arithmetic  23.2 us (8%)
  local copies, waits for them, and re-layouts  21 us (7%)
  between operations  18.5 us (6%)
  matrix products  16.3 us (6%)
    ppermute x14, waiting for transfers between devices, along(): return lax.ppermute(shard, ('section', 'y', 'x'), pairs)  99.7 us
    ppermute x14, starting transfers between devices, along(): return lax.ppermute(shard, ('section', 'y', 'x'), pairs)  26.2 us
    pallas_call x2, Pallas kernels, project_call(): pl.pallas_call(kernel, in_specs=[SMEM] + [VMEM] * (len(operands) - 1) + [...  22.2 us
    ppermute x7, starting transfers between devices, from_first(): lax.ppermute(shard, ('section', 'tensor'), [(i, 4 * to_section + (i + by)...  19.9 us
    unnamed x89, local copies, waits for them, and re-layouts  12.1 us
    dot_general x1, matrix products, on_device(): lax.dot_general(mixed_f, full_o, NT, preferred_element_type=f32)  10.4 us
    ppermute x7, waiting for transfers between devices, from_first(): lax.ppermute(shard, ('section', 'tensor'), [(i, 4 * to_section + (i + by)...  8.87 us
    all_to_all x1, starting transfers between devices, on_device(): lax.all_to_all(jnp.broadcast_to(known[None], (4,) + known.shape), 'tensor...  7.48 us
  transfers between devices with their start and end apart: 24, of which 15 were waited for; matrix products, arithmetic and copies ran while one was open for 15% of the time, Pallas kernels for 2%

profile of v3, /device:TPU:0, one launch (start us, length us, event | category | flops | bytes accessed | tf_op | source)
XLA Modules:
  0.0 289.1 jit_solution(17398033015148355982)
XLA Ops:
  7.2 2.2 copy.14
  9.4 2.1 pad_maximum_fusion.3
  11.5 3.2 %collective-permute-start.2 = (bf16[256,1024]{1,0:T(8,128)(2,1)}, bf16[256,1024]{1,0:T(8,128)(2,1)}, u32[]{:S(2)}, u32[]{:S(2)}) collective-permute-start(bf16[256,1024]{1,0:T(8,128)(2,1)} %bitcast.143), channel_id=1, source_target_pairs={{0,8},{64,96},{4,12},{68,100},{8,0},{72,104},{12,4},{76,108},{16,2... | collective-permute-start | bytes 1572872 | tf_op jit(solution)/shard_map/ppermute | solution.py:372
  25.2 6.6 %collective-permute-done.1 = bf16[256,1024]{1,0:T(8,128)(2,1)} collective-permute-done((bf16[256,1024]{1,0:T(8,128)(2,1)}, bf16[256,1024]{1,0:T(8,128)(2,1)}, u32[]{:S(2)}, u32[]{:S(2)}) %collective-permute-start.1) | collective-permute-done | bytes 524320 | tf_op jit(solution)/shard_map/ppermute | solution.py:372
  32.1 3.0 %pad_maximum_fusion.refs_1_.refs_5_ = bf16[4,256,1024]{2,1,0:T(8,128)(2,1)} fusion(bf16[1,256,1024]{2,1,0:T(8,128)(2,1)} %bitcast.34, bf16[1,256,1024]{2,1,0:T(8,128)(2,1)} %bitcast.33, bf16[1,256,1024]{2,1,0:T(8,128)(2,1)} %bitcast.32, bf16[1,256,1024]{2,1,0:T(8,128)(2,1)S(1)} %copy-done.40), kind=kLoop, calls=%fused_computation.7 | loop fusion | flops 3145728 | bytes 4194304 | tf_op jit(solution)/shard_map/stack | solution.py:383
  41.9 7.5 %all-to-all-start = ((bf16[4,384,1024]{2,1,0:T(8,128)(2,1)}), bf16[4,384,1024]{2,1,0:T(8,128)(2,1)}, u32[]{:S(2)}, u32[]{:S(2)}) async-start(bf16[4,384,1024]{2,1,0:T(8,128)(2,1)} %broadcast_in_dim.125), calls=%async_computation | async-start | bytes 6291456 | tf_op jit(solution)/shard_map/all_to_all | solution.py:479
  49.4 33.7 %collective-permute-done.3.refs_2_.refs_6_ = bf16[4,256,1024]{2,1,0:T(8,128)(2,1)} collective-permute-done((bf16[4,256,1024]{2,1,0:T(8,128)(2,1)}, bf16[4,256,1024]{2,1,0:T(8,128)(2,1)}, u32[]{:S(2)}, u32[]{:S(2)}) %collective-permute-start.3) | collective-permute-done | bytes 2097184 | tf_op jit(solution)/shard_map/ppermute | solution.py:372
  83.1 2.3 slice.258
  85.4 2.5 collective-permute-start.5
  87.9 2.3 slice.259
  91.7 4.5 %prepare.1.normed_ref.normed_a = bf16[256,4096]{1,0:T(8,128)(2,1)S(1)} custom-call(s32[7]{0:T(128)S(1)} %stack.47.flags, f32[1,4096]{1,0:T(1,128)S(1)} %copy-done.10, bf16[4,384,1024]{2,1,0:T(8,128)(2,1)} %all-to-all-done.known_ref), custom_call_target="tpu_custom_call" | custom-call | flops 8388608 | bytes 5242880 | tf_op jit(solution)/shard_map/prepare/pallas_call | solution.py:156
  97.5 19.2 %collective-permute-done.5.refs_4_.refs_8_ = bf16[2,256,1024]{2,1,0:T(8,128)(2,1)} collective-permute-done((bf16[2,256,1024]{2,1,0:T(8,128)(2,1)}, bf16[2,256,1024]{2,1,0:T(8,128)(2,1)}, u32[]{:S(2)}, u32[]{:S(2)}) %collective-permute-start.5) | collective-permute-done | bytes 1048608 | tf_op jit(solution)/shard_map/ppermute | solution.py:372
  116.7 9.8 %project_a.1 = (bf16[256,1280]{1,0:T(8,128)(2,1)}, bf16[256,1024]{1,0:T(8,128)(2,1)}) custom-call(s32[7]{0:T(128)} %copy-done.11, bf16[256,4096]{1,0:T(8,128)(2,1)} %copy-done.2, bf16[4096,1280]{1,0:T(8,128)(2,1)} %all-gather.2.cloned.1.call-done.refs_0_.full_ref.refs_4_, bf16[4,256,1024]{2,1,0:T(8,128)(2,1)} %pad_maximum_fusion.refs_1_.refs_5_, ...), custom_call_target="tpu_custom_call" | custom-call | flops 2684354560 | bytes 18874368 | tf_op jit(solution)/shard_map/project_a/pallas_call | solution.py:226
  126.5 6.5 %spread.1 = (bf16[256,1024]{1,0:T(8,128)(2,1)}, bf16[256,1024]{1,0:T(8,128)(2,1)}, bf16[256,1024]{1,0:T(8,128)(2,1)}, bf16[256,1024]{1,0:T(8,128)(2,1)}) custom-call(s32[7]{0:T(128)} %copy-done.11, bf16[256,1024]{1,0:T(8,128)(2,1)} %get-tuple-element.28.mixed_ref, bf16[4096,1280]{1,0:T(8,128)(2,1)} %all-gather.2.cloned.1.call-done.refs_0_.full_ref.refs_4_), custom_call_target="tpu_custom_call" | custom-call | flops 2147483648 | bytes 12582912 | tf_op jit(solution)/shard_map/spread/pallas_call | solution.py:262
  133.0 6.6 %collective-permute-start.9 = (bf16[256,1024]{1,0:T(8,128)(2,1)}, bf16[256,1024]{1,0:T(8,128)(2,1)S(1)}, u32[]{:S(2)}, u32[]{:S(2)}) collective-permute-start(bf16[256,1024]{1,0:T(8,128)(2,1)} %get-tuple-element.32), channel_id=1, source_target_pairs={{0,2},{1,3},{2,0},{3,1},{4,6},{5,7},{6,4},{7,5},{8,10},{9,11},{10,... | collective-permute-start | bytes 1572872 | tf_op jit(solution)/shard_map/ppermute | solution.py:376
  139.6 4.0 %collective-permute-start.8 = (bf16[256,1024]{1,0:T(8,128)(2,1)}, bf16[256,1024]{1,0:T(8,128)(2,1)S(1)}, u32[]{:S(2)}, u32[]{:S(2)}) collective-permute-start(bf16[256,1024]{1,0:T(8,128)(2,1)} %get-tuple-element.31), channel_id=1, source_target_pairs={{0,1},{1,2},{2,3},{3,0},{4,5},{5,6},{6,7},{7,4},{8,9},{9,10},{10,1... | collective-permute-start | bytes 1572872 | tf_op jit(solution)/shard_map/ppermute | solution.py:376
  143.7 3.2 %collective-permute-start.7 = (bf16[256,1024]{1,0:T(8,128)(2,1)}, bf16[256,1024]{1,0:T(8,128)(2,1)S(1)}, u32[]{:S(2)}, u32[]{:S(2)}) collective-permute-start(bf16[256,1024]{1,0:T(8,128)(2,1)} %get-tuple-element.30), channel_id=1, source_target_pairs={{0,3},{1,0},{2,1},{3,2},{4,7},{5,4},{6,5},{7,6},{8,11},{9,8},{10,9... | collective-permute-start | bytes 1572872 | tf_op jit(solution)/shard_map/ppermute | solution.py:376
  147.0 5.6 %collective-permute-done.8 = bf16[256,1024]{1,0:T(8,128)(2,1)S(1)} collective-permute-done((bf16[256,1024]{1,0:T(8,128)(2,1)}, bf16[256,1024]{1,0:T(8,128)(2,1)S(1)}, u32[]{:S(2)}, u32[]{:S(2)}) %collective-permute-start.8) | collective-permute-done | bytes 524320 | tf_op jit(solution)/shard_map/ppermute | solution.py:376
  152.6 2.4 collective-permute-done.7
  162.6 2.1 collective-permute-start.13
  164.7 6.0 %fusion.10 = bf16[384,1024]{1,0:T(8,128)(2,1)S(1)} fusion(bf16[384,4096]{1,0:T(8,128)(2,1)S(1)} %bitcast.141, bf16[4096,1280]{1,0:T(8,128)(2,1)} %all-gather.2.cloned.1.call-done.refs_0_.full_ref.refs_4_), kind=kOutput, calls=%fused_computation.9 | convolution fusion | flops 3221618688 | bytes 12320768 | tf_op jit(solution)/shard_map/dot_general | solution.py:516
  174.5 12.4 %project_b.1 = (bf16[256,4096]{1,0:T(8,128)(2,1)}, bf16[256,1280]{1,0:T(8,128)(2,1)}, bf16[256,1024]{1,0:T(8,128)(2,1)}) custom-call(s32[7]{0:T(128)} %copy-done.11, f32[1,4096]{1,0:T(1,128)} %gain_ref.3, bf16[4,384,1024]{2,1,0:T(8,128)(2,1)} %all-to-all-done.known_ref, bf16[256,1024]{1,0:T(8,128)(2,1)} %copy-done.32, bf16[256,1024]{1,0:T(8,128)(2,1)} %copy-done.38, ...), custom_call_target="tpu_custom_call" | custom-call | flops 2684354560 | bytes 18874368 | tf_op jit(solution)/shard_map/project_b/pallas_call | solution.py:226
  191.5 7.4 %terms.1 = (bf16[1152,1024]{1,0:T(8,128)(2,1)}, bf16[1152,1024]{1,0:T(8,128)(2,1)}, bf16[1152,512]{1,0:T(8,128)(2,1)S(1)}, bf16[1152,512]{1,0:T(8,128)(2,1)S(1)}, bf16[1152,1024]{1,0:T(8,128)(2,1)S(1)}) custom-call(s32[7]{0:T(128)S(1)} %copy-done.12, bf16[256,4096]{1,0:T(8,128)(2,1)S(1)} %copy-done.3, bf16[256,4096]{1,0:T(8,128)(2,1)S(1)} %copy-done.13, ...), custom_call_target="tpu_custom_call" | custom-call | flops 3623878656 | bytes 14680064 | tf_op jit(solution)/shard_map/terms/pallas_call | solution.py:311
  204.6 10.4 %fusion.4 = bf16[384,4096]{1,0:T(8,128)(2,1)} fusion(bf16[384,1024]{1,0:T(8,128)(2,1)S(1)} %pad_maximum_fusion.2, bf16[4096,1280]{1,0:T(8,128)(2,1)} %all-gather.2.cloned.1.call-done.refs_0_.full_ref.refs_4_), kind=kOutput, calls=%fused_computation.4 | convolution fusion | flops 3222798336 | bytes 12320768 | tf_op jit(solution)/shard_map/dot_general | solution.py:528
  215.0 16.6 %collective-permute-done.14 = bf16[1152,1024]{1,0:T(8,128)(2,1)} collective-permute-done((bf16[1152,1024]{1,0:T(8,128)(2,1)}, bf16[1152,1024]{1,0:T(8,128)(2,1)}, u32[]{:S(2)}, u32[]{:S(2)}) %collective-permute-start.14) | collective-permute-done | bytes 2359328 | tf_op jit(solution)/shard_map/ppermute | solution.py:372
  239.3 11.9 %collective-permute-done.16 = bf16[1152,512]{1,0:T(8,128)(2,1)S(1)} collective-permute-done((bf16[1152,512]{1,0:T(8,128)(2,1)S(1)}, bf16[1152,512]{1,0:T(8,128)(2,1)S(1)}, u32[]{:S(2)}, u32[]{:S(2)}) %collective-permute-start.16) | collective-permute-done | bytes 1179680 | tf_op jit(solution)/shard_map/ppermute | solution.py:372
  253.3 2.2 add_convert_fusion.5
  255.5 4.0 %collective-permute-start.20 = (bf16[1152,256]{1,0:T(8,128)(2,1)S(1)}, bf16[1152,256]{1,0:T(8,128)(2,1)S(1)}, u32[]{:S(2)}, u32[]{:S(2)}) collective-permute-start(bf16[1152,256]{1,0:T(8,128)(2,1)S(1)} %get-tuple-element.59), channel_id=1, source_target_pairs={{0,8},{64,96},{4,12},{68,100},{8,0},{72,104},{12,4},{76,108},{16,2... | collective-permute-start | bytes 1769480 | tf_op jit(solution)/shard_map/ppermute | solution.py:372
  259.7 3.1 %collective-permute-start.18 = (bf16[1152,256]{1,0:T(8,128)(2,1)S(1)}, bf16[1152,256]{1,0:T(8,128)(2,1)S(1)}, u32[]{:S(2)}, u32[]{:S(2)}) collective-permute-start(bf16[1152,256]{1,0:T(8,128)(2,1)S(1)} %get-tuple-element.58), channel_id=1, source_target_pairs={{0,12},{64,112},{4,0},{68,116},{8,4},{72,120},{12,8},{76,124},{16,... | collective-permute-start | bytes 1769480 | tf_op jit(solution)/shard_map/ppermute | solution.py:372
  265.1 2.4 collective-permute-done.20
  267.5 6.2 %collective-permute-done.19 = bf16[1152,256]{1,0:T(8,128)(2,1)S(1)} collective-permute-done((bf16[1152,256]{1,0:T(8,128)(2,1)S(1)}, bf16[1152,256]{1,0:T(8,128)(2,1)S(1)}, u32[]{:S(2)}, u32[]{:S(2)}) %collective-permute-start.19) | collective-permute-done | bytes 589856 | tf_op jit(solution)/shard_map/ppermute | solution.py:372
  278.6 3.7 %finish.1 = bf16[1,2,2,128,1024]{4,3,2,1,0:T(8,128)(2,1)} custom-call(s32[7]{0:T(128)} %copy-done.11, bf16[2,128,1024]{2,1,0:T(8,128)(2,1)} %select_select_fusion.new_in, bf16[2,128,1024]{2,1,0:T(8,128)(2,1)} %get-tuple-element.70.state_out, bf16[384,1024]{1,0:T(8,128)(2,1)} %reduce-scatter.2.cloned.1.call-done.summed, ...), custom_call_target="tpu_custom_call" | custom-call | flops 8388608 | bytes 5242880 | tf_op jit(solution)/shard_map/finish/pallas_call | solution.py:354
  (163 shorter events, 55.0 us)
Async XLA Ops:
  7.2 157.6 %copy-start = (bf16[1,3,1,128,4096]{4,3,2,1,0:T(8,128)(2,1)S(1)}, bf16[1,3,1,128,4096]{4,3,2,1,0:T(8,128)(2,1)}, u32[]{:S(2)}) copy-start(bf16[1,3,1,128,4096]{4,3,2,1,0:T(8,128)(2,1)} %param.21) | copy-start | bytes 9437188
  7.2 109.5 %all-gather.2.cloned.1.call-start = ((), (), s32[]{:S(2)}) async-start(), calls=%async_computation.2 | async-start | bytes 11141120 | tf_op jit(solution)/shard_map/all_gather | solution.py:444
  11.5 13.6 %collective-permute-start.2 = (bf16[256,1024]{1,0:T(8,128)(2,1)}, bf16[256,1024]{1,0:T(8,128)(2,1)}, u32[]{:S(2)}, u32[]{:S(2)}) collective-permute-start(bf16[256,1024]{1,0:T(8,128)(2,1)} %bitcast.143), channel_id=1, source_target_pairs={{0,8},{64,96},{4,12},{68,100},{8,0},{72,104},{12,4},{76,108},{16,2... | collective-permute-start | bytes 1572872 | tf_op jit(solution)/shard_map/ppermute | solution.py:372
  14.7 17.1 %collective-permute-start.1 = (bf16[256,1024]{1,0:T(8,128)(2,1)}, bf16[256,1024]{1,0:T(8,128)(2,1)}, u32[]{:S(2)}, u32[]{:S(2)}) collective-permute-start(bf16[256,1024]{1,0:T(8,128)(2,1)} %bitcast.144), channel_id=1, source_target_pairs={{0,12},{64,112},{4,0},{68,116},{8,4},{72,120},{12,8},{76,124},{16,... | collective-permute-start | bytes 1572872 | tf_op jit(solution)/shard_map/ppermute | solution.py:372
  15.9 16.2 %collective-permute-start = (bf16[256,1024]{1,0:T(8,128)(2,1)}, bf16[256,1024]{1,0:T(8,128)(2,1)}, u32[]{:S(2)}, u32[]{:S(2)}) collective-permute-start(bf16[256,1024]{1,0:T(8,128)(2,1)} %bitcast.145), channel_id=1, source_target_pairs={{0,4},{64,80},{4,8},{68,84},{8,12},{72,88},{12,0},{76,92},{16,20},... | collective-permute-start | bytes 1572872 | tf_op jit(solution)/shard_map/ppermute | solution.py:372
  20.1 18.5 %copy-start.17 = (bf16[128,1024]{1,0:T(8,128)(2,1)}, bf16[128,1024]{1,0:T(8,128)(2,1)S(1)}, u32[]{:S(2)}) copy-start(bf16[128,1024]{1,0:T(8,128)(2,1)S(1)} %fusion.37) | copy-start | bytes 786436
  35.1 48.0 %collective-permute-start.3 = (bf16[4,256,1024]{2,1,0:T(8,128)(2,1)}, bf16[4,256,1024]{2,1,0:T(8,128)(2,1)}, u32[]{:S(2)}, u32[]{:S(2)}) collective-permute-start(bf16[4,256,1024]{2,1,0:T(8,128)(2,1)} %pad_maximum_fusion.refs_1_.refs_5_), channel_id=1, source_target_pairs={{0,16},{64,68},{4,20},{68,72},{8,24},{72,76},{12,28},{76,64},{16,3... | collective-permute-start | bytes 6291464 | tf_op jit(solution)/shard_map/ppermute | solution.py:372
  36.5 51.4 %collective-permute-start.4 = (bf16[4,256,1024]{2,1,0:T(8,128)(2,1)}, bf16[4,256,1024]{2,1,0:T(8,128)(2,1)}, u32[]{:S(2)}, u32[]{:S(2)}) collective-permute-start(bf16[4,256,1024]{2,1,0:T(8,128)(2,1)} %pad_maximum_fusion.refs_1_.refs_5_), channel_id=1, source_target_pairs={{0,48},{64,76},{4,52},{68,64},{8,56},{72,68},{12,60},{76,72},{16,0... | collective-permute-start | bytes 6291464 | tf_op jit(solution)/shard_map/ppermute | solution.py:372
  41.9 49.8 %all-to-all-start = ((bf16[4,384,1024]{2,1,0:T(8,128)(2,1)}), bf16[4,384,1024]{2,1,0:T(8,128)(2,1)}, u32[]{:S(2)}, u32[]{:S(2)}) async-start(bf16[4,384,1024]{2,1,0:T(8,128)(2,1)} %broadcast_in_dim.125), calls=%async_computation | async-start | bytes 6291456 | tf_op jit(solution)/shard_map/all_to_all | solution.py:479
  49.4 227.9 %reduce-scatter.2.cloned.1.call-start = ((), (), s32[]{:S(2)}) async-start(), calls=%async_computation.3 | async-start | bytes 3932160 | tf_op jit(solution)/shard_map/reduce_scatter | solution.py:529
  85.4 31.3 %collective-permute-start.5 = (bf16[2,256,1024]{2,1,0:T(8,128)(2,1)}, bf16[2,256,1024]{2,1,0:T(8,128)(2,1)}, u32[]{:S(2)}, u32[]{:S(2)}) collective-permute-start(bf16[2,256,1024]{2,1,0:T(8,128)(2,1)} %slice.258), channel_id=1, source_target_pairs={{0,16},{64,68},{4,20},{68,72},{8,24},{72,76},{12,28},{76,64},{16,3... | collective-permute-start | bytes 3145736 | tf_op jit(solution)/shard_map/ppermute | solution.py:372
  90.2 26.5 %collective-permute-start.6 = (bf16[2,256,1024]{2,1,0:T(8,128)(2,1)}, bf16[2,256,1024]{2,1,0:T(8,128)(2,1)}, u32[]{:S(2)}, u32[]{:S(2)}) collective-permute-start(bf16[2,256,1024]{2,1,0:T(8,128)(2,1)} %slice.259), channel_id=1, source_target_pairs={{0,48},{64,76},{4,52},{68,64},{8,56},{72,68},{12,60},{76,72},{16,0... | collective-permute-start | bytes 3145736 | tf_op jit(solution)/shard_map/ppermute | solution.py:372
  133.0 14.0 %collective-permute-start.9 = (bf16[256,1024]{1,0:T(8,128)(2,1)}, bf16[256,1024]{1,0:T(8,128)(2,1)S(1)}, u32[]{:S(2)}, u32[]{:S(2)}) collective-permute-start(bf16[256,1024]{1,0:T(8,128)(2,1)} %get-tuple-element.32), channel_id=1, source_target_pairs={{0,2},{1,3},{2,0},{3,1},{4,6},{5,7},{6,4},{7,5},{8,10},{9,11},{10,... | collective-permute-start | bytes 1572872 | tf_op jit(solution)/shard_map/ppermute | solution.py:376
  139.6 13.0 %collective-permute-start.8 = (bf16[256,1024]{1,0:T(8,128)(2,1)}, bf16[256,1024]{1,0:T(8,128)(2,1)S(1)}, u32[]{:S(2)}, u32[]{:S(2)}) collective-permute-start(bf16[256,1024]{1,0:T(8,128)(2,1)} %get-tuple-element.31), channel_id=1, source_target_pairs={{0,1},{1,2},{2,3},{3,0},{4,5},{5,6},{6,7},{7,4},{8,9},{9,10},{10,1... | collective-permute-start | bytes 1572872 | tf_op jit(solution)/shard_map/ppermute | solution.py:376
  143.7 11.3 %collective-permute-start.7 = (bf16[256,1024]{1,0:T(8,128)(2,1)}, bf16[256,1024]{1,0:T(8,128)(2,1)S(1)}, u32[]{:S(2)}, u32[]{:S(2)}) collective-permute-start(bf16[256,1024]{1,0:T(8,128)(2,1)} %get-tuple-element.30), channel_id=1, source_target_pairs={{0,3},{1,0},{2,1},{3,2},{4,7},{5,4},{6,5},{7,6},{8,11},{9,8},{10,9... | collective-permute-start | bytes 1572872 | tf_op jit(solution)/shard_map/ppermute | solution.py:376
  158.7 14.0 %collective-permute-start.10 = (bf16[256,1024]{1,0:T(8,128)(2,1)S(1)}, bf16[256,1024]{1,0:T(8,128)(2,1)S(1)}, u32[]{:S(2)}, u32[]{:S(2)}) collective-permute-start(bf16[256,1024]{1,0:T(8,128)(2,1)S(1)} %pad_maximum_fusion.4), channel_id=1, source_target_pairs={{0,64},{1,65},{2,66},{3,67},{4,68},{5,69},{6,70},{7,71},{8,72},{9,... | collective-permute-start | bytes 1572872 | tf_op jit(solution)/shard_map/ppermute | solution.py:376
  160.0 12.7 %collective-permute-start.11 = (bf16[256,1024]{1,0:T(8,128)(2,1)S(1)}, bf16[256,1024]{1,0:T(8,128)(2,1)S(1)}, u32[]{:S(2)}, u32[]{:S(2)}) collective-permute-start(bf16[256,1024]{1,0:T(8,128)(2,1)S(1)} %pad_maximum_fusion.4), channel_id=1, source_target_pairs={{0,65},{1,66},{2,67},{3,64},{4,69},{5,70},{6,71},{7,68},{8,73},{9,... | collective-permute-start | bytes 1572872 | tf_op jit(solution)/shard_map/ppermute | solution.py:376
  161.3 12.3 %collective-permute-start.12 = (bf16[256,1024]{1,0:T(8,128)(2,1)S(1)}, bf16[256,1024]{1,0:T(8,128)(2,1)S(1)}, u32[]{:S(2)}, u32[]{:S(2)}) collective-permute-start(bf16[256,1024]{1,0:T(8,128)(2,1)S(1)} %pad_maximum_fusion.4), channel_id=1, source_target_pairs={{0,66},{1,67},{2,64},{3,65},{4,70},{5,71},{6,68},{7,69},{8,74},{9,... | collective-permute-start | bytes 1572872 | tf_op jit(solution)/shard_map/ppermute | solution.py:376
  162.6 11.9 %collective-permute-start.13 = (bf16[256,1024]{1,0:T(8,128)(2,1)S(1)}, bf16[256,1024]{1,0:T(8,128)(2,1)}, u32[]{:S(2)}, u32[]{:S(2)}) collective-permute-start(bf16[256,1024]{1,0:T(8,128)(2,1)S(1)} %pad_maximum_fusion.4), channel_id=1, source_target_pairs={{0,67},{1,64},{2,65},{3,66},{4,71},{5,68},{6,69},{7,70},{8,75},{9,... | collective-permute-start | bytes 1572872 | tf_op jit(solution)/shard_map/ppermute | solution.py:376
  201.3 30.4 %collective-permute-start.14 = (bf16[1152,1024]{1,0:T(8,128)(2,1)}, bf16[1152,1024]{1,0:T(8,128)(2,1)}, u32[]{:S(2)}, u32[]{:S(2)}) collective-permute-start(bf16[1152,1024]{1,0:T(8,128)(2,1)} %get-tuple-element.40), channel_id=1, source_target_pairs={{0,16},{64,68},{4,20},{68,72},{8,24},{72,76},{12,28},{76,64},{16,3... | collective-permute-start | bytes 7077896 | tf_op jit(solution)/shard_map/ppermute | solution.py:372
  202.9 29.2 %collective-permute-start.15 = (bf16[1152,1024]{1,0:T(8,128)(2,1)}, bf16[1152,1024]{1,0:T(8,128)(2,1)}, u32[]{:S(2)}, u32[]{:S(2)}) collective-permute-start(bf16[1152,1024]{1,0:T(8,128)(2,1)} %get-tuple-element.41), channel_id=1, source_target_pairs={{0,48},{64,76},{4,52},{68,64},{8,56},{72,68},{12,60},{76,72},{16,0... | collective-permute-start | bytes 7077896 | tf_op jit(solution)/shard_map/ppermute | solution.py:372
  233.8 17.5 %collective-permute-start.16 = (bf16[1152,512]{1,0:T(8,128)(2,1)S(1)}, bf16[1152,512]{1,0:T(8,128)(2,1)S(1)}, u32[]{:S(2)}, u32[]{:S(2)}) collective-permute-start(bf16[1152,512]{1,0:T(8,128)(2,1)S(1)} %add_convert_fusion.1), channel_id=1, source_target_pairs={{0,16},{64,68},{4,20},{68,72},{8,24},{72,76},{12,28},{76,64},{16,3... | collective-permute-start | bytes 3538952 | tf_op jit(solution)/shard_map/ppermute | solution.py:372
  235.3 18.0 %copy-start.5 = (bf16[1152,1024]{1,0:T(8,128)(2,1)S(1)}, bf16[1152,1024]{1,0:T(8,128)(2,1)}, u32[]{:S(2)}) copy-start(bf16[1152,1024]{1,0:T(8,128)(2,1)} %copy-done.4) | copy-start | bytes 7077892
  237.0 16.3 %collective-permute-start.17 = (bf16[1152,512]{1,0:T(8,128)(2,1)S(1)}, bf16[1152,512]{1,0:T(8,128)(2,1)S(1)}, u32[]{:S(2)}, u32[]{:S(2)}) collective-permute-start(bf16[1152,512]{1,0:T(8,128)(2,1)S(1)} %add_convert_fusion), channel_id=1, source_target_pairs={{0,48},{64,76},{4,52},{68,64},{8,56},{72,68},{12,60},{76,72},{16,0... | collective-permute-start | bytes 3538952 | tf_op jit(solution)/shard_map/ppermute | solution.py:372
  239.2 23.6 %copy-start.28 = (bf16[128,1024]{1,0:T(8,128)(2,1)}, bf16[128,1024]{1,0:T(8,128)(2,1)S(1)}, u32[]{:S(2)}) copy-start(bf16[128,1024]{1,0:T(8,128)(2,1)S(1)} %fusion.18.x_1) | copy-start | bytes 786436
  239.3 23.6 %copy-start.16 = (bf16[1,2,2,128,1024]{4,3,2,1,0:T(8,128)(2,1)S(1)}, bf16[1,2,2,128,1024]{4,3,2,1,0:T(8,128)(2,1)}, u32[]{:S(2)}) copy-start(bf16[1,2,2,128,1024]{4,3,2,1,0:T(8,128)(2,1)} %param.11) | copy-start | bytes 3145732
  239.3 23.6 %copy-start.19 = (bf16[128,1024]{1,0:T(8,128)(2,1)S(1)}, bf16[128,1024]{1,0:T(8,128)(2,1)}, u32[]{:S(2)}) copy-start(bf16[128,1024]{1,0:T(8,128)(2,1)} %copy-done.17) | copy-start | bytes 786436
  239.3 23.6 %copy-start.25 = (bf16[128,1024]{1,0:T(8,128)(2,1)S(1)}, bf16[128,1024]{1,0:T(8,128)(2,1)}, u32[]{:S(2)}) copy-start(bf16[128,1024]{1,0:T(8,128)(2,1)} %copy-done.24) | copy-start | bytes 786436
  239.3 23.5 %copy-start.36 = (bf16[128,1024]{1,0:T(8,128)(2,1)S(1)}, bf16[128,1024]{1,0:T(8,128)(2,1)}, u32[]{:S(2)}) copy-start(bf16[128,1024]{1,0:T(8,128)(2,1)} %get-tuple-element.52) | copy-start | bytes 786436
  255.5 12.0 %collective-permute-start.20 = (bf16[1152,256]{1,0:T(8,128)(2,1)S(1)}, bf16[1152,256]{1,0:T(8,128)(2,1)S(1)}, u32[]{:S(2)}, u32[]{:S(2)}) collective-permute-start(bf16[1152,256]{1,0:T(8,128)(2,1)S(1)} %get-tuple-element.59), channel_id=1, source_target_pairs={{0,8},{64,96},{4,12},{68,100},{8,0},{72,104},{12,4},{76,108},{16,2... | collective-permute-start | bytes 1769480 | tf_op jit(solution)/shard_map/ppermute | solution.py:372
  259.6 14.2 %collective-permute-start.19 = (bf16[1152,256]{1,0:T(8,128)(2,1)S(1)}, bf16[1152,256]{1,0:T(8,128)(2,1)S(1)}, u32[]{:S(2)}, u32[]{:S(2)}) collective-permute-start(bf16[1152,256]{1,0:T(8,128)(2,1)S(1)} %get-tuple-element.60), channel_id=1, source_target_pairs={{0,4},{64,80},{4,8},{68,84},{8,12},{72,88},{12,0},{76,92},{16,20},... | collective-permute-start | bytes 1769480 | tf_op jit(solution)/shard_map/ppermute | solution.py:372
  259.7 14.2 %collective-permute-start.18 = (bf16[1152,256]{1,0:T(8,128)(2,1)S(1)}, bf16[1152,256]{1,0:T(8,128)(2,1)S(1)}, u32[]{:S(2)}, u32[]{:S(2)}) collective-permute-start(bf16[1152,256]{1,0:T(8,128)(2,1)S(1)} %get-tuple-element.58), channel_id=1, source_target_pairs={{0,12},{64,112},{4,0},{68,116},{8,4},{72,120},{12,8},{76,124},{16,... | collective-permute-start | bytes 1769480 | tf_op jit(solution)/shard_map/ppermute | solution.py:372
  (35 other events, 197.0 us)
Sparse Core Ops, SparseCore 0:
  11.7 102.2 all-gather.1
  215.2 40.4 reduce-scatter.1

commit v4 on v3

--- a/solution.py
+++ b/solution.py
@@ -524,7 +524,9 @@
     grad = grad.T
 
     mixed_f = jnp.concatenate([jnp.where(first, mixed_b[:SEQ], mixed_a[:SEQ]), mixed_b], 0)
-    mixed_f, _ = lax.optimization_barrier((mixed_f, own_terms))
+    mixed_f, _, scale_row, inverse_row = lax.optimization_barrier(
+        (mixed_f, own_terms, scale_next[None], inverse_next[None])
+    )
     partial = lax.dot_general(mixed_f, full_o, NT, preferred_element_type=f32).astype(bf16)
     summed = lax.psum_scatter(partial, "tensor", scatter_dimension=1, tiled=True)
     copies_new = finish(
@@ -535,8 +537,8 @@
         jnp.where(first, x2, x0),
         y1,
         y2,
-        scale_next[None],
-        inverse_next[None],
+        scale_row,
+        inverse_row,
     )
     return (copies_new, grad[None, :, :1024], grad[None, :, 1024:])
 

time: 291 us -> 290 us (level)
  transfers between devices with their start and end apart: 24 -> 24, of which waited for: 15 -> 15; matrix products, arithmetic and copies ran while one was open for 15% -> 16% of each run, Pallas kernels for 2% -> 2%
where the time goes in v4:
time: 290 us; the launch traced here: 288 us
  waiting for transfers between devices  107 us (37%)
  starting transfers between devices  53.6 us (18%)
  Pallas kernels  47.8 us (16%)
  other arithmetic  23.2 us (8%)
  local copies, waits for them, and re-layouts  21 us (7%)
  between operations  18.5 us (6%)
  matrix products  16.3 us (6%)
    ppermute x14, waiting for transfers between devices, along(): return lax.ppermute(shard, ('section', 'y', 'x'), pairs)  98.5 us
    ppermute x14, starting transfers between devices, along(): return lax.ppermute(shard, ('section', 'y', 'x'), pairs)  26.2 us
    pallas_call x2, Pallas kernels, project_call(): pl.pallas_call(kernel, in_specs=[SMEM] + [VMEM] * (len(operands) - 1) + [...  22.2 us
    ppermute x7, starting transfers between devices, from_first(): lax.ppermute(shard, ('section', 'tensor'), [(i, 4 * to_section + (i + by)...  19.9 us
    unnamed x89, local copies, waits for them, and re-layouts  12.1 us
    dot_general x1, matrix products, on_device(): lax.dot_general(mixed_f, full_o, NT, preferred_element_type=f32)  10.4 us
    ppermute x7, waiting for transfers between devices, from_first(): lax.ppermute(shard, ('section', 'tensor'), [(i, 4 * to_section + (i + by)...  8.87 us
    all_to_all x1, starting transfers between devices, on_device(): lax.all_to_all(jnp.broadcast_to(known[None], (4,) + known.shape), 'tensor...  7.48 us
  transfers between devices with their start and end apart: 24, of which 15 were waited for; matrix products, arithmetic and copies ran while one was open for 16% of the time, Pallas kernels for 2%

profile of v4, /device:TPU:0, one launch (start us, length us, event | category | flops | bytes accessed | tf_op | source)
XLA Modules:
  0.0 287.8 jit_solution(864072845615844114)
XLA Ops:
  7.2 2.2 copy.14
  9.4 2.1 pad_maximum_fusion.3
  11.5 3.2 %collective-permute-start.2 = (bf16[256,1024]{1,0:T(8,128)(2,1)}, bf16[256,1024]{1,0:T(8,128)(2,1)}, u32[]{:S(2)}, u32[]{:S(2)}) collective-permute-start(bf16[256,1024]{1,0:T(8,128)(2,1)} %bitcast.143), channel_id=1, source_target_pairs={{0,8},{64,96},{4,12},{68,100},{8,0},{72,104},{12,4},{76,108},{16,2... | collective-permute-start | bytes 1572872 | tf_op jit(solution)/shard_map/ppermute | solution.py:372
  25.2 6.6 %collective-permute-done.1 = bf16[256,1024]{1,0:T(8,128)(2,1)} collective-permute-done((bf16[256,1024]{1,0:T(8,128)(2,1)}, bf16[256,1024]{1,0:T(8,128)(2,1)}, u32[]{:S(2)}, u32[]{:S(2)}) %collective-permute-start.1) | collective-permute-done | bytes 524320 | tf_op jit(solution)/shard_map/ppermute | solution.py:372
  32.1 3.0 %pad_maximum_fusion.refs_1_.refs_5_ = bf16[4,256,1024]{2,1,0:T(8,128)(2,1)} fusion(bf16[1,256,1024]{2,1,0:T(8,128)(2,1)} %bitcast.34, bf16[1,256,1024]{2,1,0:T(8,128)(2,1)} %bitcast.33, bf16[1,256,1024]{2,1,0:T(8,128)(2,1)} %bitcast.32, bf16[1,256,1024]{2,1,0:T(8,128)(2,1)S(1)} %copy-done.40), kind=kLoop, calls=%fused_computation.7 | loop fusion | flops 3145728 | bytes 4194304 | tf_op jit(solution)/shard_map/stack | solution.py:383
  41.9 7.5 %all-to-all-start = ((bf16[4,384,1024]{2,1,0:T(8,128)(2,1)}), bf16[4,384,1024]{2,1,0:T(8,128)(2,1)}, u32[]{:S(2)}, u32[]{:S(2)}) async-start(bf16[4,384,1024]{2,1,0:T(8,128)(2,1)} %broadcast_in_dim.125), calls=%async_computation | async-start | bytes 6291456 | tf_op jit(solution)/shard_map/all_to_all | solution.py:479
  49.4 33.7 %collective-permute-done.3.refs_2_.refs_6_ = bf16[4,256,1024]{2,1,0:T(8,128)(2,1)} collective-permute-done((bf16[4,256,1024]{2,1,0:T(8,128)(2,1)}, bf16[4,256,1024]{2,1,0:T(8,128)(2,1)}, u32[]{:S(2)}, u32[]{:S(2)}) %collective-permute-start.3) | collective-permute-done | bytes 2097184 | tf_op jit(solution)/shard_map/ppermute | solution.py:372
  83.1 2.3 slice.258
  85.4 2.5 collective-permute-start.5
  87.9 2.3 slice.259
  91.7 4.5 %prepare.1.normed_ref.normed_a = bf16[256,4096]{1,0:T(8,128)(2,1)S(1)} custom-call(s32[7]{0:T(128)S(1)} %stack.47.flags, f32[1,4096]{1,0:T(1,128)S(1)} %copy-done.10, bf16[4,384,1024]{2,1,0:T(8,128)(2,1)} %all-to-all-done.known_ref), custom_call_target="tpu_custom_call" | custom-call | flops 8388608 | bytes 5242880 | tf_op jit(solution)/shard_map/prepare/pallas_call | solution.py:156
  97.5 19.2 %collective-permute-done.5.refs_4_.refs_8_ = bf16[2,256,1024]{2,1,0:T(8,128)(2,1)} collective-permute-done((bf16[2,256,1024]{2,1,0:T(8,128)(2,1)}, bf16[2,256,1024]{2,1,0:T(8,128)(2,1)}, u32[]{:S(2)}, u32[]{:S(2)}) %collective-permute-start.5) | collective-permute-done | bytes 1048608 | tf_op jit(solution)/shard_map/ppermute | solution.py:372
  116.7 9.8 %project_a.1 = (bf16[256,1280]{1,0:T(8,128)(2,1)}, bf16[256,1024]{1,0:T(8,128)(2,1)}) custom-call(s32[7]{0:T(128)} %copy-done.11, bf16[256,4096]{1,0:T(8,128)(2,1)} %copy-done.2, bf16[4096,1280]{1,0:T(8,128)(2,1)} %all-gather.2.cloned.1.call-done.refs_0_.full_ref.refs_4_, bf16[4,256,1024]{2,1,0:T(8,128)(2,1)} %pad_maximum_fusion.refs_1_.refs_5_, ...), custom_call_target="tpu_custom_call" | custom-call | flops 2684354560 | bytes 18874368 | tf_op jit(solution)/shard_map/project_a/pallas_call | solution.py:226
  126.5 6.5 %spread.1 = (bf16[256,1024]{1,0:T(8,128)(2,1)}, bf16[256,1024]{1,0:T(8,128)(2,1)}, bf16[256,1024]{1,0:T(8,128)(2,1)}, bf16[256,1024]{1,0:T(8,128)(2,1)}) custom-call(s32[7]{0:T(128)} %copy-done.11, bf16[256,1024]{1,0:T(8,128)(2,1)} %get-tuple-element.30.mixed_ref, bf16[4096,1280]{1,0:T(8,128)(2,1)} %all-gather.2.cloned.1.call-done.refs_0_.full_ref.refs_4_), custom_call_target="tpu_custom_call" | custom-call | flops 2147483648 | bytes 12582912 | tf_op jit(solution)/shard_map/spread/pallas_call | solution.py:262
  133.0 6.6 %collective-permute-start.9 = (bf16[256,1024]{1,0:T(8,128)(2,1)}, bf16[256,1024]{1,0:T(8,128)(2,1)S(1)}, u32[]{:S(2)}, u32[]{:S(2)}) collective-permute-start(bf16[256,1024]{1,0:T(8,128)(2,1)} %get-tuple-element.34), channel_id=1, source_target_pairs={{0,2},{1,3},{2,0},{3,1},{4,6},{5,7},{6,4},{7,5},{8,10},{9,11},{10,... | collective-permute-start | bytes 1572872 | tf_op jit(solution)/shard_map/ppermute | solution.py:376
  139.6 4.0 %collective-permute-start.8 = (bf16[256,1024]{1,0:T(8,128)(2,1)}, bf16[256,1024]{1,0:T(8,128)(2,1)S(1)}, u32[]{:S(2)}, u32[]{:S(2)}) collective-permute-start(bf16[256,1024]{1,0:T(8,128)(2,1)} %get-tuple-element.33), channel_id=1, source_target_pairs={{0,1},{1,2},{2,3},{3,0},{4,5},{5,6},{6,7},{7,4},{8,9},{9,10},{10,1... | collective-permute-start | bytes 1572872 | tf_op jit(solution)/shard_map/ppermute | solution.py:376
  143.7 3.2 %collective-permute-start.7 = (bf16[256,1024]{1,0:T(8,128)(2,1)}, bf16[256,1024]{1,0:T(8,128)(2,1)S(1)}, u32[]{:S(2)}, u32[]{:S(2)}) collective-permute-start(bf16[256,1024]{1,0:T(8,128)(2,1)} %get-tuple-element.32), channel_id=1, source_target_pairs={{0,3},{1,0},{2,1},{3,2},{4,7},{5,4},{6,5},{7,6},{8,11},{9,8},{10,9... | collective-permute-start | bytes 1572872 | tf_op jit(solution)/shard_map/ppermute | solution.py:376
  147.0 5.6 %collective-permute-done.8 = bf16[256,1024]{1,0:T(8,128)(2,1)S(1)} collective-permute-done((bf16[256,1024]{1,0:T(8,128)(2,1)}, bf16[256,1024]{1,0:T(8,128)(2,1)S(1)}, u32[]{:S(2)}, u32[]{:S(2)}) %collective-permute-start.8) | collective-permute-done | bytes 524320 | tf_op jit(solution)/shard_map/ppermute | solution.py:376
  152.6 2.4 collective-permute-done.7
  162.6 2.1 collective-permute-start.13
  164.7 6.0 %fusion.10 = bf16[384,1024]{1,0:T(8,128)(2,1)S(1)} fusion(bf16[384,4096]{1,0:T(8,128)(2,1)S(1)} %bitcast.141, bf16[4096,1280]{1,0:T(8,128)(2,1)} %all-gather.2.cloned.1.call-done.refs_0_.full_ref.refs_4_), kind=kOutput, calls=%fused_computation.9 | convolution fusion | flops 3221618688 | bytes 12320768 | tf_op jit(solution)/shard_map/dot_general | solution.py:516
  174.5 12.4 %project_b.1 = (bf16[256,4096]{1,0:T(8,128)(2,1)}, bf16[256,1280]{1,0:T(8,128)(2,1)}, bf16[256,1024]{1,0:T(8,128)(2,1)}) custom-call(s32[7]{0:T(128)} %copy-done.11, f32[1,4096]{1,0:T(1,128)} %gain_ref.3, bf16[4,384,1024]{2,1,0:T(8,128)(2,1)} %all-to-all-done.known_ref, bf16[256,1024]{1,0:T(8,128)(2,1)} %copy-done.32, bf16[256,1024]{1,0:T(8,128)(2,1)} %copy-done.38, ...), custom_call_target="tpu_custom_call" | custom-call | flops 2684354560 | bytes 18874368 | tf_op jit(solution)/shard_map/project_b/pallas_call | solution.py:226
  191.5 7.4 %terms.1 = (bf16[1152,1024]{1,0:T(8,128)(2,1)}, bf16[1152,1024]{1,0:T(8,128)(2,1)}, bf16[1152,512]{1,0:T(8,128)(2,1)S(1)}, bf16[1152,512]{1,0:T(8,128)(2,1)S(1)}, bf16[1152,1024]{1,0:T(8,128)(2,1)S(1)}) custom-call(s32[7]{0:T(128)S(1)} %copy-done.12, bf16[256,4096]{1,0:T(8,128)(2,1)S(1)} %copy-done.3, bf16[256,4096]{1,0:T(8,128)(2,1)S(1)} %copy-done.13, ...), custom_call_target="tpu_custom_call" | custom-call | flops 3623878656 | bytes 14680064 | tf_op jit(solution)/shard_map/terms/pallas_call | solution.py:311
  205.9 10.4 %fusion.4 = bf16[384,4096]{1,0:T(8,128)(2,1)} fusion(bf16[384,1024]{1,0:T(8,128)(2,1)S(1)} %pad_maximum_fusion.2, bf16[4096,1280]{1,0:T(8,128)(2,1)} %all-gather.2.cloned.1.call-done.refs_0_.full_ref.refs_4_), kind=kOutput, calls=%fused_computation.4 | convolution fusion | flops 3222798336 | bytes 12320768 | tf_op jit(solution)/shard_map/dot_general | solution.py:530
  216.3 15.3 %collective-permute-done.14 = bf16[1152,1024]{1,0:T(8,128)(2,1)} collective-permute-done((bf16[1152,1024]{1,0:T(8,128)(2,1)}, bf16[1152,1024]{1,0:T(8,128)(2,1)}, u32[]{:S(2)}, u32[]{:S(2)}) %collective-permute-start.14) | collective-permute-done | bytes 2359328 | tf_op jit(solution)/shard_map/ppermute | solution.py:372
  239.2 12.0 %collective-permute-done.16 = bf16[1152,512]{1,0:T(8,128)(2,1)S(1)} collective-permute-done((bf16[1152,512]{1,0:T(8,128)(2,1)S(1)}, bf16[1152,512]{1,0:T(8,128)(2,1)S(1)}, u32[]{:S(2)}, u32[]{:S(2)}) %collective-permute-start.16) | collective-permute-done | bytes 1179680 | tf_op jit(solution)/shard_map/ppermute | solution.py:372
  253.3 2.2 add_convert_fusion.5
  255.5 4.1 %collective-permute-start.20 = (bf16[1152,256]{1,0:T(8,128)(2,1)S(1)}, bf16[1152,256]{1,0:T(8,128)(2,1)S(1)}, u32[]{:S(2)}, u32[]{:S(2)}) collective-permute-start(bf16[1152,256]{1,0:T(8,128)(2,1)S(1)} %get-tuple-element.63), channel_id=1, source_target_pairs={{0,8},{64,96},{4,12},{68,100},{8,0},{72,104},{12,4},{76,108},{16,2... | collective-permute-start | bytes 1769480 | tf_op jit(solution)/shard_map/ppermute | solution.py:372
  259.7 3.1 %collective-permute-start.18 = (bf16[1152,256]{1,0:T(8,128)(2,1)S(1)}, bf16[1152,256]{1,0:T(8,128)(2,1)S(1)}, u32[]{:S(2)}, u32[]{:S(2)}) collective-permute-start(bf16[1152,256]{1,0:T(8,128)(2,1)S(1)} %get-tuple-element.62), channel_id=1, source_target_pairs={{0,12},{64,112},{4,0},{68,116},{8,4},{72,120},{12,8},{76,124},{16,... | collective-permute-start | bytes 1769480 | tf_op jit(solution)/shard_map/ppermute | solution.py:372
  265.2 2.4 collective-permute-done.20
  267.6 6.2 %collective-permute-done.19 = bf16[1152,256]{1,0:T(8,128)(2,1)S(1)} collective-permute-done((bf16[1152,256]{1,0:T(8,128)(2,1)S(1)}, bf16[1152,256]{1,0:T(8,128)(2,1)S(1)}, u32[]{:S(2)}, u32[]{:S(2)}) %collective-permute-start.19) | collective-permute-done | bytes 589856 | tf_op jit(solution)/shard_map/ppermute | solution.py:372
  277.3 3.7 %finish.1 = bf16[1,2,2,128,1024]{4,3,2,1,0:T(8,128)(2,1)} custom-call(s32[7]{0:T(128)} %copy-done.11, bf16[2,128,1024]{2,1,0:T(8,128)(2,1)} %select_select_fusion.new_in, bf16[2,128,1024]{2,1,0:T(8,128)(2,1)} %get-tuple-element.74.state_out, bf16[384,1024]{1,0:T(8,128)(2,1)} %reduce-scatter.2.cloned.1.call-done.summed, ...), custom_call_target="tpu_custom_call" | custom-call | flops 8388608 | bytes 5242880 | tf_op jit(solution)/shard_map/finish/pallas_call | solution.py:354
  (163 shorter events, 54.9 us)
Async XLA Ops:
  7.2 157.6 %copy-start = (bf16[1,3,1,128,4096]{4,3,2,1,0:T(8,128)(2,1)S(1)}, bf16[1,3,1,128,4096]{4,3,2,1,0:T(8,128)(2,1)}, u32[]{:S(2)}) copy-start(bf16[1,3,1,128,4096]{4,3,2,1,0:T(8,128)(2,1)} %param.21) | copy-start | bytes 9437188
  7.2 109.5 %all-gather.2.cloned.1.call-start = ((), (), s32[]{:S(2)}) async-start(), calls=%async_computation.2 | async-start | bytes 11141120 | tf_op jit(solution)/shard_map/all_gather | solution.py:444
  11.5 13.6 %collective-permute-start.2 = (bf16[256,1024]{1,0:T(8,128)(2,1)}, bf16[256,1024]{1,0:T(8,128)(2,1)}, u32[]{:S(2)}, u32[]{:S(2)}) collective-permute-start(bf16[256,1024]{1,0:T(8,128)(2,1)} %bitcast.143), channel_id=1, source_target_pairs={{0,8},{64,96},{4,12},{68,100},{8,0},{72,104},{12,4},{76,108},{16,2... | collective-permute-start | bytes 1572872 | tf_op jit(solution)/shard_map/ppermute | solution.py:372
  14.7 17.1 %collective-permute-start.1 = (bf16[256,1024]{1,0:T(8,128)(2,1)}, bf16[256,1024]{1,0:T(8,128)(2,1)}, u32[]{:S(2)}, u32[]{:S(2)}) collective-permute-start(bf16[256,1024]{1,0:T(8,128)(2,1)} %bitcast.144), channel_id=1, source_target_pairs={{0,12},{64,112},{4,0},{68,116},{8,4},{72,120},{12,8},{76,124},{16,... | collective-permute-start | bytes 1572872 | tf_op jit(solution)/shard_map/ppermute | solution.py:372
  15.9 16.2 %collective-permute-start = (bf16[256,1024]{1,0:T(8,128)(2,1)}, bf16[256,1024]{1,0:T(8,128)(2,1)}, u32[]{:S(2)}, u32[]{:S(2)}) collective-permute-start(bf16[256,1024]{1,0:T(8,128)(2,1)} %bitcast.145), channel_id=1, source_target_pairs={{0,4},{64,80},{4,8},{68,84},{8,12},{72,88},{12,0},{76,92},{16,20},... | collective-permute-start | bytes 1572872 | tf_op jit(solution)/shard_map/ppermute | solution.py:372
  20.1 18.5 %copy-start.17 = (bf16[128,1024]{1,0:T(8,128)(2,1)}, bf16[128,1024]{1,0:T(8,128)(2,1)S(1)}, u32[]{:S(2)}) copy-start(bf16[128,1024]{1,0:T(8,128)(2,1)S(1)} %fusion.37) | copy-start | bytes 786436
  35.1 48.0 %collective-permute-start.3 = (bf16[4,256,1024]{2,1,0:T(8,128)(2,1)}, bf16[4,256,1024]{2,1,0:T(8,128)(2,1)}, u32[]{:S(2)}, u32[]{:S(2)}) collective-permute-start(bf16[4,256,1024]{2,1,0:T(8,128)(2,1)} %pad_maximum_fusion.refs_1_.refs_5_), channel_id=1, source_target_pairs={{0,16},{64,68},{4,20},{68,72},{8,24},{72,76},{12,28},{76,64},{16,3... | collective-permute-start | bytes 6291464 | tf_op jit(solution)/shard_map/ppermute | solution.py:372
  36.5 51.4 %collective-permute-start.4 = (bf16[4,256,1024]{2,1,0:T(8,128)(2,1)}, bf16[4,256,1024]{2,1,0:T(8,128)(2,1)}, u32[]{:S(2)}, u32[]{:S(2)}) collective-permute-start(bf16[4,256,1024]{2,1,0:T(8,128)(2,1)} %pad_maximum_fusion.refs_1_.refs_5_), channel_id=1, source_target_pairs={{0,48},{64,76},{4,52},{68,64},{8,56},{72,68},{12,60},{76,72},{16,0... | collective-permute-start | bytes 6291464 | tf_op jit(solution)/shard_map/ppermute | solution.py:372
  41.9 49.8 %all-to-all-start = ((bf16[4,384,1024]{2,1,0:T(8,128)(2,1)}), bf16[4,384,1024]{2,1,0:T(8,128)(2,1)}, u32[]{:S(2)}, u32[]{:S(2)}) async-start(bf16[4,384,1024]{2,1,0:T(8,128)(2,1)} %broadcast_in_dim.125), calls=%async_computation | async-start | bytes 6291456 | tf_op jit(solution)/shard_map/all_to_all | solution.py:479
  49.4 227.9 %reduce-scatter.2.cloned.1.call-start = ((), (), s32[]{:S(2)}) async-start(), calls=%async_computation.3 | async-start | bytes 3932160 | tf_op jit(solution)/shard_map/reduce_scatter | solution.py:531
  85.4 31.3 %collective-permute-start.5 = (bf16[2,256,1024]{2,1,0:T(8,128)(2,1)}, bf16[2,256,1024]{2,1,0:T(8,128)(2,1)}, u32[]{:S(2)}, u32[]{:S(2)}) collective-permute-start(bf16[2,256,1024]{2,1,0:T(8,128)(2,1)} %slice.258), channel_id=1, source_target_pairs={{0,16},{64,68},{4,20},{68,72},{8,24},{72,76},{12,28},{76,64},{16,3... | collective-permute-start | bytes 3145736 | tf_op jit(solution)/shard_map/ppermute | solution.py:372
  90.2 26.5 %collective-permute-start.6 = (bf16[2,256,1024]{2,1,0:T(8,128)(2,1)}, bf16[2,256,1024]{2,1,0:T(8,128)(2,1)}, u32[]{:S(2)}, u32[]{:S(2)}) collective-permute-start(bf16[2,256,1024]{2,1,0:T(8,128)(2,1)} %slice.259), channel_id=1, source_target_pairs={{0,48},{64,76},{4,52},{68,64},{8,56},{72,68},{12,60},{76,72},{16,0... | collective-permute-start | bytes 3145736 | tf_op jit(solution)/shard_map/ppermute | solution.py:372
  133.0 14.0 %collective-permute-start.9 = (bf16[256,1024]{1,0:T(8,128)(2,1)}, bf16[256,1024]{1,0:T(8,128)(2,1)S(1)}, u32[]{:S(2)}, u32[]{:S(2)}) collective-permute-start(bf16[256,1024]{1,0:T(8,128)(2,1)} %get-tuple-element.34), channel_id=1, source_target_pairs={{0,2},{1,3},{2,0},{3,1},{4,6},{5,7},{6,4},{7,5},{8,10},{9,11},{10,... | collective-permute-start | bytes 1572872 | tf_op jit(solution)/shard_map/ppermute | solution.py:376
  139.6 13.0 %collective-permute-start.8 = (bf16[256,1024]{1,0:T(8,128)(2,1)}, bf16[256,1024]{1,0:T(8,128)(2,1)S(1)}, u32[]{:S(2)}, u32[]{:S(2)}) collective-permute-start(bf16[256,1024]{1,0:T(8,128)(2,1)} %get-tuple-element.33), channel_id=1, source_target_pairs={{0,1},{1,2},{2,3},{3,0},{4,5},{5,6},{6,7},{7,4},{8,9},{9,10},{10,1... | collective-permute-start | bytes 1572872 | tf_op jit(solution)/shard_map/ppermute | solution.py:376
  143.7 11.3 %collective-permute-start.7 = (bf16[256,1024]{1,0:T(8,128)(2,1)}, bf16[256,1024]{1,0:T(8,128)(2,1)S(1)}, u32[]{:S(2)}, u32[]{:S(2)}) collective-permute-start(bf16[256,1024]{1,0:T(8,128)(2,1)} %get-tuple-element.32), channel_id=1, source_target_pairs={{0,3},{1,0},{2,1},{3,2},{4,7},{5,4},{6,5},{7,6},{8,11},{9,8},{10,9... | collective-permute-start | bytes 1572872 | tf_op jit(solution)/shard_map/ppermute | solution.py:376
  158.7 14.0 %collective-permute-start.10 = (bf16[256,1024]{1,0:T(8,128)(2,1)S(1)}, bf16[256,1024]{1,0:T(8,128)(2,1)S(1)}, u32[]{:S(2)}, u32[]{:S(2)}) collective-permute-start(bf16[256,1024]{1,0:T(8,128)(2,1)S(1)} %pad_maximum_fusion.4), channel_id=1, source_target_pairs={{0,64},{1,65},{2,66},{3,67},{4,68},{5,69},{6,70},{7,71},{8,72},{9,... | collective-permute-start | bytes 1572872 | tf_op jit(solution)/shard_map/ppermute | solution.py:376
  160.0 12.7 %collective-permute-start.11 = (bf16[256,1024]{1,0:T(8,128)(2,1)S(1)}, bf16[256,1024]{1,0:T(8,128)(2,1)S(1)}, u32[]{:S(2)}, u32[]{:S(2)}) collective-permute-start(bf16[256,1024]{1,0:T(8,128)(2,1)S(1)} %pad_maximum_fusion.4), channel_id=1, source_target_pairs={{0,65},{1,66},{2,67},{3,64},{4,69},{5,70},{6,71},{7,68},{8,73},{9,... | collective-permute-start | bytes 1572872 | tf_op jit(solution)/shard_map/ppermute | solution.py:376
  161.3 12.3 %collective-permute-start.12 = (bf16[256,1024]{1,0:T(8,128)(2,1)S(1)}, bf16[256,1024]{1,0:T(8,128)(2,1)S(1)}, u32[]{:S(2)}, u32[]{:S(2)}) collective-permute-start(bf16[256,1024]{1,0:T(8,128)(2,1)S(1)} %pad_maximum_fusion.4), channel_id=1, source_target_pairs={{0,66},{1,67},{2,64},{3,65},{4,70},{5,71},{6,68},{7,69},{8,74},{9,... | collective-permute-start | bytes 1572872 | tf_op jit(solution)/shard_map/ppermute | solution.py:376
  162.6 11.9 %collective-permute-start.13 = (bf16[256,1024]{1,0:T(8,128)(2,1)S(1)}, bf16[256,1024]{1,0:T(8,128)(2,1)}, u32[]{:S(2)}, u32[]{:S(2)}) collective-permute-start(bf16[256,1024]{1,0:T(8,128)(2,1)S(1)} %pad_maximum_fusion.4), channel_id=1, source_target_pairs={{0,67},{1,64},{2,65},{3,66},{4,71},{5,68},{6,69},{7,70},{8,75},{9,... | collective-permute-start | bytes 1572872 | tf_op jit(solution)/shard_map/ppermute | solution.py:376
  201.3 30.4 %collective-permute-start.14 = (bf16[1152,1024]{1,0:T(8,128)(2,1)}, bf16[1152,1024]{1,0:T(8,128)(2,1)}, u32[]{:S(2)}, u32[]{:S(2)}) collective-permute-start(bf16[1152,1024]{1,0:T(8,128)(2,1)} %get-tuple-element.44), channel_id=1, source_target_pairs={{0,16},{64,68},{4,20},{68,72},{8,24},{72,76},{12,28},{76,64},{16,3... | collective-permute-start | bytes 7077896 | tf_op jit(solution)/shard_map/ppermute | solution.py:372
  202.9 29.2 %collective-permute-start.15 = (bf16[1152,1024]{1,0:T(8,128)(2,1)}, bf16[1152,1024]{1,0:T(8,128)(2,1)}, u32[]{:S(2)}, u32[]{:S(2)}) collective-permute-start(bf16[1152,1024]{1,0:T(8,128)(2,1)} %get-tuple-element.45), channel_id=1, source_target_pairs={{0,48},{64,76},{4,52},{68,64},{8,56},{72,68},{12,60},{76,72},{16,0... | collective-permute-start | bytes 7077896 | tf_op jit(solution)/shard_map/ppermute | solution.py:372
  233.7 17.5 %collective-permute-start.16 = (bf16[1152,512]{1,0:T(8,128)(2,1)S(1)}, bf16[1152,512]{1,0:T(8,128)(2,1)S(1)}, u32[]{:S(2)}, u32[]{:S(2)}) collective-permute-start(bf16[1152,512]{1,0:T(8,128)(2,1)S(1)} %add_convert_fusion.1), channel_id=1, source_target_pairs={{0,16},{64,68},{4,20},{68,72},{8,24},{72,76},{12,28},{76,64},{16,3... | collective-permute-start | bytes 3538952 | tf_op jit(solution)/shard_map/ppermute | solution.py:372
  235.2 18.1 %copy-start.5 = (bf16[1152,1024]{1,0:T(8,128)(2,1)S(1)}, bf16[1152,1024]{1,0:T(8,128)(2,1)}, u32[]{:S(2)}) copy-start(bf16[1152,1024]{1,0:T(8,128)(2,1)} %copy-done.4) | copy-start | bytes 7077892
  237.0 16.3 %collective-permute-start.17 = (bf16[1152,512]{1,0:T(8,128)(2,1)S(1)}, bf16[1152,512]{1,0:T(8,128)(2,1)S(1)}, u32[]{:S(2)}, u32[]{:S(2)}) collective-permute-start(bf16[1152,512]{1,0:T(8,128)(2,1)S(1)} %add_convert_fusion), channel_id=1, source_target_pairs={{0,48},{64,76},{4,52},{68,64},{8,56},{72,68},{12,60},{76,72},{16,0... | collective-permute-start | bytes 3538952 | tf_op jit(solution)/shard_map/ppermute | solution.py:372
  239.2 23.7 %copy-start.28 = (bf16[128,1024]{1,0:T(8,128)(2,1)}, bf16[128,1024]{1,0:T(8,128)(2,1)S(1)}, u32[]{:S(2)}) copy-start(bf16[128,1024]{1,0:T(8,128)(2,1)S(1)} %fusion.18.x_1) | copy-start | bytes 786436
  239.2 23.7 %copy-start.16 = (bf16[1,2,2,128,1024]{4,3,2,1,0:T(8,128)(2,1)S(1)}, bf16[1,2,2,128,1024]{4,3,2,1,0:T(8,128)(2,1)}, u32[]{:S(2)}) copy-start(bf16[1,2,2,128,1024]{4,3,2,1,0:T(8,128)(2,1)} %param.11) | copy-start | bytes 3145732
  239.2 23.7 %copy-start.19 = (bf16[128,1024]{1,0:T(8,128)(2,1)S(1)}, bf16[128,1024]{1,0:T(8,128)(2,1)}, u32[]{:S(2)}) copy-start(bf16[128,1024]{1,0:T(8,128)(2,1)} %copy-done.17) | copy-start | bytes 786436
  239.2 23.6 %copy-start.25 = (bf16[128,1024]{1,0:T(8,128)(2,1)S(1)}, bf16[128,1024]{1,0:T(8,128)(2,1)}, u32[]{:S(2)}) copy-start(bf16[128,1024]{1,0:T(8,128)(2,1)} %copy-done.24) | copy-start | bytes 786436
  239.2 23.6 %copy-start.36 = (bf16[128,1024]{1,0:T(8,128)(2,1)S(1)}, bf16[128,1024]{1,0:T(8,128)(2,1)}, u32[]{:S(2)}) copy-start(bf16[128,1024]{1,0:T(8,128)(2,1)} %get-tuple-element.56) | copy-start | bytes 786436
  255.5 12.1 %collective-permute-start.20 = (bf16[1152,256]{1,0:T(8,128)(2,1)S(1)}, bf16[1152,256]{1,0:T(8,128)(2,1)S(1)}, u32[]{:S(2)}, u32[]{:S(2)}) collective-permute-start(bf16[1152,256]{1,0:T(8,128)(2,1)S(1)} %get-tuple-element.63), channel_id=1, source_target_pairs={{0,8},{64,96},{4,12},{68,100},{8,0},{72,104},{12,4},{76,108},{16,2... | collective-permute-start | bytes 1769480 | tf_op jit(solution)/shard_map/ppermute | solution.py:372
  259.6 14.2 %collective-permute-start.19 = (bf16[1152,256]{1,0:T(8,128)(2,1)S(1)}, bf16[1152,256]{1,0:T(8,128)(2,1)S(1)}, u32[]{:S(2)}, u32[]{:S(2)}) collective-permute-start(bf16[1152,256]{1,0:T(8,128)(2,1)S(1)} %get-tuple-element.64), channel_id=1, source_target_pairs={{0,4},{64,80},{4,8},{68,84},{8,12},{72,88},{12,0},{76,92},{16,20},... | collective-permute-start | bytes 1769480 | tf_op jit(solution)/shard_map/ppermute | solution.py:372
  259.7 14.2 %collective-permute-start.18 = (bf16[1152,256]{1,0:T(8,128)(2,1)S(1)}, bf16[1152,256]{1,0:T(8,128)(2,1)S(1)}, u32[]{:S(2)}, u32[]{:S(2)}) collective-permute-start(bf16[1152,256]{1,0:T(8,128)(2,1)S(1)} %get-tuple-element.62), channel_id=1, source_target_pairs={{0,12},{64,112},{4,0},{68,116},{8,4},{72,120},{12,8},{76,124},{16,... | collective-permute-start | bytes 1769480 | tf_op jit(solution)/shard_map/ppermute | solution.py:372
  (35 other events, 195.6 us)
Sparse Core Ops, SparseCore 0:
  11.7 102.2 all-gather.1
  216.4 40.4 reduce-scatter.1
